TPU v7x, 32 devices: a whole 2x2x4 slice. The times are simulated.
32 devices in a mesh: dp: 4 (over y, core), fsdp: 8 (over z, x).
Axes of the slice: x: 2, y: 2, z: 4, core: 2. Of those that a mesh axis runs over, the one named last changes fastest.
Arguments:
- tokens: bfloat16 [131072, 512], P(('dp', 'fsdp')), may hold values from -6 to 6
- cotangent: bfloat16 [131072, 512], P(('dp', 'fsdp')), may hold values from -6 to 6
- w_qkv: bfloat16 [512, 1536], P('fsdp', 'dp'), may hold values from -0.03125 to 0.03125
- w_out: bfloat16 [512, 512], P('fsdp', 'dp'), may hold values from -0.5 to 0.5
- w_in: bfloat16 [512, 2048], P('fsdp', 'dp'), may hold values from -0.25 to 0.25
- w_back: bfloat16 [2048, 512], P('fsdp', 'dp'), may hold values from -0.125 to 0.125
- vec_params: bfloat16 [8, 512], P('dp', 'fsdp'), may hold values from -7.2 to 24
- b_in: bfloat16 [2048], P(('dp', 'fsdp')), may hold values from -3 to 3
- item_lengths: int32 [32, 4], P(('dp', 'fsdp')), may hold values from 256 to 4096, as said below
- bucket_counts: int32 [32, 3], P(('dp', 'fsdp')), may hold values from 0 to 1, as said below
Outputs:
- layer_out: bfloat16 [131072, 512], P(('dp', 'fsdp'))
- tokens_grad: bfloat16 [131072, 512], P(('dp', 'fsdp'))
- grad_qkv: float32 [512, 1536], P('fsdp', 'dp')
- grad_out: float32 [512, 512], P('fsdp', 'dp')
- grad_in: float32 [512, 2048], P('fsdp', 'dp')
- grad_back: float32 [2048, 512], P('fsdp', 'dp')
- grad_vec: float32 [8, 512], P('dp', 'fsdp')
- grad_bias_in: float32 [2048], P(('dp', 'fsdp'))
Inputs may be any that keep to these rules, and one draw needn't show every extreme that they name: `item_lengths`: slots of one microbatch hold that microbatch's item length; an item of a 4-slot microbatch has more than 2048 rows, of a 2-slot one more than 1024, of a 1-slot one 1024 // 4 or more, and none more than its microbatch's rows. `bucket_counts`: each row (c0, c1, c2) has 4 c0 + 2 c1 + c2 = 4 and c0 >= 1; microbatches lie in that order.
All inputs are finite; a program needn't handle non-finite values.
Results may differ from a plain program's by a relative error of at most 0.012.
Values may be sent and summed in bfloat16 or wider, within the bound.
A program may use at most 384 MiB of HBM per device.

v0:
```python
import jax
import jax.numpy as jnp
from jax import lax
from jax.sharding import PartitionSpec as P

HEADS = 8
BAND = 30
BLOCK = 512


norm_eps = 1e-05
exact = lax.Precision.HIGHEST


def layout(counts, lengths, slot_count, slot_rows):
    slot_ids = jnp.arange(slot_count, dtype=jnp.int32)
    four_end = 4 * counts[0]
    two_end = four_end + 2 * counts[1]
    start_slot = jnp.where(
        slot_ids < four_end,
        slot_ids // 4 * 4,
        jnp.where(slot_ids < two_end, four_end + (slot_ids - four_end) // 2 * 2, slot_ids),
    )
    item_rows = jnp.broadcast_to(start_slot[:, None], (slot_count, slot_rows)).reshape(-1)
    length_rows = jnp.broadcast_to(lengths[:, None], (slot_count, slot_rows)).reshape(-1)
    row_ids = jnp.arange(slot_count * slot_rows, dtype=jnp.int32)
    place_rows = (row_ids // slot_rows - item_rows) * slot_rows + row_ids % slot_rows
    valid_rows = (place_rows < length_rows).astype(jnp.float32)
    same_item = (start_slot[:, None] == start_slot[None, :]).astype(jnp.float32)
    inv_length = 1.0 / lengths.astype(jnp.float32)
    return (item_rows, valid_rows, same_item, inv_length)


def band_mask(item_pad, valid_pad, item_rows, block_id):
    first_row = block_id * BLOCK
    query_row = first_row + jnp.arange(BLOCK, dtype=jnp.int32)
    key_row = first_row - BAND + jnp.arange(BLOCK + 2 * BAND, dtype=jnp.int32)
    item_query = lax.dynamic_slice_in_dim(item_rows, first_row, BLOCK, 0)
    item_key = lax.dynamic_slice_in_dim(item_pad, first_row, BLOCK + 2 * BAND, 0)
    valid_key = lax.dynamic_slice_in_dim(valid_pad, first_row, BLOCK + 2 * BAND, 0)
    offset = query_row[:, None] - key_row[None, :]
    return (
        (jnp.abs(offset) <= BAND)
        & (item_query[:, None] == item_key[None, :])
        & ((valid_key[None, :] > 0.5) | (offset == 0))
    )


def block_inputs(query_all, key_pad, value_pad, block_id):
    first_row = block_id * BLOCK
    model_width = query_all.shape[1]
    head_size = model_width // HEADS
    block_query = lax.dynamic_slice_in_dim(query_all, first_row, BLOCK, 0).reshape(
        BLOCK, HEADS, head_size
    )
    block_keys = lax.dynamic_slice_in_dim(key_pad, first_row, BLOCK + 2 * BAND, 0).reshape(
        BLOCK + 2 * BAND, HEADS, head_size
    )
    block_values = lax.dynamic_slice_in_dim(value_pad, first_row, BLOCK + 2 * BAND, 0).reshape(
        BLOCK + 2 * BAND, HEADS, head_size
    )
    return (block_query, block_keys, block_values)


def band_probs(block_query, block_keys, mask_now):
    score_scale = block_query.shape[2] ** (-0.5)
    scores = (
        jnp.einsum("qhd,khd->hqk", block_query, block_keys, preferred_element_type=jnp.float32)
        * score_scale
    )
    scores = jnp.where(mask_now[None], scores, -1e30)
    exp_scores = jnp.exp(scores - jnp.max(scores, axis=-1, keepdims=True))
    return exp_scores / jnp.sum(exp_scores, axis=-1, keepdims=True)


def normed(values_in, gain, shift):
    row_mean = jnp.mean(values_in, axis=-1, keepdims=True)
    centered = values_in - row_mean
    inv_std = lax.rsqrt(jnp.mean(centered * centered, axis=-1, keepdims=True) + norm_eps)
    return centered * inv_std * gain + shift


def far_field(query_in, keys_in, values_in, valid_rows, same_item, inv_length):
    slot_count = same_item.shape[0]
    row_count, model_width = query_in.shape
    shape_four = (slot_count, row_count // slot_count, HEADS, model_width // HEADS)
    query_four = query_in.reshape(shape_four)
    keys_four = keys_in.reshape(shape_four)
    values_four = values_in.reshape(shape_four)
    valid_four = valid_rows.reshape(slot_count, row_count // slot_count, 1, 1)
    lift_query = jax.nn.elu(query_four) + 1.0
    lift_keys = (jax.nn.elu(keys_four) + 1.0) * valid_four
    bent_query = jnp.tanh(query_four)
    bent_keys = jnp.tanh(keys_four) * valid_four
    state_one = jnp.einsum("srhd,srhe->shde", lift_keys, values_four, precision=exact)
    state_one = jnp.einsum("st,thde->shde", same_item, state_one, precision=exact)
    total_one = jnp.einsum("st,thd->shd", same_item, jnp.sum(lift_keys, axis=1), precision=exact)
    numer = jnp.einsum("srhd,shde->srhe", lift_query, state_one, precision=exact)
    denom = jnp.einsum("srhd,shd->srh", lift_query, total_one, precision=exact)
    state_two = jnp.einsum("srhd,srhe->shde", bent_keys, values_four, precision=exact)
    state_two = jnp.einsum("st,thde->shde", same_item, state_two, precision=exact)
    far_two = jnp.einsum(
        "srhd,shde->srhe", bent_query, state_two, precision=exact
    ) * inv_length.reshape(slot_count, 1, 1, 1)
    return (
        (numer / denom[..., None]).reshape(row_count, model_width),
        far_two.reshape(row_count, model_width),
    )


def fold_back(extended, row_count):
    block_count, span_rows, model_width = extended.shape
    head_part = extended[:, :BLOCK].reshape(block_count * BLOCK, model_width)
    tail_part = jnp.pad(extended[:, BLOCK:], ((0, 0), (0, BLOCK - 2 * BAND), (0, 0))).reshape(
        block_count * BLOCK, model_width
    )
    summed = jnp.pad(head_part, ((0, BLOCK), (0, 0))) + jnp.pad(tail_part, ((BLOCK, 0), (0, 0)))
    return summed[BAND : BAND + row_count]


def rows_product(left_side, right_side):
    return lax.dot_general(
        left_side, right_side, (((0,), (0,)), ((), ())), preferred_element_type=jnp.float32
    )


def cols_product(left_side, right_side):
    return lax.dot_general(
        left_side, right_side, (((1,), (1,)), ((), ())), preferred_element_type=jnp.float32
    )


def collect(w_qkv, w_out, w_in, w_back, vec_params, b_in):
    section_one = (
        lax.all_gather(w_qkv, "fsdp", axis=0, tiled=True),
        lax.all_gather(w_out, "fsdp", axis=0, tiled=True),
        lax.all_gather(w_in, "fsdp", axis=0, tiled=True),
        lax.all_gather(w_back, "fsdp", axis=0, tiled=True),
        lax.all_gather(vec_params, "fsdp", axis=1, tiled=True),
        lax.all_gather(b_in, "fsdp", axis=0, tiled=True),
    )
    return (
        lax.all_gather(section_one[0], "dp", axis=1, tiled=True),
        lax.all_gather(section_one[1], "dp", axis=1, tiled=True),
        lax.all_gather(section_one[2], "dp", axis=1, tiled=True),
        lax.all_gather(section_one[3], "dp", axis=1, tiled=True),
        lax.all_gather(section_one[4], "dp", axis=0, tiled=True),
        lax.all_gather(section_one[5], "dp", axis=0, tiled=True),
    )


def spread(grad_qkv, grad_out, grad_in, grad_back, grad_vec, grad_bias_in):
    section_one = (
        lax.psum_scatter(
            grad_qkv.astype(jnp.bfloat16), "dp", scatter_dimension=1, tiled=True
        ).astype(jnp.float32),
        lax.psum_scatter(
            grad_out.astype(jnp.bfloat16), "dp", scatter_dimension=1, tiled=True
        ).astype(jnp.float32),
        lax.psum_scatter(
            grad_in.astype(jnp.bfloat16), "dp", scatter_dimension=1, tiled=True
        ).astype(jnp.float32),
        lax.psum_scatter(
            grad_back.astype(jnp.bfloat16), "dp", scatter_dimension=1, tiled=True
        ).astype(jnp.float32),
        lax.psum_scatter(
            grad_vec.astype(jnp.bfloat16), "dp", scatter_dimension=0, tiled=True
        ).astype(jnp.float32),
        lax.psum_scatter(
            grad_bias_in.astype(jnp.bfloat16), "dp", scatter_dimension=0, tiled=True
        ).astype(jnp.float32),
    )
    return (
        lax.psum_scatter(section_one[0], "fsdp", scatter_dimension=0, tiled=True),
        lax.psum_scatter(section_one[1], "fsdp", scatter_dimension=0, tiled=True),
        lax.psum_scatter(section_one[2], "fsdp", scatter_dimension=0, tiled=True),
        lax.psum_scatter(section_one[3], "fsdp", scatter_dimension=0, tiled=True),
        lax.psum_scatter(section_one[4], "fsdp", scatter_dimension=1, tiled=True),
        lax.psum_scatter(section_one[5], "fsdp", scatter_dimension=0, tiled=True),
    )


def shards(
    tokens, cotangent, w_qkv, w_out, w_in, w_back, vec_params, b_in, item_lengths, bucket_counts
):
    slot_count = item_lengths.shape[1]
    row_count, model_width = tokens.shape
    slot_rows = row_count // slot_count
    head_size = model_width // HEADS
    score_scale = head_size ** (-0.5)
    block_ids = jnp.arange(row_count // BLOCK, dtype=jnp.int32)
    item_rows, valid_rows, same_item, inv_length = layout(
        bucket_counts[0], item_lengths[0], slot_count, slot_rows
    )
    item_pad = jnp.pad(item_rows, (BAND, BAND), constant_values=-1)
    valid_pad = jnp.pad(valid_rows, (BAND, BAND))
    valid_col = valid_rows[:, None]
    qkv_w, out_w, in_w, back_w, vecs, in_bias = collect(
        w_qkv, w_out, w_in, w_back, vec_params, b_in
    )
    vec_wide = vecs.astype(jnp.float32)
    tokens_wide = tokens.astype(jnp.float32)
    norm_one, pull_one = jax.vjp(normed, tokens_wide, vec_wide[0], vec_wide[1])
    h_one = norm_one.astype(jnp.bfloat16)
    qkv = jnp.dot(h_one, qkv_w, preferred_element_type=jnp.float32).astype(jnp.bfloat16)
    query_all = qkv[:, :model_width]
    key_all = qkv[:, model_width : 2 * model_width]
    value_all = qkv[:, 2 * model_width :]
    key_pad = jnp.pad(key_all, ((BAND, BAND), (0, 0)))
    value_pad = jnp.pad(value_all, ((BAND, BAND), (0, 0)))

    def near_block(block_id):
        mask_now = band_mask(item_pad, valid_pad, item_rows, block_id)
        block_query, block_keys, block_values = block_inputs(
            query_all, key_pad, value_pad, block_id
        )
        probs = band_probs(block_query, block_keys, mask_now).astype(jnp.bfloat16)
        return jnp.einsum(
            "hqk,khd->qhd", probs, block_values, preferred_element_type=jnp.float32
        ).reshape(BLOCK, model_width)

    near_out = lax.map(near_block, block_ids).reshape(row_count, model_width)
    (far_a, far_b), pull_far = jax.vjp(
        lambda query_in, keys_in, values_in: far_field(
            query_in, keys_in, values_in, valid_rows, same_item, inv_length
        ),
        query_all.astype(jnp.float32),
        key_all.astype(jnp.float32),
        value_all.astype(jnp.float32),
    )
    mixed = (vec_wide[5] * near_out + vec_wide[6] * far_a + vec_wide[7] * far_b).astype(
        jnp.bfloat16
    )
    resid = tokens_wide + jnp.dot(mixed, out_w, preferred_element_type=jnp.float32)
    norm_two, pull_two = jax.vjp(normed, resid, vec_wide[2], vec_wide[3])
    h_two = norm_two.astype(jnp.bfloat16)
    pre_act = jnp.dot(h_two, in_w, preferred_element_type=jnp.float32) + in_bias.astype(jnp.float32)
    act_wide, pull_act = jax.vjp(jax.nn.gelu, pre_act)
    act = act_wide.astype(jnp.bfloat16)
    ffn_out = jnp.dot(act, back_w, preferred_element_type=jnp.float32) + vec_wide[4]
    layer_out = (valid_col * (resid + ffn_out)).astype(jnp.bfloat16)
    qkv_w, out_w, in_w, back_w, vecs, in_bias = collect(
        w_qkv, w_out, w_in, w_back, vec_params, b_in
    )
    vec_wide = vecs.astype(jnp.float32)
    grad_seed = valid_col * cotangent.astype(jnp.float32)
    d_ffn = grad_seed.astype(jnp.bfloat16)
    grad_back = rows_product(act, d_ffn)
    grad_bias_back = jnp.sum(d_ffn.astype(jnp.float32), axis=0)
    d_pre = pull_act(cols_product(d_ffn, back_w))[0].astype(jnp.bfloat16)
    grad_in = rows_product(h_two, d_pre)
    grad_bias_in = jnp.sum(d_pre.astype(jnp.float32), axis=0)
    d_resid, grad_gain_two, grad_shift_two = pull_two(cols_product(d_pre, in_w))
    d_resid = d_resid + grad_seed
    d_attn = d_resid.astype(jnp.bfloat16)
    grad_out = rows_product(mixed, d_attn)
    d_mix = cols_product(d_attn, out_w)
    grad_blend_near = jnp.sum(d_mix * near_out, axis=0)
    grad_blend_one = jnp.sum(d_mix * far_a, axis=0)
    grad_blend_two = jnp.sum(d_mix * far_b, axis=0)
    d_near = (vec_wide[5] * d_mix).astype(jnp.bfloat16)

    def near_grad(block_id):
        mask_now = band_mask(item_pad, valid_pad, item_rows, block_id)
        block_query, block_keys, block_values = block_inputs(
            query_all, key_pad, value_pad, block_id
        )
        probs = band_probs(block_query, block_keys, mask_now)
        probs_low = probs.astype(jnp.bfloat16)
        d_block = lax.dynamic_slice_in_dim(d_near, block_id * BLOCK, BLOCK, 0).reshape(
            BLOCK, HEADS, head_size
        )
        d_probs = jnp.einsum(
            "qhe,khe->hqk", d_block, block_values, preferred_element_type=jnp.float32
        )
        d_values = jnp.einsum(
            "hqk,qhe->khe", probs_low, d_block, preferred_element_type=jnp.float32
        )
        d_scores = (probs * (d_probs - jnp.sum(probs * d_probs, axis=-1, keepdims=True))).astype(
            jnp.bfloat16
        )
        d_query = (
            jnp.einsum("hqk,khd->qhd", d_scores, block_keys, preferred_element_type=jnp.float32)
            * score_scale
        )
        d_keys = (
            jnp.einsum("hqk,qhd->khd", d_scores, block_query, preferred_element_type=jnp.float32)
            * score_scale
        )
        return (
            d_query.reshape(BLOCK, model_width),
            d_keys.reshape(BLOCK + 2 * BAND, model_width),
            d_values.reshape(BLOCK + 2 * BAND, model_width),
        )

    dq_near, dk_extended, dv_extended = lax.map(near_grad, block_ids)
    dq_far, dk_far, dv_far = pull_far((vec_wide[6] * d_mix, vec_wide[7] * d_mix))
    d_qkv = jnp.concatenate(
        [
            dq_near.reshape(row_count, model_width) + dq_far,
            fold_back(dk_extended, row_count) + dk_far,
            fold_back(dv_extended, row_count) + dv_far,
        ],
        axis=1,
    ).astype(jnp.bfloat16)
    grad_qkv = rows_product(h_one, d_qkv)
    d_tokens, grad_gain_one, grad_shift_one = pull_one(cols_product(d_qkv, qkv_w))
    tokens_grad = (d_tokens + d_resid).astype(jnp.bfloat16)
    grad_vec = jnp.stack(
        [
            grad_gain_one,
            grad_shift_one,
            grad_gain_two,
            grad_shift_two,
            grad_bias_back,
            grad_blend_near,
            grad_blend_one,
            grad_blend_two,
        ],
        axis=0,
    )
    owned = spread(grad_qkv, grad_out, grad_in, grad_back, grad_vec, grad_bias_in)
    return (layer_out, tokens_grad, owned[0], owned[1], owned[2], owned[3], owned[4], owned[5])


def solution(mesh):
    in_specs = (
        P(("dp", "fsdp"), None),
        P(("dp", "fsdp"), None),
        P("fsdp", "dp"),
        P("fsdp", "dp"),
        P("fsdp", "dp"),
        P("fsdp", "dp"),
        P("dp", "fsdp"),
        P(("dp", "fsdp")),
        P(("dp", "fsdp"), None),
        P(("dp", "fsdp"), None),
    )
    out_specs = (
        P(("dp", "fsdp"), None),
        P(("dp", "fsdp"), None),
        P("fsdp", "dp"),
        P("fsdp", "dp"),
        P("fsdp", "dp"),
        P("fsdp", "dp"),
        P("dp", "fsdp"),
        P(("dp", "fsdp")),
    )
    return jax.shard_map(shards, mesh=mesh, in_specs=in_specs, out_specs=out_specs, check_vma=False)
```

profile of v0, /device:TPU:0, one launch (start us, length us, event | category | flops | bytes accessed | tf_op | source)
XLA Modules:
  0.0 1965.9 jit_solution(929732776186088824)
XLA Ops:
  7.2 35.2 %all_gather.48 = bf16[512,384]{1,0:T(8,128)(2,1)} all-gather(bf16[64,384]{1,0:T(8,128)(2,1)} %param.16), channel_id=1, replica_groups=mesh['dp'=4,'fsdp'=8] {'fsdp'}, dimensions={0}, use_global_device_ids=true | all-gather | bytes 442368 | tf_op jit(solution)/shard_map/all_gather | solution.py:135
  42.4 33.7 %all_gather.52 = bf16[512,512]{1,0:T(8,128)(2,1)} all-gather(bf16[64,512]{1,0:T(8,128)(2,1)} %param.18), channel_id=1, replica_groups=mesh['dp'=4,'fsdp'=8] {'fsdp'}, dimensions={0}, use_global_device_ids=true | all-gather | bytes 589824 | tf_op jit(solution)/shard_map/all_gather | solution.py:137
  76.2 33.6 %all_gather.56 = bf16[2048,128]{1,0:T(8,128)(2,1)} all-gather(bf16[256,128]{1,0:T(8,128)(2,1)} %param.19), channel_id=1, replica_groups=mesh['dp'=4,'fsdp'=8] {'fsdp'}, dimensions={0}, use_global_device_ids=true | all-gather | bytes 589824 | tf_op jit(solution)/shard_map/all_gather | solution.py:138
  128.8 20.5 %all-gather = bf16[8,64,2]{1,2,0:T(2,128)(2,1)S(1)} all-gather(bf16[1,64,2]{1,2,0:T(2,128)(2,1)S(1)} %bitcast.335), channel_id=1, replica_groups=mesh['dp'=4,'fsdp'=8] {'fsdp'}, dimensions={0}, use_global_device_ids=true | all-gather | bytes 2304 | tf_op jit(solution)/shard_map/all_gather | solution.py:139
  155.3 30.5 %all_gather.50 = bf16[512,128]{1,0:T(8,128)(2,1)S(1)} all-gather(bf16[64,128]{1,0:T(8,128)(2,1)S(1)} %copy-done.61), channel_id=1, replica_groups=mesh['dp'=4,'fsdp'=8] {'fsdp'}, dimensions={0}, use_global_device_ids=true | all-gather | bytes 147456 | tf_op jit(solution)/shard_map/all_gather | solution.py:136
  195.0 17.1 all-reduce.10
  385.3 14.4 reshape.658
  431.9 138.0 %while.28 = (s32[]{:T(128)}, f32[8,512,512]{2,1,0:T(8,128)}, s32[8]{0:T(128)S(1)}, bf16[4156,512]{0,1:T(8,128)(2,1)}, s32[4096]{0:T(1024)S(1)}, /*index=5*/s32[4...) while((s32[]{:T(128)}, f32[8,512,512]{2,1,0:T(8,128)}, ...), condition=%wide.region_5.6_spmd, body=%wide.region_2.5_spmd.sunk | while | flops 616188096 | bytes 29717792 | solution.py:222
  628.1 27.0 %multiply_convert_fusion.1 = (bf16[4096,2048]{1,0:T(8,128)(2,1)}, f32[4096,2048]{1,0:T(8,128)}) fusion(f32[2048]{0:T(1024)S(1)} %bitcast.326, bf16[512,2048]{1,0:T(8,128)(2,1)} %all-gather.9.cloned.1.call-done, f32[4096,512]{0,1:T(8,128)} %copy-done.4, f32[512]{0:T(512)S(1)} %bitcast.331, f32[512]{0:T(512)S(1)} %bitcast.320, f32[4096]{0:T(1024)S(1)} %fusion.147, ...), kind=kOutput, calls=%fused_computation.67 | convolution fusion | flops 8684306432 | bytes 60862464 | tf_op jit(solution)/shard_map/dot_general | solution.py:237
  655.1 39.3 %fusion.171 = (bf16[2048]{0:T(1024)(128)(2,1)}, bf16[4096,2048]{1,0:T(8,128)(2,1)}) fusion(f32[4096,2048]{1,0:T(8,128)} %get-tuple-element.453, f32[2048]{0:T(1024)S(1)} %bitcast.327, bf16[2048,512]{1,0:T(8,128)(2,1)} %all-gather.11.cloned.1.call-done, bf16[4096,512]{0,1:T(8,128)(2,1)} %copy.157, f32[4096]{0:T(1024)S(1)} %copy-done.32), kind=kOutput, calls=%fused_computation.274 | convolution fusion | flops 8780773376 | bytes 56651776 | tf_op jit(solution)/shard_map/dot_general | solution.py:128
  694.4 15.0 fusion.170
  738.4 17.0 multiply_reduce_fusion.1
  795.1 14.4 fusion.62
  813.8 419.5 %while.29 = (s32[]{:T(128)}, f32[8,512,512]{2,1,0:T(8,128)}, f32[8,572,512]{2,1,0:T(8,128)}, f32[8,572,512]{2,1,0:T(8,128)}, s32[8]{0:T(128)S(1)}, /*index=5*/bf...) while((s32[]{:T(128)}, f32[8,512,512]{2,1,0:T(8,128)}, ...), condition=%wide.region_15.16_spmd, body=%wide.region_11.15_spmd.sunk | while | flops 1532817664 | bytes 99411808 | solution.py:296
  1291.7 15.9 fusion.72
  1307.7 23.4 %fusion.58 = f32[4,1024,8,64]{1,3,2,0:T(8,128)} fusion(f32[4,1024,8,64]{1,3,2,0:T(8,128)S(1)} %bitcast.273, f32[4,8,1024,64]{2,3,1,0:T(8,128)} %fusion.64, f32[4,8,64]{2,1,0:T(8,128)S(1)} %copy-done.62, f32[4,8,1024]{2,1,0:T(8,128)S(1)} %get-tuple-element.434, f32[4,8,64,1024]{3,0,2,1:T(4,128)} %multiply_bitcast_fusion, f32[4,8,64,64]{3,0,2,1:T(4,128)S(1)} %copy-done.17), kind=kOutput, calls=%fused_computation.106 | convolution fusion | flops 1639972864 | bytes 34217984 | tf_op jit(solution)/shard_map/transpose(jvp(srhd,shde->srhe))/dot_general | solution.py:102
  1388.7 15.3 fusion.99
  1537.6 16.5 convolution_convert_fusion.1
  1649.8 16.3 multiply_convert_fusion.3
  1672.5 19.4 all-reduce.13
  1697.8 62.7 %reduce-scatter.20.cloned.1.call-done = f32[64,128]{1,0:T(8,128)} async-done(((f32[512,128]{1,0:T(8,128)}), f32[64,128]{1,0:T(8,128)}) %reduce-scatter.20.cloned.1.call-update) | async-done | bytes 32784 | tf_op jit(solution)/shard_map/reduce_scatter | solution.py:175
  1760.5 65.3 %reduce-scatter.18.cloned.1.call-done = f32[64,384]{1,0:T(8,128)} async-done(((f32[512,384]{1,0:T(8,128)}), f32[64,384]{1,0:T(8,128)}) %reduce-scatter.18.cloned.1.call-update) | async-done | bytes 98320 | tf_op jit(solution)/shard_map/reduce_scatter | solution.py:174
  1825.8 66.8 %reduce-scatter.24.cloned.1.call-done = f32[64,512]{1,0:T(8,128)} async-done(((f32[512,512]{1,0:T(8,128)}), f32[64,512]{1,0:T(8,128)}) %reduce-scatter.24.cloned.1.call-update) | async-done | bytes 131088 | tf_op jit(solution)/shard_map/reduce_scatter | solution.py:176
  1892.6 66.2 %reduce-scatter.26.cloned.1.call-done = f32[256,128]{1,0:T(8,128)} async-done(((f32[2048,128]{1,0:T(8,128)}), f32[256,128]{1,0:T(8,128)}) %reduce-scatter.26.cloned.1.call-update) | async-done | bytes 131088 | tf_op jit(solution)/shard_map/reduce_scatter | solution.py:177
  (667 shorter events, 1268.6 us)
Async XLA Ops:
  7.2 217.5 %all-gather.7.cloned.1.call-start = ((), (), s32[]{:S(2)}) async-start(), calls=%async_computation.9 | async-start | bytes 1966080 | tf_op jit(solution)/shard_map/all_gather | solution.py:143
  42.4 585.7 %all-gather.9.cloned.1.call-start = ((), (), s32[]{:S(2)}) async-start(), calls=%async_computation.10 | async-start | bytes 2621440 | tf_op jit(solution)/shard_map/all_gather | solution.py:145
  76.1 578.9 %all-gather.11.cloned.1.call-start = ((), (), s32[]{:S(2)}) async-start(), calls=%async_computation.11 | async-start | bytes 2621440 | tf_op jit(solution)/shard_map/all_gather | solution.py:146
  109.8 1510.8 %reduce-scatter.30.cloned.1.call-start = ((), (), s32[]{:S(2)}) async-start(), calls=%async_computation.18 | async-start | bytes 655360
  112.5 457.4 %copy-start.49 = (s32[4]{0:T(128)}, s32[4]{0:T(128)S(1)}, u32[]{:S(2)}) copy-start(s32[4]{0:T(128)S(1)} %compare_select_fusion.5) | copy-start | bytes 52
  113.2 201.0 %copy-start.25 = (f32[4,1024]{1,0:T(4,128)}, f32[4,1024]{1,0:T(4,128)S(1)}, u32[]{:S(2)}) copy-start(f32[4,1024]{1,0:T(4,128)S(1)} %fusion.144) | copy-start | bytes 49156
  115.2 78.2 %copy-start.76 = (u32[32]{0:T(128)S(1)}, u32[32]{0:T(128)}, u32[]{:S(2)}) copy-start(u32[32]{0:T(128)} %constant.299) | copy-start | bytes 388
  115.2 79.5 %copy-start.80 = (bf16[64]{0:T(256)(128)(2,1)S(1)}, bf16[64]{0:T(256)(128)(2,1)}, u32[]{:S(2)}) copy-start(bf16[64]{0:T(256)(128)(2,1)} %param.21) | copy-start | bytes 388
  124.9 109.4 %copy-start.29 = (f32[4096]{0:T(1024)}, f32[4096]{0:T(1024)S(1)}, u32[]{:S(2)}) copy-start(f32[4096]{0:T(1024)S(1)} %broadcast_multiply_fusion.3) | copy-start | bytes 49156
  128.8 105.4 %copy-start.39 = (f32[4096]{0:T(1024)}, f32[4096]{0:T(1024)S(1)}, u32[]{:S(2)}) copy-start(f32[4096]{0:T(1024)S(1)} %fusion.146) | copy-start | bytes 49156
  155.2 79.0 %copy-start.51 = (f32[1,512]{1,0:T(1,128)}, f32[1,512]{1,0:T(1,128)S(1)}, u32[]{:S(2)}) copy-start(f32[1,512]{1,0:T(1,128)S(1)} %get-tuple-element.442) | copy-start | bytes 6148
  155.2 79.0 %copy-start.74 = (f32[1,512]{1,0:T(1,128)}, f32[1,512]{1,0:T(1,128)S(1)}, u32[]{:S(2)}) copy-start(f32[1,512]{1,0:T(1,128)S(1)} %get-tuple-element.441) | copy-start | bytes 6148
  155.3 69.5 %copy-start.31 = (f32[4096]{0:T(1024)}, f32[4096]{0:T(1024)S(1)}, u32[]{:S(2)}) copy-start(f32[4096]{0:T(1024)S(1)} %fusion.145) | copy-start | bytes 49156
  431.9 140.9 %copy-start.63 = (f32[4]{0:T(128)S(1)}, f32[4]{0:T(128)}, u32[]{:S(2)}) copy-start(f32[4]{0:T(128)} %convert_divide_fusion) | copy-start | bytes 52
  623.8 102.8 %copy-start.34 = (f32[4096]{0:T(1024)}, f32[4096]{0:T(1024)S(1)}, u32[]{:S(2)}) copy-start(f32[4096]{0:T(1024)S(1)} %broadcast_multiply_fusion.2) | copy-start | bytes 49156
  628.0 98.6 %copy-start.45 = (f32[4096]{0:T(1024)}, f32[4096]{0:T(1024)S(1)}, u32[]{:S(2)}) copy-start(f32[4096]{0:T(1024)S(1)} %fusion.147) | copy-start | bytes 49156
  1485.2 137.2 %reduce-scatter.28.cloned.1.call-start = ((), (), s32[]{:S(2)}) async-start(), calls=%async_computation.17 | async-start | bytes 1966080
  1537.5 87.3 %reduce-scatter.22.cloned.1.call-start = ((), (), s32[]{:S(2)}) async-start(), calls=%async_computation.14 | async-start | bytes 2621440 | tf_op jit(solution)/shard_map/reduce_scatter | solution.py:160
  1554.1 93.2 %reduce-scatter.32.cloned.1.call-start = ((), (), s32[]{:S(2)}) async-start(), calls=%async_computation.19 | async-start | bytes 2621440
  1570.6 125.8 %reduce-scatter.34.cloned.1.call-start = ((), (), s32[]{:S(2)}) async-start(), calls=%async_computation.20 | async-start | bytes 294912
  1620.6 140.0 %reduce-scatter.20.cloned.1.call-start = ((), (), s32[]{:S(2)}) async-start(), calls=%async_computation.13 | async-start | bytes 294912 | tf_op jit(solution)/shard_map/reduce_scatter | solution.py:175
  1622.4 203.4 %reduce-scatter.18.cloned.1.call-start = ((), (), s32[]{:S(2)}) async-start(), calls=%async_computation.12 | async-start | bytes 884736 | tf_op jit(solution)/shard_map/reduce_scatter | solution.py:174
  1624.7 267.9 %reduce-scatter.24.cloned.1.call-start = ((), (), s32[]{:S(2)}) async-start(), calls=%async_computation.15 | async-start | bytes 1179648 | tf_op jit(solution)/shard_map/reduce_scatter | solution.py:176
  1626.9 331.9 %reduce-scatter.26.cloned.1.call-start = ((), (), s32[]{:S(2)}) async-start(), calls=%async_computation.16 | async-start | bytes 1179648 | tf_op jit(solution)/shard_map/reduce_scatter | solution.py:177
  (87 other events, 950.0 us)
Sparse Core Ops, SparseCore 0:
  42.5 20.5 all-gather.6
  76.3 23.6 all-gather.8
  109.9 23.9 all-gather.10
  1485.4 19.7 reduce-scatter.29
  1537.6 26.1 reduce-scatter.27
  1566.2 31.4 reduce-scatter.21
  1600.3 31.4 reduce-scatter.31
  1635.2 61.1 reduce-scatter.33
  1700.3 60.1 reduce-scatter.19
  1764.2 61.5 reduce-scatter.17
  1830.2 62.3 reduce-scatter.23
  1896.4 62.3 reduce-scatter.25
where the time goes:
time: 1980 us; the launch traced here: 1970 us
  matrix products  674 us (34%)
  local copies, waits for them, and re-layouts  543 us (27%)
  waiting for transfers between devices  265 us (13%)
  other arithmetic  234 us (12%)
  blocking collectives  218 us (11%)
    sub x16, matrix products, band_probs(): exp_scores = jnp.exp(scores - jnp.max(scores, axis=-1, keepdims=True))  94.9 us
    convert_element_type x8, other arithmetic, near_grad(): (probs * (d_probs - jnp.sum(probs * d_probs, axis=-1, keepdims=True))).as...  88.6 us
    dot_general x4, matrix products, cols_product(): lax.dot_general(left_side, right_side, (((1,), (1,)), ((), ())), preferre...  83.8 us
    reduce_scatter x1, waiting for transfers between devices, spread(): lax.psum_scatter(section_one[2], 'fsdp', scatter_dimension=0, tiled=True)  66.8 us
    reduce_scatter x1, waiting for transfers between devices, spread(): lax.psum_scatter(section_one[3], 'fsdp', scatter_dimension=0, tiled=True)  66.2 us
    reduce_scatter x1, waiting for transfers between devices, spread(): lax.psum_scatter(section_one[0], 'fsdp', scatter_dimension=0, tiled=True)  65.3 us
    unnamed x205, local copies, waits for them, and re-layouts  63.6 us
    reduce_scatter x1, waiting for transfers between devices, spread(): lax.psum_scatter(section_one[1], 'fsdp', scatter_dimension=0, tiled=True)  62.7 us
  transfers between devices with their start and end apart: 12, of which 5 were waited for; matrix products, arithmetic and copies ran while one was open for 32% of the time, Pallas kernels for 0%

commit v1 on v0

v1 whole, which is shorter than its diff:
```python
import functools
import math

import jax
import jax.numpy as jnp
import numpy as np
from jax import lax
from jax.experimental import pallas as pl
from jax.experimental.pallas import tpu as pltpu
from jax.sharding import PartitionSpec as P

HEADS = 8
BAND = 30
QB = 64
HALO = 32
KW = QB + 2 * HALO
GW = 256

norm_eps = 1e-05
f32 = jnp.float32
bf16 = jnp.bfloat16
exact = lax.Precision.HIGHEST
VMEM_LIMIT = 60 * 1024 * 1024


def nn(a, b):
    return lax.dot_general(a, b, (((1,), (0,)), ((), ())), preferred_element_type=f32)


def nt(a, b):
    return lax.dot_general(a, b, (((1,), (1,)), ((), ())), preferred_element_type=f32)


def tn(a, b):
    return lax.dot_general(a, b, (((0,), (0,)), ((), ())), preferred_element_type=f32)


def nt_exact(a, b):
    return lax.dot_general(
        a, b, (((1,), (1,)), ((), ())), preferred_element_type=f32, precision=exact
    )


def lift(t):
    return jnp.where(t > 0, t + 1.0, jnp.exp(jnp.minimum(t, 0.0)))


def moments(x):
    mean = jnp.mean(x, axis=-1, keepdims=True)
    cen = x - mean
    inv = lax.rsqrt(jnp.mean(cen * cen, axis=-1, keepdims=True) + norm_eps)
    return cen * inv, inv


def fold8(x):
    return jnp.sum(x.reshape(x.shape[0] // 8, 8, x.shape[1]), axis=0)


def row_valid(step, rows, width, length):
    ids = step * rows + lax.broadcasted_iota(jnp.int32, (rows, width), 0)
    return ids < length


def same_head(head):
    r = lax.broadcasted_iota(jnp.int32, (GW, GW), 0) // head
    c = lax.broadcasted_iota(jnp.int32, (GW, GW), 1) // head
    return r == c


def spread_rows(x, mask_low):
    return jnp.concatenate([x] * (GW // QB), axis=0) * mask_low


def pick_heads(x, head):
    lane = lax.broadcasted_iota(jnp.int32, (QB, GW), 1) // head
    out = x[:QB]
    for h in range(1, GW // QB):
        out = jnp.where(lane == h, x[h * QB : (h + 1) * QB], out)
    return out


def qkv_kernel(len_ref, tok_ref, vec_ref, w_ref, qkv_ref, m1_ref, m2_ref, c_ref, st_ref, t_ref):
    step = pl.program_id(0)
    rows, width = tok_ref.shape
    groups = width // GW
    head = width // HEADS
    length = len_ref[0, 0]

    @pl.when(step == 0)
    def _():
        st_ref[...] = jnp.zeros_like(st_ref)
        t_ref[...] = jnp.zeros_like(t_ref)

    z, _ = moments(tok_ref[...].astype(f32))
    h = (z * vec_ref[0:1] + vec_ref[1:2]).astype(bf16)
    qkv_ref[:, :width] = nn(h, w_ref[:, :width]).astype(bf16)
    valid = row_valid(step, rows, GW, length)
    for g in range(groups):
        kc = slice(width + g * GW, width + (g + 1) * GW)
        vc = slice(2 * width + g * GW, 2 * width + (g + 1) * GW)
        k = nn(h, w_ref[:, kc]).astype(bf16)
        v = nn(h, w_ref[:, vc]).astype(bf16)
        qkv_ref[:, kc] = k
        qkv_ref[:, vc] = v
        kw = k.astype(f32)
        phi = jnp.where(valid, lift(kw), 0.0)
        bent = jnp.where(valid, jnp.tanh(kw), 0.0)
        both = jnp.concatenate([phi.astype(bf16), bent.astype(bf16)], axis=1)
        st_ref[g] += tn(v, both)
        t_ref[g] += fold8(phi)

    @pl.when(step == pl.num_programs(0) - 1)
    def _():
        mask = same_head(head).astype(f32)
        inv_len = 1.0 / length.astype(f32)
        ones = jnp.ones((8, GW), f32)
        for g in range(groups):
            tb = jnp.sum(t_ref[g], axis=0, keepdims=True) * mask
            s1 = st_ref[g][:, :GW] * mask
            s2 = st_ref[g][:, GW:] * mask
            c_col = jnp.sum(s1, axis=1, keepdims=True) / jnp.sum(tb, axis=1, keepdims=True)
            c_row = nt_exact(ones, s1) / nt_exact(ones, tb)
            m1_ref[g, :GW] = (s1 - c_col * tb).astype(bf16)
            m1_ref[g, GW:] = tb.astype(bf16)
            m2_ref[g] = (s2 * inv_len).astype(bf16)
            c_ref[g] = c_row


def first_pass(length, tokens, vecs, w_qkv, tile):
    rows, width = tokens.shape
    groups = width // GW
    const = lambda *shape: pl.BlockSpec(shape, lambda i: (0,) * len(shape))
    return pl.pallas_call(
        qkv_kernel,
        grid=(rows // tile,),
        in_specs=[
            pl.BlockSpec(memory_space=pltpu.SMEM),
            pl.BlockSpec((tile, width), lambda i: (i, 0)),
            const(8, width),
            const(width, 3 * width),
        ],
        out_specs=[
            pl.BlockSpec((tile, 3 * width), lambda i: (i, 0)),
            const(groups, 2 * GW, GW),
            const(groups, GW, GW),
            const(groups, 8, GW),
        ],
        out_shape=[
            jax.ShapeDtypeStruct((rows, 3 * width), bf16),
            jax.ShapeDtypeStruct((groups, 2 * GW, GW), bf16),
            jax.ShapeDtypeStruct((groups, GW, GW), bf16),
            jax.ShapeDtypeStruct((groups, 8, GW), f32),
        ],
        scratch_shapes=[
            pltpu.VMEM((groups, GW, 2 * GW), f32),
            pltpu.VMEM((groups, 8, GW), f32),
        ],
        compiler_params=pltpu.CompilerParams(vmem_limit_bytes=VMEM_LIMIT),
        cost_estimate=pl.CostEstimate(
            flops=2 * rows * width * 4 * width, bytes_accessed=rows * width * 8, transcendentals=0
        ),
        name="first_pass",
    )(length, tokens, vecs, w_qkv)


def mix_kernel(
    len_ref,
    q_ref,
    k_lo,
    k_ref,
    k_hi,
    v_lo,
    v_ref,
    v_hi,
    m1_ref,
    m2_ref,
    c_ref,
    band_ref,
    hm_ref,
    near_ref,
    fa_ref,
    fb_ref,
    rn_ref,
    p_ref,
    kk,
    vv,
):
    step = pl.program_id(0)
    rows, width = q_ref.shape
    groups = width // GW
    head = width // HEADS
    scale = head ** (-0.5)
    length = len_ref[0, 0]
    kk[:HALO] = k_lo[...]
    kk[HALO : HALO + rows] = k_ref[...]
    kk[HALO + rows :] = k_hi[...]
    vv[:HALO] = v_lo[...]
    vv[HALO : HALO + rows] = v_ref[...]
    vv[HALO + rows :] = v_hi[...]
    hm = hm_ref[...]
    for b in range(rows // QB):
        base = step * rows + b * QB - HALO
        key = base + lax.broadcasted_iota(jnp.int32, (KW, GW), 0)
        bias = jnp.where((key >= 0) & (key < length), band_ref[...], -1e30)
        for g in range(groups):
            cols = slice(g * GW, (g + 1) * GW)
            qs = spread_rows(q_ref[b * QB : (b + 1) * QB, cols] * scale, hm)
            s = nt(kk[b * QB : b * QB + KW, cols], qs) + bias
            e = jnp.exp(s - jnp.max(s, axis=0, keepdims=True))
            p = (e * (1.0 / jnp.sum(e, axis=0, keepdims=True))).astype(bf16)
            p_ref[b, :, cols] = p
            o = tn(p, vv[b * QB : b * QB + KW, cols])
            near_ref[b * QB : (b + 1) * QB, cols] = pick_heads(o, head).astype(bf16)
    for g in range(groups):
        cols = slice(g * GW, (g + 1) * GW)
        q = q_ref[:, cols].astype(f32)
        both = nt(lift(q).astype(bf16), m1_ref[g])
        rn = 1.0 / both[:, GW:]
        rn_ref[:, cols] = rn.astype(bf16)
        fa_ref[:, cols] = (both[:, :GW] * rn).astype(bf16)
        fb_ref[:, cols] = nt(jnp.tanh(q).astype(bf16), m2_ref[g]).astype(bf16)


def halo_specs(tile, width, col, rows):
    per = tile // HALO
    last = rows // HALO - 1
    return [
        pl.BlockSpec((HALO, width), lambda i: (jnp.maximum(i * per - 1, 0), col)),
        pl.BlockSpec((tile, width), lambda i: (i, col)),
        pl.BlockSpec((HALO, width), lambda i: (jnp.minimum((i + 1) * per, last), col)),
    ]


def band_table(head):
    key = np.arange(KW)[:, None] - HALO
    query = np.arange(GW)[None, :] % QB
    return np.where(np.abs(key - query) <= BAND, 0.0, -1e30).astype(np.float32)


def head_table(head):
    r = np.arange(GW)[:, None] // QB
    c = np.arange(GW)[None, :] // head
    return (r == c).astype(np.float32)


def second_pass(length, qkv, m1, m2, c, tile):
    rows = qkv.shape[0]
    width = qkv.shape[1] // 3
    groups = width // GW
    const = lambda *shape: pl.BlockSpec(shape, lambda i: (0,) * len(shape))
    block = pl.BlockSpec((tile, width), lambda i: (i, 0))
    head = width // HEADS
    return pl.pallas_call(
        mix_kernel,
        grid=(rows // tile,),
        in_specs=[
            pl.BlockSpec(memory_space=pltpu.SMEM),
            block,
            *halo_specs(tile, width, 1, rows),
            *halo_specs(tile, width, 2, rows),
            const(groups, 2 * GW, GW),
            const(groups, GW, GW),
            const(groups, 8, GW),
            const(KW, GW),
            const(GW, GW),
        ],
        out_specs=[
            block,
            block,
            block,
            block,
            pl.BlockSpec((tile // QB, KW, width), lambda i: (i, 0, 0)),
        ],
        out_shape=[jax.ShapeDtypeStruct((rows, width), bf16)] * 4
        + [jax.ShapeDtypeStruct((rows // QB, KW, width), bf16)],
        scratch_shapes=[pltpu.VMEM((tile + 2 * HALO, width), bf16)] * 2,
        compiler_params=pltpu.CompilerParams(vmem_limit_bytes=VMEM_LIMIT),
        cost_estimate=pl.CostEstimate(
            flops=2 * rows * width * 4 * width, bytes_accessed=rows * width * 18, transcendentals=0
        ),
        name="second_pass",
    )(
        length,
        qkv,
        qkv,
        qkv,
        qkv,
        qkv,
        qkv,
        qkv,
        m1,
        m2,
        c,
        jnp.asarray(band_table(head)),
        jnp.asarray(head_table(head), bf16),
    )


def ffn_kernel(
    chunk,
    len_ref,
    tok_ref,
    cot_ref,
    near_ref,
    fa_ref,
    fb_ref,
    rn_ref,
    q_ref,
    c_ref,
    vec_ref,
    bin_ref,
    wout_ref,
    win_ref,
    wback_ref,
    out_ref,
    datt_ref,
    dmix_ref,
    dn_ref,
    gin_ref,
    gback_ref,
    gout_ref,
    gvec_ref,
    gbias_ref,
    m3_ref,
    m4_ref,
    dt_ref,
    a_in,
    a_back,
    a_out,
    a_st,
    a_bent,
):
    step = pl.program_id(0)
    rows, width = tok_ref.shape
    hidden = win_ref.shape[1]
    groups = width // GW
    head = width // HEADS
    length = len_ref[0, 0]

    @pl.when(step == 0)
    def _():
        a_in[...] = jnp.zeros_like(a_in)
        a_back[...] = jnp.zeros_like(a_back)
        a_out[...] = jnp.zeros_like(a_out)
        a_st[...] = jnp.zeros_like(a_st)
        a_bent[...] = jnp.zeros_like(a_bent)
        gvec_ref[...] = jnp.zeros_like(gvec_ref)
        gbias_ref[...] = jnp.zeros_like(gbias_ref)

    c_row = jnp.concatenate([c_ref[g, 0:1] for g in range(groups)], axis=1)
    near = near_ref[...].astype(f32)
    fac = fa_ref[...].astype(f32)
    far_b = fb_ref[...].astype(f32)
    mixed = (
        vec_ref[5:6] * near + vec_ref[6:7] * (fac + c_row) + vec_ref[7:8] * far_b
    ).astype(bf16)
    resid = tok_ref[...].astype(f32) + nn(mixed, wout_ref[...])
    z2, r2 = moments(resid)
    h2 = (z2 * vec_ref[2:3] + vec_ref[3:4]).astype(bf16)
    valid = row_valid(step, rows, width, length)
    seed = jnp.where(valid, cot_ref[...].astype(f32), 0.0)
    d_ffn = seed.astype(bf16)
    s0 = math.sqrt(2.0 / math.pi)
    s1 = s0 * 0.044715
    ffn = jnp.zeros((rows, width), f32)
    dh2 = jnp.zeros((rows, width), f32)
    for lo in range(0, hidden, chunk):
        cols = slice(lo, lo + chunk)
        x = nn(h2, win_ref[:, cols]) + bin_ref[0:1, cols]
        x2 = x * x
        t = jnp.tanh(x * (s0 + s1 * x2))
        half = 0.5 + 0.5 * t
        act = x * half
        slope = half + (act - act * half) * (2 * s0 + 6 * s1 * x2)
        act = act.astype(bf16)
        ffn += nn(act, wback_ref[cols, :])
        a_back[:, cols] += tn(d_ffn, act)
        d_pre = slope * nt(d_ffn, wback_ref[cols, :])
        gbias_ref[:, cols] += fold8(d_pre)
        d_pre = d_pre.astype(bf16)
        a_in[:, cols] += tn(h2, d_pre)
        dh2 += nt(d_pre, win_ref[:, cols])
    out_ref[...] = jnp.where(valid, resid + ffn + vec_ref[4:5], 0.0).astype(bf16)
    gvec_ref[2] += fold8(dh2 * z2)
    gvec_ref[3] += fold8(dh2)
    gvec_ref[4] += fold8(seed)
    dz = dh2 * vec_ref[2:3]
    d_resid = seed + r2 * (
        dz
        - jnp.mean(dz, axis=-1, keepdims=True)
        - z2 * jnp.mean(dz * z2, axis=-1, keepdims=True)
    )
    d_attn = d_resid.astype(bf16)
    datt_ref[...] = d_attn
    a_out[...] += tn(mixed, d_attn)
    d_mix = nt(d_attn, wout_ref[...])
    dmix_ref[...] = d_mix.astype(bf16)
    gvec_ref[5] += fold8(d_mix * near)
    gvec_ref[6] += fold8(d_mix * fac)
    gvec_ref[7] += fold8(d_mix * far_b)
    gvec_ref[0] += fold8(d_mix)
    d_num = (vec_ref[6:7] * d_mix * rn_ref[...].astype(f32)).astype(bf16)
    dn_ref[...] = d_num
    d_den = (d_num.astype(f32) * fac).astype(bf16)
    d_far = (vec_ref[7:8] * d_mix).astype(bf16)
    for g in range(groups):
        cols = slice(g * GW, (g + 1) * GW)
        q = q_ref[:, cols].astype(f32)
        a_st[g] += tn(lift(q).astype(bf16), jnp.concatenate([d_num[:, cols], d_den[:, cols]], axis=1))
        a_bent[g] += tn(jnp.tanh(q).astype(bf16), d_far[:, cols])

    @pl.when(step == pl.num_programs(0) - 1)
    def _():
        mask = same_head(head).astype(f32)
        inv_len = 1.0 / length.astype(f32)
        ones = jnp.ones((8, GW), f32)
        for g in range(groups):
            m3_ref[g] = (a_st[g][:, :GW] * mask).astype(bf16)
            m4_ref[g] = (a_bent[g] * mask * inv_len).astype(bf16)
            dt_ref[g] = -nt_exact(ones, a_st[g][:, GW:] * mask)
        gin_ref[...] = a_in[...].astype(gin_ref.dtype)
        gback_ref[...] = a_back[...].astype(gback_ref.dtype)
        gout_ref[...] = a_out[...].astype(gout_ref.dtype)
        gvec_ref[6] += gvec_ref[0] * c_row


def third_pass(length, tokens, cot, near, fa, fb, rn, qkv, c, vecs, b_in, w_out, w_in, w_back, tile, chunk):
    rows, width = tokens.shape
    hidden = w_in.shape[1]
    groups = width // GW
    const = lambda *shape: pl.BlockSpec(shape, lambda i: (0,) * len(shape))
    block = pl.BlockSpec((tile, width), lambda i: (i, 0))
    sds = jax.ShapeDtypeStruct
    return pl.pallas_call(
        functools.partial(ffn_kernel, chunk),
        grid=(rows // tile,),
        in_specs=[pl.BlockSpec(memory_space=pltpu.SMEM)]
        + [block] * 7
        + [
            const(groups, 8, GW),
            const(8, width),
            const(1, hidden),
            const(width, width),
            const(width, hidden),
            const(hidden, width),
        ],
        out_specs=[block] * 4
        + [
            const(width, hidden),
            const(width, hidden),
            const(width, width),
            const(8, 8, width),
            const(8, hidden),
            const(groups, GW, GW),
            const(groups, GW, GW),
            const(groups, 8, GW),
        ],
        out_shape=[sds((rows, width), bf16)] * 4
        + [
            sds((width, hidden), bf16),
            sds((width, hidden), bf16),
            sds((width, width), bf16),
            sds((8, 8, width), f32),
            sds((8, hidden), f32),
            sds((groups, GW, GW), bf16),
            sds((groups, GW, GW), bf16),
            sds((groups, 8, GW), f32),
        ],
        scratch_shapes=[
            pltpu.VMEM((width, hidden), f32),
            pltpu.VMEM((width, hidden), f32),
            pltpu.VMEM((width, width), f32),
            pltpu.VMEM((groups, GW, 2 * GW), f32),
            pltpu.VMEM((groups, GW, GW), f32),
        ],
        compiler_params=pltpu.CompilerParams(vmem_limit_bytes=VMEM_LIMIT),
        cost_estimate=pl.CostEstimate(
            flops=2 * rows * width * (6 * hidden + 4 * width),
            bytes_accessed=rows * width * 22,
            transcendentals=0,
        ),
        name="third_pass",
    )(length, tokens, cot, near, fa, fb, rn, qkv, c, vecs, b_in, w_out, w_in, w_back)


def back_kernel(
    len_ref,
    q_ref,
    k_lo,
    k_ref,
    k_hi,
    v_lo,
    v_ref,
    v_hi,
    p_ref,
    dmix_ref,
    qkv_ref,
    tok_ref,
    datt_ref,
    dn_ref,
    fa_ref,
    dmp_ref,
    m1_ref,
    m2_ref,
    m3_ref,
    m4_ref,
    dt_ref,
    c_ref,
    vec_ref,
    w_ref,
    hm_ref,
    dtok_ref,
    gqkv_ref,
    gvec_ref,
    kk,
    vv,
    dq_s,
    dk_s,
    dv_s,
    a_qkv,
):
    step = pl.program_id(0)
    steps = pl.num_programs(0) - 1
    rows, width = q_ref.shape
    groups = width // GW
    head = width // HEADS
    scale = head ** (-0.5)
    length = len_ref[0, 0]

    @pl.when(step == 0)
    def _():
        dk_s[: 2 * HALO] = jnp.zeros((2 * HALO, width), f32)
        dv_s[: 2 * HALO] = jnp.zeros((2 * HALO, width), f32)
        a_qkv[...] = jnp.zeros_like(a_qkv)
        gvec_ref[...] = jnp.zeros_like(gvec_ref)

    @pl.when(step < steps)
    def _():
        kk[:HALO] = k_lo[...]
        kk[HALO : HALO + rows] = k_ref[...]
        kk[HALO + rows :] = k_hi[...]
        vv[:HALO] = v_lo[...]
        vv[HALO : HALO + rows] = v_ref[...]
        vv[HALO + rows :] = v_hi[...]
        hm = hm_ref[...]
        slot = lax.rem(step, 2)
        for g in range(groups):
            cols = slice(g * GW, (g + 1) * GW)
            for b in range(rows // QB):
                here = slice(b * QB, (b + 1) * QB)
                window = slice(b * QB, b * QB + KW)
                qs = spread_rows(q_ref[here, cols] * scale, hm)
                d_near = (vec_ref[5:6, cols] * dmix_ref[here, cols].astype(f32)).astype(bf16)
                ds = spread_rows(d_near, hm)
                p = p_ref[b, :, cols]
                pw = p.astype(f32)
                t = pw * nt(vv[window, cols], ds)
                d_s = (t - pw * jnp.sum(t, axis=0, keepdims=True)).astype(bf16)
                dk = nn(d_s, qs)
                dv = nn(p, ds)
                dq_s[slot, here, cols] = pick_heads(tn(d_s, kk[window, cols]), head) * scale
                lo = pl.multiple_of(step * rows + b * QB, QB)
                dk_s[pl.ds(lo, QB), cols] += dk[:QB]
                dk_s[pl.ds(lo + QB, QB), cols] = dk[QB:]
                dv_s[pl.ds(lo, QB), cols] += dv[:QB]
                dv_s[pl.ds(lo + QB, QB), cols] = dv[QB:]

    @pl.when(step > 0)
    def _():
        slot = lax.rem(step + 1, 2)
        z1, r1 = moments(tok_ref[...].astype(f32))
        h1 = (z1 * vec_ref[0:1] + vec_ref[1:2]).astype(bf16)
        valid = row_valid(step - 1, rows, GW, length)
        lo = pl.multiple_of((step - 1) * rows + HALO, HALO)
        dqs, dks, dvs = [], [], []
        for g in range(groups):
            cols = slice(g * GW, (g + 1) * GW)
            q = qkv_ref[:, g * GW : (g + 1) * GW].astype(f32)
            k = qkv_ref[:, width + g * GW : width + (g + 1) * GW].astype(f32)
            v = qkv_ref[:, 2 * width + g * GW : 2 * width + (g + 1) * GW]
            d_num = dn_ref[:, cols]
            d_den = (d_num.astype(f32) * -fa_ref[:, cols].astype(f32)).astype(bf16)
            d_far = (vec_ref[7:8, cols] * dmp_ref[:, cols].astype(f32)).astype(bf16)
            bent_q = jnp.tanh(q)
            dq = (
                dq_s[slot, :, cols]
                + nn(jnp.concatenate([d_num, d_den], axis=1), m1_ref[g]) * jnp.minimum(lift(q), 1.0)
                + nn(d_far, m2_ref[g]) * (1.0 - bent_q * bent_q)
            )
            lift_k = lift(k)
            bent_k = jnp.tanh(k)
            v_cen = (v.astype(f32) - c_ref[g, 0:1]).astype(bf16)
            dk = (nt(v_cen, m3_ref[g]) + dt_ref[g, 0:1]) * jnp.minimum(lift_k, 1.0) + nt(
                v, m4_ref[g]
            ) * (1.0 - bent_k * bent_k)
            both = jnp.concatenate([lift_k.astype(bf16), bent_k.astype(bf16)], axis=1)
            dv = nn(both, jnp.concatenate([m3_ref[g], m4_ref[g]], axis=0))
            dqs.append(dq.astype(bf16))
            dks.append((dk_s[pl.ds(lo, rows), cols] + jnp.where(valid, dk, 0.0)).astype(bf16))
            dvs.append((dv_s[pl.ds(lo, rows), cols] + jnp.where(valid, dv, 0.0)).astype(bf16))
        d_qkv = jnp.concatenate(dqs + dks + dvs, axis=1)
        a_qkv[...] += tn(h1, d_qkv)
        dh1 = nt(d_qkv, w_ref[...])
        gvec_ref[0] += fold8(dh1 * z1)
        gvec_ref[1] += fold8(dh1)
        dz = dh1 * vec_ref[0:1]
        dtok_ref[...] = (
            datt_ref[...].astype(f32)
            + r1
            * (
                dz
                - jnp.mean(dz, axis=-1, keepdims=True)
                - z1 * jnp.mean(dz * z1, axis=-1, keepdims=True)
            )
        ).astype(bf16)

    @pl.when(step == steps)
    def _():
        gqkv_ref[...] = a_qkv[...].astype(gqkv_ref.dtype)


def fourth_pass(
    length, qkv, p, d_mix, tokens, d_attn, d_num, fa, m1, m2, m3, m4, dt, c, vecs, w_qkv, tile
):
    rows, width = tokens.shape
    groups = width // GW
    steps = rows // tile
    const = lambda *shape: pl.BlockSpec(shape, lambda i: (0,) * len(shape))
    now = lambda i: jnp.minimum(i, steps - 1)
    old = lambda i: jnp.maximum(i - 1, 0)
    per = tile // HALO
    last = rows // HALO - 1

    def halo(col):
        return [
            pl.BlockSpec((HALO, width), lambda i: (jnp.maximum(now(i) * per - 1, 0), col)),
            pl.BlockSpec((tile, width), lambda i: (now(i), col)),
            pl.BlockSpec((HALO, width), lambda i: (jnp.minimum((now(i) + 1) * per, last), col)),
        ]

    block = pl.BlockSpec((tile, width), lambda i: (now(i), 0))
    late = pl.BlockSpec((tile, width), lambda i: (old(i), 0))
    head = width // HEADS
    sds = jax.ShapeDtypeStruct
    return pl.pallas_call(
        back_kernel,
        grid=(steps + 1,),
        in_specs=[
            pl.BlockSpec(memory_space=pltpu.SMEM),
            block,
            *halo(1),
            *halo(2),
            pl.BlockSpec((tile // QB, KW, width), lambda i: (now(i), 0, 0)),
            block,
            pl.BlockSpec((tile, 3 * width), lambda i: (old(i), 0)),
            late,
            late,
            late,
            late,
            late,
            const(groups, 2 * GW, GW),
            const(groups, GW, GW),
            const(groups, GW, GW),
            const(groups, GW, GW),
            const(groups, 8, GW),
            const(groups, 8, GW),
            const(8, width),
            const(width, 3 * width),
            const(GW, GW),
        ],
        out_specs=[late, const(width, 3 * width), const(2, 8, width)],
        out_shape=[
            sds((rows, width), bf16),
            sds((width, 3 * width), bf16),
            sds((2, 8, width), f32),
        ],
        scratch_shapes=[
            pltpu.VMEM((tile + 2 * HALO, width), bf16),
            pltpu.VMEM((tile + 2 * HALO, width), bf16),
            pltpu.VMEM((2, tile, width), f32),
            pltpu.VMEM((rows + 2 * HALO, width), f32),
            pltpu.VMEM((rows + 2 * HALO, width), f32),
            pltpu.VMEM((width, 3 * width), f32),
        ],
        compiler_params=pltpu.CompilerParams(vmem_limit_bytes=VMEM_LIMIT),
        cost_estimate=pl.CostEstimate(
            flops=2 * rows * width * 14 * width, bytes_accessed=rows * width * 24, transcendentals=0
        ),
        name="fourth_pass",
    )(
        length,
        qkv,
        qkv,
        qkv,
        qkv,
        qkv,
        qkv,
        qkv,
        p,
        d_mix,
        qkv,
        tokens,
        d_attn,
        d_num,
        fa,
        d_mix,
        m1,
        m2,
        m3,
        m4,
        dt,
        c,
        vecs,
        w_qkv,
        jnp.asarray(head_table(head), bf16),
    )


TILES = dict(one=512, two=512, three=512, chunk=512, four=512)


def layer(tokens, cot, w_qkv, w_out, w_in, w_back, vecs, b_in, lengths, T=TILES):
    qkv, m1, m2, c = first_pass(lengths, tokens, vecs, w_qkv, T["one"])
    near, fa, fb, rn, p = second_pass(lengths, qkv, m1, m2, c, T["two"])
    (out, d_attn, d_mix, d_num, g_in, g_back, g_out, g_vec, g_bias, m3, m4, dt) = third_pass(
        lengths, tokens, cot, near, fa, fb, rn, qkv, c, vecs, b_in, w_out, w_in, w_back, T["three"], T["chunk"]
    )
    d_tok, g_qkv, g_vec1 = fourth_pass(
        lengths, qkv, p, d_mix, tokens, d_attn, d_num, fa, m1, m2, m3, m4, dt, c, vecs, w_qkv, T["four"]
    )
    grad_vec = jnp.concatenate([jnp.sum(g_vec1, axis=1), jnp.sum(g_vec, axis=1)[2:]], axis=0)
    return out, d_tok, g_qkv, g_out, g_in, g_back, grad_vec, jnp.sum(g_bias, axis=0)


def collect(w_qkv, w_out, w_in, w_back, vec_params, b_in):
    section_one = (
        lax.all_gather(w_qkv, "fsdp", axis=0, tiled=True),
        lax.all_gather(w_out, "fsdp", axis=0, tiled=True),
        lax.all_gather(w_in, "fsdp", axis=0, tiled=True),
        lax.all_gather(w_back, "fsdp", axis=0, tiled=True),
        lax.all_gather(vec_params, "fsdp", axis=1, tiled=True),
        lax.all_gather(b_in, "fsdp", axis=0, tiled=True),
    )
    return (
        lax.all_gather(section_one[0], "dp", axis=1, tiled=True),
        lax.all_gather(section_one[1], "dp", axis=1, tiled=True),
        lax.all_gather(section_one[2], "dp", axis=1, tiled=True),
        lax.all_gather(section_one[3], "dp", axis=1, tiled=True),
        lax.all_gather(section_one[4], "dp", axis=0, tiled=True),
        lax.all_gather(section_one[5], "dp", axis=0, tiled=True),
    )


def spread(grad_qkv, grad_out, grad_in, grad_back, grad_vec, grad_bias_in):
    section_one = (
        lax.psum_scatter(
            grad_qkv.astype(jnp.bfloat16), "dp", scatter_dimension=1, tiled=True
        ).astype(jnp.float32),
        lax.psum_scatter(
            grad_out.astype(jnp.bfloat16), "dp", scatter_dimension=1, tiled=True
        ).astype(jnp.float32),
        lax.psum_scatter(
            grad_in.astype(jnp.bfloat16), "dp", scatter_dimension=1, tiled=True
        ).astype(jnp.float32),
        lax.psum_scatter(
            grad_back.astype(jnp.bfloat16), "dp", scatter_dimension=0, tiled=True
        ).astype(jnp.float32),
        lax.psum_scatter(
            grad_vec.astype(jnp.bfloat16), "dp", scatter_dimension=0, tiled=True
        ).astype(jnp.float32),
        lax.psum_scatter(
            grad_bias_in.astype(jnp.bfloat16), "dp", scatter_dimension=0, tiled=True
        ).astype(jnp.float32),
    )
    return (
        lax.psum_scatter(section_one[0], "fsdp", scatter_dimension=0, tiled=True),
        lax.psum_scatter(section_one[1], "fsdp", scatter_dimension=0, tiled=True),
        lax.psum_scatter(section_one[2], "fsdp", scatter_dimension=0, tiled=True),
        lax.psum_scatter(section_one[3], "fsdp", scatter_dimension=1, tiled=True).T,
        lax.psum_scatter(section_one[4], "fsdp", scatter_dimension=1, tiled=True),
        lax.psum_scatter(section_one[5], "fsdp", scatter_dimension=0, tiled=True),
    )


def shards(
    tokens, cotangent, w_qkv, w_out, w_in, w_back, vec_params, b_in, item_lengths, bucket_counts
):
    qkv_w, out_w, in_w, back_w, vecs, in_bias = collect(
        w_qkv, w_out, w_in, w_back, vec_params, b_in
    )
    out, d_tok, g_qkv, g_out, g_in, g_back, g_vec, g_bias = layer(
        tokens,
        cotangent,
        qkv_w,
        out_w,
        in_w,
        back_w,
        vecs.astype(f32),
        in_bias.astype(f32)[None],
        item_lengths,
    )
    return (out, d_tok) + spread(g_qkv, g_out, g_in, g_back, g_vec, g_bias)


def solution(mesh):
    in_specs = (
        P(("dp", "fsdp"), None),
        P(("dp", "fsdp"), None),
        P("fsdp", "dp"),
        P("fsdp", "dp"),
        P("fsdp", "dp"),
        P("fsdp", "dp"),
        P("dp", "fsdp"),
        P(("dp", "fsdp")),
        P(("dp", "fsdp"), None),
        P(("dp", "fsdp"), None),
    )
    out_specs = (
        P(("dp", "fsdp"), None),
        P(("dp", "fsdp"), None),
        P("fsdp", "dp"),
        P("fsdp", "dp"),
        P("fsdp", "dp"),
        P("fsdp", "dp"),
        P("dp", "fsdp"),
        P(("dp", "fsdp")),
    )
    return jax.shard_map(shards, mesh=mesh, in_specs=in_specs, out_specs=out_specs, check_vma=False)
```

time: 1980 us -> 800 us (0.40)
  matrix products: 674 us -> 0 us
  local copies, waits for them, and re-layouts: 543 us -> 14.9 us
  other arithmetic: 234 us -> 6.76 us
  Pallas kernels: 0 us -> 199 us
  waiting for transfers between devices: 265 us -> 340 us
    dot_general x72 -> x0, matrix products: 579 us -> none  [the longest x4 83.8 us: cols_product(): lax.dot_general(left_side, right_side, (((1,), (1,)), ((), ())), preferre...]
    reshape x23 -> x0, local copies, waits for them, and re-layouts: 242 us -> none  [the longest x4 52.5 us: far_field(): (numer / denom[..., None]).reshape(row_count, model_width)]
    pallas_call x0 -> x4, Pallas kernels: none -> 199 us  [the longest x1 94.9 us: third_pass(): pl.pallas_call(functools.partial(ffn_kernel, chunk), grid=(rows // tile,)...]
    convert_element_type x14 -> x0, other arithmetic: 116 us -> none  [the longest x8 88.6 us: near_grad(): (probs * (d_probs - jnp.sum(probs * d_probs, axis=-1, keepdims=True))).as...]
    sub x16 -> x0, matrix products: 94.9 us -> none  [band_probs(): exp_scores = jnp.exp(scores - jnp.max(scores, axis=-1, keepdims=True))]
    dynamic_slice x104 -> x0, local copies, waits for them, and re-layouts: 91.7 us -> none  [the longest x16 27.7 us: block_inputs(): lax.dynamic_slice_in_dim(key_pad, first_row, BLOCK + 2 * BAND, 0)]
    dynamic_update_slice x56 -> x0, local copies, waits for them, and re-layouts: 52 us -> none  [the longest x24 29.7 us: shards(): dq_near, dk_extended, dv_extended = lax.map(near_grad, block_ids)]
    unnamed x205 -> x22, local copies, waits for them, and re-layouts: 63.6 us -> 14.3 us
  transfers between devices with their start and end apart: 12 -> 12, of which waited for: 5 -> 7; matrix products, arithmetic and copies ran while one was open for 32% -> 3% of each run, Pallas kernels for 0% -> 13%
where the time goes in v1:
time: 800 us; the launch traced here: 799 us
  waiting for transfers between devices  340 us (42%)
  blocking collectives  221 us (28%)
  Pallas kernels  199 us (25%)
  between operations  17 us (2%)
  local copies, waits for them, and re-layouts  14.9 us (2%)
    pallas_call x1, Pallas kernels, third_pass(): pl.pallas_call(functools.partial(ffn_kernel, chunk), grid=(rows // tile,)...  94.9 us
    reduce_scatter x1, waiting for transfers between devices, spread(): lax.psum_scatter(section_one[2], 'fsdp', scatter_dimension=0, tiled=True)  66.1 us
    reduce_scatter x1, waiting for transfers between devices, spread(): lax.psum_scatter(section_one[0], 'fsdp', scatter_dimension=0, tiled=True)  65.8 us
    reduce_scatter x1, waiting for transfers between devices, spread(): lax.psum_scatter(section_one[3], 'fsdp', scatter_dimension=1, tiled=True)  65 us
    reduce_scatter x1, waiting for transfers between devices, spread(): lax.psum_scatter(section_one[1], 'fsdp', scatter_dimension=0, tiled=True)  62.7 us
    pallas_call x1, Pallas kernels, fourth_pass(): pl.pallas_call(back_kernel, grid=(steps + 1,), in_specs=[pl.BlockSpec(mem...  61 us
    unnamed x3, blocking collectives  49.2 us
    unnamed x15, waiting for transfers between devices  48.4 us
  transfers between devices with their start and end apart: 12, of which 7 were waited for; matrix products, arithmetic and copies ran while one was open for 3% of the time, Pallas kernels for 13%

profile of v1, /device:TPU:0, one launch (start us, length us, event | category | flops | bytes accessed | tf_op | source)
XLA Modules:
  0.0 798.9 jit_solution(2229259654646886540)
XLA Ops:
  7.2 35.2 %all_gather.38 = bf16[512,384]{1,0:T(8,128)(2,1)} all-gather(bf16[64,384]{1,0:T(8,128)(2,1)} %param.15), channel_id=1, replica_groups=mesh['dp'=4,'fsdp'=8] {'fsdp'}, dimensions={0}, use_global_device_ids=true | all-gather | bytes 442368 | tf_op jit(solution)/shard_map/all_gather | solution.py:737
  42.4 33.7 %all_gather.46 = bf16[2048,128]{1,0:T(8,128)(2,1)} all-gather(bf16[256,128]{1,0:T(8,128)(2,1)} %param.18), channel_id=1, replica_groups=mesh['dp'=4,'fsdp'=8] {'fsdp'}, dimensions={0}, use_global_device_ids=true | all-gather | bytes 589824 | tf_op jit(solution)/shard_map/all_gather | solution.py:740
  76.2 33.6 %all_gather.44 = bf16[512,512]{1,0:T(8,128)(2,1)} all-gather(bf16[64,512]{1,0:T(8,128)(2,1)} %param.17), channel_id=1, replica_groups=mesh['dp'=4,'fsdp'=8] {'fsdp'}, dimensions={0}, use_global_device_ids=true | all-gather | bytes 589824 | tf_op jit(solution)/shard_map/all_gather | solution.py:739
  109.9 20.7 %all-gather = bf16[8,64,2]{1,2,0:T(2,128)(2,1)S(1)} all-gather(bf16[1,64,2]{1,2,0:T(2,128)(2,1)} %bitcast.29), channel_id=1, replica_groups=mesh['dp'=4,'fsdp'=8] {'fsdp'}, dimensions={0}, use_global_device_ids=true | all-gather | bytes 2304 | tf_op jit(solution)/shard_map/all_gather | solution.py:741
  130.7 5.1 all-gather.1
  139.3 17.1 %all-reduce = bf16[512]{0:T(512)(128)(2,1)S(1)} all-reduce(bf16[512]{0:T(512)(128)(2,1)S(1)} %dynamic-update-slice), channel_id=1, replica_groups=mesh['dp'=4,'fsdp'=8] {'fsdp'}, use_global_device_ids=true, to_apply=%add | all-reduce | flops 512 | bytes 2048
  156.5 5.2 all-gather.2
  162.2 30.7 %all_gather.42 = bf16[512,128]{1,0:T(8,128)(2,1)S(1)} all-gather(bf16[64,128]{1,0:T(8,128)(2,1)} %param.16), channel_id=1, replica_groups=mesh['dp'=4,'fsdp'=8] {'fsdp'}, dimensions={0}, use_global_device_ids=true | all-gather | bytes 147456 | tf_op jit(solution)/shard_map/all_gather | solution.py:738
  192.9 7.6 all_gather.43.wout_ref
  200.6 20.2 %first_pass.1 = (bf16[4096,1536]{1,0:T(8,128)(2,1)}, bf16[2,512,256]{2,1,0:T(8,128)(2,1)}, bf16[2,256,256]{2,1,0:T(8,128)(2,1)}, f32[2,8,256]{2,1,0:T(8,128)}) custom-call(s32[1,4]{1,0:T(1,128)} %len_ref.7, bf16[4096,512]{1,0:T(8,128)(2,1)} %tok_ref.5, f32[8,512]{1,0:T(8,128)} %reshape.26.vec_ref, bf16[512,1536]{1,0:T(8,128)(2,1)} %all-gather.7.cloned.1.call-done.w_ref), custom_call_target="tpu_custom_call" | custom-call | flops 8589934592 | bytes 16777216 | tf_op jit(solution)/shard_map/first_pass/pallas_call | solution.py:133
  220.8 22.8 %second_pass.1 = (bf16[4096,512]{1,0:T(8,128)(2,1)}, bf16[4096,512]{1,0:T(8,128)(2,1)}, bf16[4096,512]{1,0:T(8,128)(2,1)}, bf16[4096,512]{1,0:T(8,128)(2,1)}, bf16[64,128,512]{2,1,0:T(8,128)(2,1)}) custom-call(s32[1,4]{1,0:T(1,128)} %len_ref.7, bf16[4096,1536]{1,0:T(8,128)(2,1)} %get-tuple-element.32.q_ref.k_lo.k_ref.k_hi.v_lo.v_ref.v_hi.qkv_ref, ...), custom_call_target="tpu_custom_call" | custom-call | flops 8589934592 | bytes 37748736 | tf_op jit(solution)/shard_map/second_pass/pallas_call | solution.py:253
  243.6 94.9 %third_pass.1 = (bf16[4096,512]{1,0:T(8,128)(2,1)}, bf16[4096,512]{1,0:T(8,128)(2,1)}, bf16[4096,512]{1,0:T(8,128)(2,1)}, bf16[4096,512]{1,0:T(8,128)(2,1)}, bf1...) custom-call(s32[1,4]{1,0:T(1,128)} %len_ref.7, ...), custom_call_target="tpu_custom_call" | custom-call | flops 60129542144 | bytes 46137344 | tf_op jit(solution)/shard_map/third_pass/pallas_call | solution.py:434
  340.7 61.0 %fourth_pass.1 = (bf16[4096,512]{1,0:T(8,128)(2,1)}, bf16[512,1536]{1,0:T(8,128)(2,1)}, f32[2,8,512]{2,1,0:T(8,128)}) custom-call(s32[1,4]{1,0:T(1,128)} %len_ref.7, bf16[4096,1536]{1,0:T(8,128)(2,1)} %get-tuple-element.32.q_ref.k_lo.k_ref.k_hi.v_lo.v_ref.v_hi.qkv_ref, bf16[4096,1536]{1,0:T(8,128)(2,1)} %get-tuple-element.32.q_ref.k_lo.k_ref.k_hi.v_lo.v_ref.v_hi.qkv_ref, ...), custom_call_target="tpu_custom_call" | custom-call | flops 30064771072 | bytes 50331648 | tf_op jit(solution)/shard_map/fourth_pass/pallas_call | solution.py:645
  401.7 2.7 copy.25
  406.6 10.7 %all-reduce.4 = (bf16[8,512]{1,0:T(8,128)(2,1)S(1)}, bf16[2048]{0:T(1024)(128)(2,1)S(1)}) all-reduce(bf16[8,512]{1,0:T(8,128)(2,1)S(1)} %pad_maximum_fusion, bf16[2048]{0:T(1024)(128)(2,1)S(1)} %reduce_sum.29), channel_id=10, replica_groups=mesh['dp'=4,'fsdp'=8] {'dp'}, use_global_device_ids=true, to_apply=%region_10.0.clone | all-reduce | flops 6144 | bytes 24576
  422.4 8.4 %reduce-scatter.28.cloned.1.call-done = bf16[384,512]{1,0:T(8,128)(2,1)} async-done(((bf16[1536,512]{1,0:T(8,128)(2,1)}), bf16[384,512]{1,0:T(8,128)(2,1)}) %reduce-scatter.28.cloned.1.call-update) | async-done | bytes 393232
  433.0 31.9 %reduce-scatter.20.cloned.1.call-done = bf16[512,512]{1,0:T(8,128)(2,1)} async-done(((bf16[512,2048]{1,0:T(8,128)(2,1)}), bf16[512,512]{1,0:T(8,128)(2,1)}) %reduce-scatter.20.cloned.1.call-update) | async-done | bytes 524304 | tf_op jit(solution)/shard_map/reduce_scatter | solution.py:762
  464.9 2.2 convert_element_type.29
  468.5 21.3 %all-reduce.3 = f32[512]{0:T(512)S(1)} all-reduce(f32[512]{0:T(512)S(1)} %dynamic-slice_convert_fusion.1), channel_id=13, replica_groups=mesh['dp'=4,'fsdp'=8] {'fsdp'}, use_global_device_ids=true, to_apply=%region_14.0.clone | all-reduce | flops 512 | bytes 4096
  490.4 39.0 %reduce-scatter.32.cloned.1.call-done = f32[64,2]{1,0:T(8,128)} async-done(((f32[512,2]{1,0:T(8,128)}), f32[64,2]{1,0:T(8,128)}) %reduce-scatter.32.cloned.1.call-update) | async-done | bytes 528
  530.8 65.0 %reduce-scatter.26.cloned.1.call-done = f32[128,256]{1,0:T(8,128)} async-done(((f32[128,2048]{1,0:T(8,128)}), f32[128,256]{1,0:T(8,128)}) %reduce-scatter.26.cloned.1.call-update) | async-done | bytes 131088 | tf_op jit(solution)/shard_map/reduce_scatter | solution.py:779
  597.5 62.7 %reduce-scatter.18.cloned.1.call-done = f32[64,128]{1,0:T(8,128)} async-done(((f32[512,128]{1,0:T(8,128)}), f32[64,128]{1,0:T(8,128)}) %reduce-scatter.18.cloned.1.call-update) | async-done | bytes 32784 | tf_op jit(solution)/shard_map/reduce_scatter | solution.py:777
  660.1 65.8 %reduce-scatter.16.cloned.1.call-done = f32[64,384]{1,0:T(8,128)} async-done(((f32[512,384]{1,0:T(8,128)}), f32[64,384]{1,0:T(8,128)}) %reduce-scatter.16.cloned.1.call-update) | async-done | bytes 98320 | tf_op jit(solution)/shard_map/reduce_scatter | solution.py:776
  726.0 66.1 %reduce-scatter.22.cloned.1.call-done = f32[64,512]{1,0:T(8,128)} async-done(((f32[512,512]{1,0:T(8,128)}), f32[64,512]{1,0:T(8,128)}) %reduce-scatter.22.cloned.1.call-update) | async-done | bytes 131088 | tf_op jit(solution)/shard_map/reduce_scatter | solution.py:778
  (63 shorter events, 18.3 us)
Async XLA Ops:
  7.2 193.4 %all-gather.7.cloned.1.call-start = ((), (), s32[]{:S(2)}) async-start(), calls=%async_computation.9 | async-start | bytes 1966080 | tf_op jit(solution)/shard_map/all_gather | solution.py:745
  42.4 201.2 %all-gather.11.cloned.1.call-start = ((), (), s32[]{:S(2)}) async-start(), calls=%async_computation.11 | async-start | bytes 2621440 | tf_op jit(solution)/shard_map/all_gather | solution.py:748
  76.1 167.5 %all-gather.9.cloned.1.call-start = ((), (), s32[]{:S(2)}) async-start(), calls=%async_computation.10 | async-start | bytes 2621440 | tf_op jit(solution)/shard_map/all_gather | solution.py:747
  109.8 308.5 %reduce-scatter.24.cloned.1.call-start = ((), (), s32[]{:S(2)}) async-start(), calls=%async_computation.16 | async-start | bytes 2621440 | tf_op jit(solution)/shard_map/reduce_scatter | solution.py:765
  338.5 82.0 %reduce-scatter.30.cloned.1.call-start = ((), (), s32[]{:S(2)}) async-start(), calls=%async_computation.19 | async-start | bytes 655360
  340.6 90.2 %reduce-scatter.28.cloned.1.call-start = ((), (), s32[]{:S(2)}) async-start(), calls=%async_computation.18 | async-start | bytes 1966080
  401.7 3.5 copy-start.3
  401.7 4.8 copy-start.2
  401.7 4.8 copy-start
  401.7 4.8 copy-start.1
  404.4 60.5 %reduce-scatter.20.cloned.1.call-start = ((), (), s32[]{:S(2)}) async-start(), calls=%async_computation.14 | async-start | bytes 2621440 | tf_op jit(solution)/shard_map/reduce_scatter | solution.py:762
  405.2 124.3 %reduce-scatter.32.cloned.1.call-start = ((), (), s32[]{:S(2)}) async-start(), calls=%async_computation.20 | async-start | bytes 294912
  418.2 177.6 %reduce-scatter.26.cloned.1.call-start = ((), (), s32[]{:S(2)}) async-start(), calls=%async_computation.17 | async-start | bytes 1179648 | tf_op jit(solution)/shard_map/reduce_scatter | solution.py:779
  420.5 239.7 %reduce-scatter.18.cloned.1.call-start = ((), (), s32[]{:S(2)}) async-start(), calls=%async_computation.13 | async-start | bytes 294912 | tf_op jit(solution)/shard_map/reduce_scatter | solution.py:777
  422.3 303.7 %reduce-scatter.16.cloned.1.call-start = ((), (), s32[]{:S(2)}) async-start(), calls=%async_computation.12 | async-start | bytes 884736 | tf_op jit(solution)/shard_map/reduce_scatter | solution.py:776
  433.0 359.1 %reduce-scatter.22.cloned.1.call-start = ((), (), s32[]{:S(2)}) async-start(), calls=%async_computation.15 | async-start | bytes 1179648 | tf_op jit(solution)/shard_map/reduce_scatter | solution.py:778
Sparse Core Ops, SparseCore 0:
  42.5 20.5 all-gather.6
  76.3 23.9 all-gather.10
  109.9 23.6 all-gather.8
  338.6 29.4 reduce-scatter.23
  370.6 21.6 reduce-scatter.29
  404.5 26.2 reduce-scatter.27
  433.5 31.3 reduce-scatter.19
  468.3 61.1 reduce-scatter.31
  532.9 62.9 reduce-scatter.25
  599.9 60.1 reduce-scatter.17
  664.4 61.5 reduce-scatter.15
  729.8 62.2 reduce-scatter.21

commit v2 on v1

--- a/solution.py
+++ b/solution.py
@@ -41,6 +41,10 @@
     )
 
 
+def first_part(cols):
+    return 128 * ((cols // 128 + 1) // 2) if cols >= 256 else cols // 2
+
+
 def lift(t):
     return jnp.where(t > 0, t + 1.0, jnp.exp(jnp.minimum(t, 0.0)))
 
@@ -77,6 +81,18 @@
     for h in range(1, GW // QB):
         out = jnp.where(lane == h, x[h * QB : (h + 1) * QB], out)
     return out
+
+
+def cut_blocks(ref, acc, lo=0, step=None, swap=False):
+    n_dp, n_fsdp, r, c = ref.shape
+    step = c if step is None else step
+    for d in range(n_dp):
+        for f in range(n_fsdp):
+            if swap:
+                block = acc[d * r : (d + 1) * r, f * c : (f + 1) * c]
+            else:
+                block = acc[f * r : (f + 1) * r, d * step + lo : d * step + lo + c]
+            ref[d, f] = block.astype(ref.dtype)
 
 
 def qkv_kernel(len_ref, tok_ref, vec_ref, w_ref, qkv_ref, m1_ref, m2_ref, c_ref, st_ref, t_ref):
@@ -418,16 +434,17 @@
             m3_ref[g] = (a_st[g][:, :GW] * mask).astype(bf16)
             m4_ref[g] = (a_bent[g] * mask * inv_len).astype(bf16)
             dt_ref[g] = -nt_exact(ones, a_st[g][:, GW:] * mask)
-        gin_ref[...] = a_in[...].astype(gin_ref.dtype)
-        gback_ref[...] = a_back[...].astype(gback_ref.dtype)
-        gout_ref[...] = a_out[...].astype(gout_ref.dtype)
+        cut_blocks(gin_ref, a_in)
+        cut_blocks(gback_ref, a_back, swap=True)
+        cut_blocks(gout_ref, a_out)
         gvec_ref[6] += gvec_ref[0] * c_row
 
 
-def third_pass(length, tokens, cot, near, fa, fb, rn, qkv, c, vecs, b_in, w_out, w_in, w_back, tile, chunk):
+def third_pass(ways, length, tokens, cot, near, fa, fb, rn, qkv, c, vecs, b_in, w_out, w_in, w_back, tile, chunk):
     rows, width = tokens.shape
     hidden = w_in.shape[1]
     groups = width // GW
+    n_dp, n_fsdp = ways
     const = lambda *shape: pl.BlockSpec(shape, lambda i: (0,) * len(shape))
     block = pl.BlockSpec((tile, width), lambda i: (i, 0))
     sds = jax.ShapeDtypeStruct
@@ -446,9 +463,9 @@
         ],
         out_specs=[block] * 4
         + [
-            const(width, hidden),
-            const(width, hidden),
-            const(width, width),
+            const(n_dp, n_fsdp, width // n_fsdp, hidden // n_dp),
+            const(n_dp, n_fsdp, width // n_dp, hidden // n_fsdp),
+            const(n_dp, n_fsdp, width // n_fsdp, width // n_dp),
             const(8, 8, width),
             const(8, hidden),
             const(groups, GW, GW),
@@ -457,9 +474,9 @@
         ],
         out_shape=[sds((rows, width), bf16)] * 4
         + [
-            sds((width, hidden), bf16),
-            sds((width, hidden), bf16),
-            sds((width, width), bf16),
+            sds((n_dp, n_fsdp, width // n_fsdp, hidden // n_dp), bf16),
+            sds((n_dp, n_fsdp, width // n_dp, hidden // n_fsdp), bf16),
+            sds((n_dp, n_fsdp, width // n_fsdp, width // n_dp), bf16),
             sds((8, 8, width), f32),
             sds((8, hidden), f32),
             sds((groups, GW, GW), bf16),
@@ -510,7 +527,8 @@
     w_ref,
     hm_ref,
     dtok_ref,
-    gqkv_ref,
+    ga_ref,
+    gb_ref,
     gvec_ref,
     kk,
     vv,
@@ -616,15 +634,19 @@
 
     @pl.when(step == steps)
     def _():
-        gqkv_ref[...] = a_qkv[...].astype(gqkv_ref.dtype)
+        step_cols = ga_ref.shape[3] + gb_ref.shape[3]
+        cut_blocks(ga_ref, a_qkv, 0, step_cols)
+        cut_blocks(gb_ref, a_qkv, ga_ref.shape[3], step_cols)
 
 
 def fourth_pass(
-    length, qkv, p, d_mix, tokens, d_attn, d_num, fa, m1, m2, m3, m4, dt, c, vecs, w_qkv, tile
+    ways, length, qkv, p, d_mix, tokens, d_attn, d_num, fa, m1, m2, m3, m4, dt, c, vecs, w_qkv, tile
 ):
     rows, width = tokens.shape
     groups = width // GW
     steps = rows // tile
+    n_dp, n_fsdp = ways
+    part = first_part(3 * width // n_dp)
     const = lambda *shape: pl.BlockSpec(shape, lambda i: (0,) * len(shape))
     now = lambda i: jnp.minimum(i, steps - 1)
     old = lambda i: jnp.maximum(i - 1, 0)
@@ -668,10 +690,16 @@
             const(width, 3 * width),
             const(GW, GW),
         ],
-        out_specs=[late, const(width, 3 * width), const(2, 8, width)],
+        out_specs=[
+            late,
+            const(n_dp, n_fsdp, width // n_fsdp, part),
+            const(n_dp, n_fsdp, width // n_fsdp, 3 * width // n_dp - part),
+            const(2, 8, width),
+        ],
         out_shape=[
             sds((rows, width), bf16),
-            sds((width, 3 * width), bf16),
+            sds((n_dp, n_fsdp, width // n_fsdp, part), bf16),
+            sds((n_dp, n_fsdp, width // n_fsdp, 3 * width // n_dp - part), bf16),
             sds((2, 8, width), f32),
         ],
         scratch_shapes=[
@@ -719,87 +747,326 @@
 TILES = dict(one=512, two=512, three=512, chunk=512, four=512)
 
 
-def layer(tokens, cot, w_qkv, w_out, w_in, w_back, vecs, b_in, lengths, T=TILES):
+def layer(ways, tokens, cot, w_qkv, w_out, w_in, w_back, vecs, b_in, lengths, T=TILES):
     qkv, m1, m2, c = first_pass(lengths, tokens, vecs, w_qkv, T["one"])
     near, fa, fb, rn, p = second_pass(lengths, qkv, m1, m2, c, T["two"])
     (out, d_attn, d_mix, d_num, g_in, g_back, g_out, g_vec, g_bias, m3, m4, dt) = third_pass(
-        lengths, tokens, cot, near, fa, fb, rn, qkv, c, vecs, b_in, w_out, w_in, w_back, T["three"], T["chunk"]
+        ways, lengths, tokens, cot, near, fa, fb, rn, qkv, c, vecs, b_in, w_out, w_in, w_back, T["three"], T["chunk"]
     )
-    d_tok, g_qkv, g_vec1 = fourth_pass(
-        lengths, qkv, p, d_mix, tokens, d_attn, d_num, fa, m1, m2, m3, m4, dt, c, vecs, w_qkv, T["four"]
+    d_tok, g_a, g_b, g_vec1 = fourth_pass(
+        ways, lengths, qkv, p, d_mix, tokens, d_attn, d_num, fa, m1, m2, m3, m4, dt, c, vecs, w_qkv, T["four"]
     )
     grad_vec = jnp.concatenate([jnp.sum(g_vec1, axis=1), jnp.sum(g_vec, axis=1)[2:]], axis=0)
-    return out, d_tok, g_qkv, g_out, g_in, g_back, grad_vec, jnp.sum(g_bias, axis=0)
-
-
-def collect(w_qkv, w_out, w_in, w_back, vec_params, b_in):
-    section_one = (
-        lax.all_gather(w_qkv, "fsdp", axis=0, tiled=True),
-        lax.all_gather(w_out, "fsdp", axis=0, tiled=True),
-        lax.all_gather(w_in, "fsdp", axis=0, tiled=True),
-        lax.all_gather(w_back, "fsdp", axis=0, tiled=True),
-        lax.all_gather(vec_params, "fsdp", axis=1, tiled=True),
-        lax.all_gather(b_in, "fsdp", axis=0, tiled=True),
+    return out, d_tok, g_a, g_b, g_out, g_in, g_back, grad_vec, jnp.sum(g_bias, axis=0)
+
+
+MESH = pl.DeviceIdType.MESH
+
+
+class Place:
+    def __init__(self, n_dp, n_fsdp):
+        self.m = n_fsdp // 2
+        self.nh = n_dp // 2
+        d = lax.axis_index("dp")
+        f = lax.axis_index("fsdp")
+        self.dh, self.dl = d // 2, lax.rem(d, 2)
+        self.fh, self.fl = f // 2, lax.rem(f, 2)
+
+    def dev(self, dh=None, dl=None, fh=None, fl=None):
+        dh = self.dh if dh is None else dh
+        dl = self.dl if dl is None else dl
+        fh = self.fh if fh is None else fh
+        fl = self.fl if fl is None else fl
+        return {"dp": dh * 2 + dl, "fsdp": fh * 2 + fl}
+
+    def partners(self):
+        out = [self.dev(fh=lax.rem(self.fh + o, self.m)) for o in range(1, self.m)]
+        out += [self.dev(dh=lax.rem(self.dh + o, self.nh)) for o in range(1, self.nh)]
+        return out + [self.dev(fl=1 - self.fl), self.dev(dl=1 - self.dl)]
+
+
+def greet(place):
+    barrier = pltpu.get_barrier_semaphore()
+    who = place.partners()
+    for dev in who:
+        pl.semaphore_signal(barrier, inc=1, device_id=dev, device_id_type=MESH)
+    pl.semaphore_wait(barrier, len(who))
+
+
+def copy_to(src, dst, send, recv, dev):
+    return pltpu.make_async_remote_copy(
+        src_ref=src, dst_ref=dst, send_sem=send, recv_sem=recv, device_id=dev, device_id_type=MESH
     )
+
+
+class Gather:
+    def __init__(self, place, shard, got, sems, local, first, order):
+        self.p, self.shard, self.got, self.order = place, shard, got, order
+        self.send, self.recv, self.local, self.first = sems[0], sems[1], local, first
+
+    def own(self):
+        p = self.p
+        return pltpu.make_async_copy(self.shard, self.got.at[p.dh, p.dl, p.fh, p.fl], self.local)
+
+    def stage(self, k):
+        p, g = self.p, self.got
+        i = self.first
+        if k == 0:
+            out = []
+            for o in range(1, p.m):
+                out.append(
+                    copy_to(self.shard, g.at[p.dh, p.dl, p.fh, p.fl], self.send.at[i + o - 1],
+                            self.recv.at[i + o - 1], p.dev(fh=lax.rem(p.fh + o, p.m)))
+                )
+            return out
+        i += p.m - 1
+        x_first = self.order == "x"
+        if k == 3:
+            ref = g.at[:, p.dl]
+            return [copy_to(ref, ref, self.send.at[i + p.nh], self.recv.at[i + p.nh], p.dev(dl=1 - p.dl))]
+        if (k == 1) == x_first:
+            ref = g.at[p.dh, p.dl, :, p.fl] if k == 1 else g.at[:, p.dl, :, p.fl]
+            return [copy_to(ref, ref, self.send.at[i], self.recv.at[i], p.dev(fl=1 - p.fl))]
+        ref = g.at[p.dh, p.dl, :, p.fl] if k == 1 else g.at[p.dh, p.dl]
+        return [
+            copy_to(ref, ref, self.send.at[i + o], self.recv.at[i + o], p.dev(dh=lax.rem(p.dh + o, p.nh)))
+            for o in range(1, p.nh)
+        ]
+
+    @staticmethod
+    def count(n_dp, n_fsdp):
+        return n_fsdp // 2 - 1 + 1 + n_dp // 2 - 1 + 1
+
+
+def gather_kernel(n_dp, n_fsdp, orders, rounds, *refs):
+    n = len(orders)
+    shards, gots = refs[:n], refs[n : 2 * n]
+    send, recv, local = refs[2 * n :]
+    place = Place(n_dp, n_fsdp)
+    per = Gather.count(n_dp, n_fsdp)
+    pieces = [Gather(place, shards[j], gots[j], (send, recv), local.at[j], j * per, orders[j]) for j in range(n)]
+    owns = [p.own() for p in pieces]
+    for o in owns:
+        o.start()
+    greet(place)
+    flight = {}
+    for j, k in rounds:
+        if k == 1:
+            owns[j].wait()
+        if k > 0:
+            for c in flight[j, k - 1]:
+                c.wait()
+        if k < 4:
+            flight[j, k] = pieces[j].stage(k)
+            for c in flight[j, k]:
+                c.start()
+
+
+def gather_all(mesh_shape, arrays, orders, rounds, cid=0, vmem=False):
+    n_dp, n_fsdp = mesh_shape["dp"], mesh_shape["fsdp"]
+    n = len(arrays)
+    per = Gather.count(n_dp, n_fsdp)
+    sp = pl.BlockSpec(memory_space=pltpu.VMEM) if vmem else pl.BlockSpec(memory_space=pl.ANY)
+    return pl.pallas_call(
+        functools.partial(gather_kernel, n_dp, n_fsdp, orders, rounds),
+        in_specs=[sp] * n,
+        out_specs=[sp] * n,
+        out_shape=[jax.ShapeDtypeStruct((n_dp // 2, 2, n_fsdp // 2, 2) + a.shape, a.dtype) for a in arrays],
+        scratch_shapes=[
+            pltpu.SemaphoreType.DMA((n * per,)),
+            pltpu.SemaphoreType.DMA((n * per,)),
+            pltpu.SemaphoreType.DMA((n,)),
+        ],
+        compiler_params=pltpu.CompilerParams(collective_id=cid, has_side_effects=True, vmem_limit_bytes=VMEM_LIMIT),
+        name="gather_weights",
+    )(*arrays)
+
+
+class Scatter:
+    def __init__(self, place, src, out, bufs, send, recv, local, order):
+        self.p, self.src, self.out, self.order = place, src, out, order
+        self.acc, self.r0, self.r1, self.r2, self.r3 = bufs
+        self.send, self.recv, self.local = send, recv, local
+
+    @staticmethod
+    def count(n_dp, n_fsdp):
+        return 1 + 1 + (n_dp // 2 - 1) + (n_fsdp // 2 - 1)
+
+    @staticmethod
+    def scratch(n_dp, n_fsdp, r, c, order, dtype):
+        nh, m = n_dp // 2, n_fsdp // 2
+        if order == "x":
+            one, two = (nh, m, r, c), (nh - 1, m, r, c)
+        else:
+            one, two = (nh - 1, m, 2, r, c), (m, r, c)
+        shapes = [(nh, m, 2, r, c), (nh, m, 2, r, c), one, two, (m - 1, r, c)]
+        return [pltpu.VMEM(s, dtype) for s in shapes]
+
+    def own(self):
+        return pltpu.make_async_copy(self.src.at[:, self.p.dl], self.acc, self.local)
+
+    def stage(self, k):
+        p = self.p
+        if k == 0:
+            ref = self.src.at[:, 1 - p.dl]
+            return [copy_to(ref, self.r0, self.send.at[0], self.recv.at[0], p.dev(dl=1 - p.dl))]
+        if k == 3:
+            i = p.nh
+            out = []
+            for o in range(1, p.m):
+                fh = lax.rem(p.fh + o, p.m)
+                out.append(
+                    copy_to(self.acc.at[p.dh, fh, p.fl], self.r3.at[o - 1], self.send.at[i + o], self.recv.at[i + o],
+                            p.dev(fh=fh))
+                )
+            return out
+        if (k == 1) == (self.order == "x"):
+            ref = self.acc.at[:, :, 1 - p.fl] if k == 1 else self.acc.at[p.dh, :, 1 - p.fl]
+            dst = self.r1 if k == 1 else self.r2
+            return [copy_to(ref, dst, self.send.at[1], self.recv.at[1], p.dev(fl=1 - p.fl))]
+        out = []
+        for o in range(1, p.nh):
+            dh = lax.rem(p.dh + o, p.nh)
+            ref = self.acc.at[dh] if k == 1 else self.acc.at[dh, :, p.fl]
+            dst = self.r1.at[o - 1] if k == 1 else self.r2.at[o - 1]
+            out.append(copy_to(ref, dst, self.send.at[1 + o], self.recv.at[1 + o], p.dev(dh=dh)))
+        return out
+
+    def add(self, k):
+        p, acc = self.p, self.acc
+        nh, m = p.nh, p.m
+        dt = acc.dtype
+
+        def put(index, others):
+            total = acc[index].astype(f32)
+            for o in others:
+                total = total + o.astype(f32)
+            acc[index] = total.astype(dt)
+
+        if k == 3:
+            total = acc[p.dh, p.fh, p.fl].astype(f32)
+            for o in range(1, m):
+                total = total + self.r3[o - 1].astype(f32)
+            self.out[...] = total
+            return
+
+        @pl.loop(0, m)
+        def _(i):
+            if k == 0:
+                for a in range(nh):
+                    for b in range(2):
+                        put((a, i, b), [self.r0[a, i, b]])
+            elif k == 1 and self.order == "x":
+                for a in range(nh):
+                    put((a, i, p.fl), [self.r1[a, i]])
+            elif k == 1:
+                for b in range(2):
+                    put((p.dh, i, b), [self.r1[o - 1, i, b] for o in range(1, nh)])
+            elif self.order == "x":
+                put((p.dh, i, p.fl), [self.r2[o - 1, i] for o in range(1, nh)])
+            else:
+                put((p.dh, i, p.fl), [self.r2[i]])
+
+
+def scatter_kernel(n_dp, n_fsdp, orders, *refs):
+    n = len(orders)
+    srcs, outs = refs[:n], refs[n : 2 * n]
+    bufs = [refs[2 * n + 5 * j : 2 * n + 5 * (j + 1)] for j in range(n)]
+    sems = refs[7 * n :]
+    place = Place(n_dp, n_fsdp)
+    pieces = [
+        Scatter(place, srcs[j], outs[j], bufs[j], sems[2 * j], sems[2 * j + 1], sems[2 * n].at[j], orders[j])
+        for j in range(n)
+    ]
+    owns = [p.own() for p in pieces]
+    for o in owns:
+        o.start()
+    greet(place)
+    flight = {}
+    for j in range(n):
+        flight[j] = pieces[j].stage(0)
+        for c in flight[j]:
+            c.start()
+    for o in owns:
+        o.wait()
+    for k in range(4):
+        for j in range(n):
+            for c in flight[j]:
+                c.wait()
+            pieces[j].add(k)
+            if k < 3:
+                flight[j] = pieces[j].stage(k + 1)
+                for c in flight[j]:
+                    c.start()
+
+
+def scatter_all(mesh_shape, arrays, orders, cid):
+    n_dp, n_fsdp = mesh_shape["dp"], mesh_shape["fsdp"]
+    n = len(arrays)
+    per = Scatter.count(n_dp, n_fsdp)
+    scratch = []
+    for a, order in zip(arrays, orders):
+        scratch += Scatter.scratch(n_dp, n_fsdp, a.shape[-2], a.shape[-1], order, a.dtype)
+    scratch += [pltpu.SemaphoreType.DMA((per,))] * (2 * n) + [pltpu.SemaphoreType.DMA((n,))]
+    return pl.pallas_call(
+        functools.partial(scatter_kernel, n_dp, n_fsdp, orders),
+        in_specs=[pl.BlockSpec(memory_space=pl.ANY)] * n,
+        out_specs=[pl.BlockSpec(memory_space=pltpu.VMEM)] * n,
+        out_shape=[jax.ShapeDtypeStruct(a.shape[-2:], f32) for a in arrays],
+        scratch_shapes=scratch,
+        compiler_params=pltpu.CompilerParams(
+            collective_id=cid, has_side_effects=True, vmem_limit_bytes=VMEM_LIMIT
+        ),
+        name="scatter_grads",
+    )(*arrays)
+
+
+def shards(
+    tokens, cotangent, w_qkv, w_out, w_in, w_back, vec_params, b_in, item_lengths, bucket_counts, *, ways
+):
+    n_dp, n_fsdp = ways
+    shape = {"dp": n_dp, "fsdp": n_fsdp}
+    width = tokens.shape[1]
+    cols = width // n_fsdp
+    part = first_part(w_qkv.shape[1])
+    small = jnp.zeros((16, 128), bf16).at[:2, :cols].set(vec_params).at[2, :cols].set(b_in)
+    pieces = [w_qkv[:, :part], w_qkv[:, part:], w_in, w_back, w_out, small]
+    orders = ["x", "y", "x", "y", "y", "x"]
+    rounds = [(j, k) for k in range(5) for j in (0, 1, 5, 2, 3, 4)]
+    got = gather_all(shape, pieces, orders, rounds, cid=0)
+
+    def whole(g):
+        return g.reshape(n_dp, n_fsdp, *g.shape[-2:])
+
+    def lay(g):
+        g = whole(g)
+        return g.transpose(1, 2, 0, 3).reshape(n_fsdp * g.shape[2], n_dp * g.shape[3])
+
+    qkv_w = jnp.concatenate([whole(got[0]), whole(got[1])], axis=3)
+    qkv_w = lay(qkv_w)
+    small = whole(got[5])
+    vecs = small[:, :, :2, :cols].transpose(0, 2, 1, 3).reshape(2 * n_dp, width).astype(f32)
+    in_bias = small[:, :, 2, :cols].reshape(1, -1).astype(f32)
+    out, d_tok, g_a, g_b, g_out, g_in, g_back, g_vec, g_bias = layer(
+        ways, tokens, cotangent, qkv_w, lay(got[4]), lay(got[2]), lay(got[3]), vecs, in_bias, item_lengths
+    )
+    g_vec = g_vec.reshape(n_dp, 2, n_fsdp, cols).transpose(0, 2, 1, 3)
+    g_bias = g_bias.reshape(n_dp, n_fsdp, 1, cols)
+    g_small = jnp.zeros((n_dp, n_fsdp, 8, 128), f32)
+    g_small = g_small.at[:, :, :2, :cols].set(g_vec).at[:, :, 2:3, :cols].set(g_bias)
+    grads = [g_a, g_b, g_in, g_back, g_out, g_small]
+    grads = [g.reshape(n_dp // 2, 2, n_fsdp // 2, 2, *g.shape[2:]) for g in grads]
+    r_a, r_b, r_in, r_back, r_out, r_small = scatter_all(shape, grads, ["x", "y", "x", "y", "y", "x"], cid=1)
     return (
-        lax.all_gather(section_one[0], "dp", axis=1, tiled=True),
-        lax.all_gather(section_one[1], "dp", axis=1, tiled=True),
-        lax.all_gather(section_one[2], "dp", axis=1, tiled=True),
-        lax.all_gather(section_one[3], "dp", axis=1, tiled=True),
-        lax.all_gather(section_one[4], "dp", axis=0, tiled=True),
-        lax.all_gather(section_one[5], "dp", axis=0, tiled=True),
+        out,
+        d_tok,
+        jnp.concatenate([r_a, r_b], axis=1),
+        r_out,
+        r_in,
+        r_back.T,
+        r_small[:2, :cols],
+        r_small[2, :cols],
     )
-
-
-def spread(grad_qkv, grad_out, grad_in, grad_back, grad_vec, grad_bias_in):
-    section_one = (
-        lax.psum_scatter(
-            grad_qkv.astype(jnp.bfloat16), "dp", scatter_dimension=1, tiled=True
-        ).astype(jnp.float32),
-        lax.psum_scatter(
-            grad_out.astype(jnp.bfloat16), "dp", scatter_dimension=1, tiled=True
-        ).astype(jnp.float32),
-        lax.psum_scatter(
-            grad_in.astype(jnp.bfloat16), "dp", scatter_dimension=1, tiled=True
-        ).astype(jnp.float32),
-        lax.psum_scatter(
-            grad_back.astype(jnp.bfloat16), "dp", scatter_dimension=0, tiled=True
-        ).astype(jnp.float32),
-        lax.psum_scatter(
-            grad_vec.astype(jnp.bfloat16), "dp", scatter_dimension=0, tiled=True
-        ).astype(jnp.float32),
-        lax.psum_scatter(
-            grad_bias_in.astype(jnp.bfloat16), "dp", scatter_dimension=0, tiled=True
-        ).astype(jnp.float32),
-    )
-    return (
-        lax.psum_scatter(section_one[0], "fsdp", scatter_dimension=0, tiled=True),
-        lax.psum_scatter(section_one[1], "fsdp", scatter_dimension=0, tiled=True),
-        lax.psum_scatter(section_one[2], "fsdp", scatter_dimension=0, tiled=True),
-        lax.psum_scatter(section_one[3], "fsdp", scatter_dimension=1, tiled=True).T,
-        lax.psum_scatter(section_one[4], "fsdp", scatter_dimension=1, tiled=True),
-        lax.psum_scatter(section_one[5], "fsdp", scatter_dimension=0, tiled=True),
-    )
-
-
-def shards(
-    tokens, cotangent, w_qkv, w_out, w_in, w_back, vec_params, b_in, item_lengths, bucket_counts
-):
-    qkv_w, out_w, in_w, back_w, vecs, in_bias = collect(
-        w_qkv, w_out, w_in, w_back, vec_params, b_in
-    )
-    out, d_tok, g_qkv, g_out, g_in, g_back, g_vec, g_bias = layer(
-        tokens,
-        cotangent,
-        qkv_w,
-        out_w,
-        in_w,
-        back_w,
-        vecs.astype(f32),
-        in_bias.astype(f32)[None],
-        item_lengths,
-    )
-    return (out, d_tok) + spread(g_qkv, g_out, g_in, g_back, g_vec, g_bias)
 
 
 def solution(mesh):
@@ -825,4 +1092,6 @@
         P("dp", "fsdp"),
         P(("dp", "fsdp")),
     )
-    return jax.shard_map(shards, mesh=mesh, in_specs=in_specs, out_specs=out_specs, check_vma=False)
+    ways = (mesh.shape["dp"], mesh.shape["fsdp"])
+    body = functools.partial(shards, ways=ways)
+    return jax.shard_map(body, mesh=mesh, in_specs=in_specs, out_specs=out_specs, check_vma=False)

time: 800 us -> 334 us (0.42)
  waiting for transfers between devices: 340 us -> 0 us
  blocking collectives: 221 us -> 0 us
  Pallas kernels: 199 us -> 300 us
  between operations: 17 us -> 0.81 us
  local copies, waits for them, and re-layouts: 14.9 us -> 28.4 us
    reduce_scatter x6 -> x0, waiting for transfers between devices: 292 us -> none  [the longest x1 66.1 us: spread(): lax.psum_scatter(section_one[2], 'fsdp', scatter_dimension=0, tiled=True)]
    all_gather x8 -> x0, blocking collectives: 172 us -> none  [the longest x1 35.2 us: collect(): lax.all_gather(w_qkv, 'fsdp', axis=0, tiled=True)]
    pallas_call x0 -> x2, Pallas kernels: none -> 102 us  [the longest x1 52.7 us: gather_all(): pl.pallas_call(functools.partial(gather_kernel, n_dp, n_fsdp, orders, rou...]
    unnamed x3 -> x0, blocking collectives: 49.2 us -> none
    unnamed x15 -> x0, waiting for transfers between devices: 48.4 us -> none
  transfers between devices with their start and end apart: 12 -> 0, of which waited for: 7 -> 0; matrix products, arithmetic and copies ran while one was open for 3% -> 0% of each run, Pallas kernels for 13% -> 0%
where the time goes in v2:
time: 334 us; the launch traced here: 333 us
  Pallas kernels  300 us (90%)
  local copies, waits for them, and re-layouts  28.4 us (9%)
    pallas_call x1, Pallas kernels, third_pass(): pl.pallas_call(functools.partial(ffn_kernel, chunk), grid=(rows // tile,)...  94.5 us
    pallas_call x1, Pallas kernels, fourth_pass(): pl.pallas_call(back_kernel, grid=(steps + 1,), in_specs=[pl.BlockSpec(mem...  61 us
    pallas_call x1, Pallas kernels, gather_all(): pl.pallas_call(functools.partial(gather_kernel, n_dp, n_fsdp, orders, rou...  52.7 us
    pallas_call x1, Pallas kernels, scatter_all(): pl.pallas_call(functools.partial(scatter_kernel, n_dp, n_fsdp, orders), i...  48.9 us
    pallas_call x1, Pallas kernels, second_pass(): pl.pallas_call(mix_kernel, grid=(rows // tile,), in_specs=[pl.BlockSpec(m...  23 us
    pallas_call x1, Pallas kernels, first_pass(): pl.pallas_call(qkv_kernel, grid=(rows // tile,), in_specs=[pl.BlockSpec(m...  20.2 us
    unnamed x19, local copies, waits for them, and re-layouts  10.6 us
    reshape x5, local copies, waits for them, and re-layouts, whole(): return g.reshape(n_dp, n_fsdp, *g.shape[-2:])  7.16 us

profile of v2, /device:TPU:0, one launch (start us, length us, event | category | flops | bytes accessed | tf_op | source)
XLA Modules:
  0.0 332.8 jit_solution(15947143476160559927)
XLA Ops:
  2.1 1.3 slice.125.refs_1_
  3.4 1.4 slice.124.refs_0_
  4.8 52.7 %gather_weights.1 = (bf16[2,2,4,2,64,256]{5,4,3,2,1,0:T(8,128)(2,1)}, bf16[2,2,4,2,64,128]{5,4,3,2,1,0:T(8,128)(2,1)}, bf16[2,2,4,2,64,512]{5,4,3,2,1,0:T(8,128)...) custom-call(bf16[64,256]{1,0:T(8,128)(2,1)} %slice.124.refs_0_, ...), custom_call_target="tpu_custom_call" | custom-call | tf_op jit(solution)/shard_map/gather_weights/pallas_call | solution.py:870
  57.5 2.0 copy.29
  59.6 0.9 slice.132
  62.7 1.5 copy.30
  64.1 0.9 pad_maximum_fusion
  65.0 1.4 copy.39
  66.8 0.9 copy.48
  67.7 1.6 copy.33
  69.3 2.0 copy.41
  71.3 1.6 copy.34
  72.9 1.7 copy.47
  74.7 20.2 %first_pass.1 = (bf16[4096,1536]{1,0:T(8,128)(2,1)}, bf16[2,512,256]{2,1,0:T(8,128)(2,1)}, bf16[2,256,256]{2,1,0:T(8,128)(2,1)}, f32[2,8,256]{2,1,0:T(8,128)}) custom-call(s32[1,4]{1,0:T(1,128)} %len_ref.7, bf16[4096,512]{1,0:T(8,128)(2,1)} %tok_ref.5, f32[8,512]{1,0:T(8,128)} %reshape.242.vec_ref, bf16[512,1536]{1,0:T(8,128)(2,1)} %bitcast.47), custom_call_target="tpu_custom_call" | custom-call | flops 8589934592 | bytes 16777216 | tf_op jit(solution)/shard_map/first_pass/pallas_call | solution.py:149
  94.9 23.0 %second_pass.1 = (bf16[4096,512]{1,0:T(8,128)(2,1)}, bf16[4096,512]{1,0:T(8,128)(2,1)}, bf16[4096,512]{1,0:T(8,128)(2,1)}, bf16[4096,512]{1,0:T(8,128)(2,1)}, bf16[64,128,512]{2,1,0:T(8,128)(2,1)}) custom-call(s32[1,4]{1,0:T(1,128)} %len_ref.7, bf16[4096,1536]{1,0:T(8,128)(2,1)} %get-tuple-element.96.q_ref.k_lo.k_ref.k_hi.v_lo.v_ref.v_hi.qkv_ref, ...), custom_call_target="tpu_custom_call" | custom-call | flops 8589934592 | bytes 37748736 | tf_op jit(solution)/shard_map/second_pass/pallas_call | solution.py:269
  117.8 94.5 %third_pass.1 = (bf16[4096,512]{1,0:T(8,128)(2,1)}, bf16[4096,512]{1,0:T(8,128)(2,1)}, bf16[4096,512]{1,0:T(8,128)(2,1)}, bf16[4096,512]{1,0:T(8,128)(2,1)}, bf1...) custom-call(s32[1,4]{1,0:T(1,128)} %len_ref.7, ...), custom_call_target="tpu_custom_call" | custom-call | flops 60129542144 | bytes 46137344 | tf_op jit(solution)/shard_map/third_pass/pallas_call | solution.py:451
  212.4 61.0 %fourth_pass.1 = (bf16[4096,512]{1,0:T(8,128)(2,1)}, bf16[4,8,64,256]{3,2,1,0:T(8,128)(2,1)}, bf16[4,8,64,128]{3,2,1,0:T(8,128)(2,1)}, f32[2,8,512]{2,1,0:T(8,128)}) custom-call(s32[1,4]{1,0:T(1,128)} %len_ref.7, bf16[4096,1536]{1,0:T(8,128)(2,1)} %get-tuple-element.96.q_ref.k_lo.k_ref.k_hi.v_lo.v_ref.v_hi.qkv_ref, ...), custom_call_target="tpu_custom_call" | custom-call | flops 30064771072 | bytes 50331648 | tf_op jit(solution)/shard_map/fourth_pass/pallas_call | solution.py:667
  275.4 48.9 %scatter_grads.1 = (f32[64,256]{1,0:T(8,128)}, f32[64,128]{1,0:T(8,128)}, f32[64,512]{1,0:T(8,128)}, f32[128,256]{1,0:T(8,128)}, f32[64,128]{1,0:T(8,128)}, /*index=5*/f32[8,128]{1,0:T(8,128)}) custom-call(bf16[2,2,4,2,64,256]{5,4,3,2,1,0:T(8,128)(2,1)} %bitcast.57, bf16[2,2,4,2,64,128]{5,4,3,2,1,0:T(8,128)(2,1)} %bitcast.60, ...), custom_call_target="tpu_custom_call" | custom-call | tf_op jit(solution)/shard_map/scatter_grads/pallas_call | solution.py:1011
  324.3 1.5 pad_maximum_fusion.1
  325.8 1.2 slice_bitcast_fusion
  327.0 1.2 slice.129
  328.2 1.7 copy.36
  329.9 1.4 copy.53
  331.2 1.6 copy.54
  (30 shorter events, 6.0 us)
Async XLA Ops:
  2.1 2.7 copy-start.5
  64.1 2.3 copy-start.2
  65.0 2.7 copy-start.1
  69.3 2.0 copy-start
  212.4 61.8 %copy-start.4 = (f32[8,2048]{1,0:T(8,128)S(1)}, f32[8,2048]{1,0:T(8,128)}, u32[]{:S(2)}) copy-start(f32[8,2048]{1,0:T(8,128)} %get-tuple-element.123) | copy-start | bytes 196612
  212.4 61.9 %copy-start.3 = (f32[8,8,512]{2,1,0:T(8,128)S(1)}, f32[8,8,512]{2,1,0:T(8,128)}, u32[]{:S(2)}) copy-start(f32[8,8,512]{2,1,0:T(8,128)} %get-tuple-element.122) | copy-start | bytes 393220

commit v3 on v1

v3 whole, which is shorter than its diff:
```python
import functools
import math

import jax
import jax.numpy as jnp
import numpy as np
from jax import lax
from jax.experimental import pallas as pl
from jax.experimental.pallas import tpu as pltpu
from jax.sharding import PartitionSpec as P

HEADS = 8
BAND = 30
QB = 64
HALO = 32
KW = QB + 2 * HALO
GW = 256

norm_eps = 1e-05
f32 = jnp.float32
bf16 = jnp.bfloat16
exact = lax.Precision.HIGHEST
VMEM_LIMIT = 60 * 1024 * 1024


def nn(a, b):
    return lax.dot_general(a, b, (((1,), (0,)), ((), ())), preferred_element_type=f32)


def nt(a, b):
    return lax.dot_general(a, b, (((1,), (1,)), ((), ())), preferred_element_type=f32)


def tn(a, b):
    return lax.dot_general(a, b, (((0,), (0,)), ((), ())), preferred_element_type=f32)


def nt_exact(a, b):
    return lax.dot_general(
        a, b, (((1,), (1,)), ((), ())), preferred_element_type=f32, precision=exact
    )


def first_part(cols):
    return 128 * ((cols // 128 + 1) // 2) if cols >= 256 else cols // 2


def lift(t):
    return jnp.where(t > 0, t + 1.0, jnp.exp(jnp.minimum(t, 0.0)))


def moments(x):
    mean = jnp.mean(x, axis=-1, keepdims=True)
    cen = x - mean
    inv = lax.rsqrt(jnp.mean(cen * cen, axis=-1, keepdims=True) + norm_eps)
    return cen * inv, inv


def fold8(x):
    return jnp.sum(x.reshape(x.shape[0] // 8, 8, x.shape[1]), axis=0)


def row_valid(step, rows, width, length):
    ids = step * rows + lax.broadcasted_iota(jnp.int32, (rows, width), 0)
    return ids < length


def same_head(head):
    r = lax.broadcasted_iota(jnp.int32, (GW, GW), 0) // head
    c = lax.broadcasted_iota(jnp.int32, (GW, GW), 1) // head
    return r == c


def spread_rows(x, mask_low):
    return jnp.concatenate([x] * (GW // QB), axis=0) * mask_low


def pick_heads(x, head):
    lane = lax.broadcasted_iota(jnp.int32, (QB, GW), 1) // head
    out = x[:QB]
    for h in range(1, GW // QB):
        out = jnp.where(lane == h, x[h * QB : (h + 1) * QB], out)
    return out


def join_blocks(ref, got, lo=0, step=None):
    n_dp, n_fsdp, r, c = got.shape
    step = c if step is None else step
    for d in range(n_dp):
        for f in range(n_fsdp):
            ref[f * r : (f + 1) * r, d * step + lo : d * step + lo + c] = got[d, f]


def cut_blocks(ref, acc, lo=0, step=None, swap=False):
    n_dp, n_fsdp, r, c = ref.shape
    step = c if step is None else step
    for d in range(n_dp):
        for f in range(n_fsdp):
            if swap:
                block = acc[d * r : (d + 1) * r, f * c : (f + 1) * c]
            else:
                block = acc[f * r : (f + 1) * r, d * step + lo : d * step + lo + c]
            ref[d, f] = block.astype(ref.dtype)


def band_table(head):
    key = np.arange(KW)[:, None] - HALO
    query = np.arange(GW)[None, :] % QB
    return np.where(np.abs(key - query) <= BAND, 0.0, -1e30).astype(np.float32)


def head_table(head):
    r = np.arange(GW)[:, None] // QB
    c = np.arange(GW)[None, :] // head
    return (r == c).astype(np.float32)


MESH = pl.DeviceIdType.MESH


class Place:
    def __init__(self, n_dp, n_fsdp):
        self.m = n_fsdp // 2
        self.nh = n_dp // 2
        d = lax.axis_index("dp")
        f = lax.axis_index("fsdp")
        self.dh, self.dl = d // 2, lax.rem(d, 2)
        self.fh, self.fl = f // 2, lax.rem(f, 2)

    def dev(self, dh=None, dl=None, fh=None, fl=None):
        dh = self.dh if dh is None else dh
        dl = self.dl if dl is None else dl
        fh = self.fh if fh is None else fh
        fl = self.fl if fl is None else fl
        return {"dp": dh * 2 + dl, "fsdp": fh * 2 + fl}

    def partners(self):
        out = [self.dev(fh=lax.rem(self.fh + o, self.m)) for o in range(1, self.m)]
        out += [self.dev(dh=lax.rem(self.dh + o, self.nh)) for o in range(1, self.nh)]
        return out + [self.dev(fl=1 - self.fl), self.dev(dl=1 - self.dl)]


def greet(place):
    barrier = pltpu.get_barrier_semaphore()
    who = place.partners()
    for dev in who:
        pl.semaphore_signal(barrier, inc=1, device_id=dev, device_id_type=MESH)
    pl.semaphore_wait(barrier, len(who))


def copy_to(src, dst, send, recv, dev):
    return pltpu.make_async_remote_copy(
        src_ref=src, dst_ref=dst, send_sem=send, recv_sem=recv, device_id=dev, device_id_type=MESH
    )


class Gather:
    def __init__(self, place, shard, got, send, recv, local, order):
        self.p, self.shard, self.got, self.order = place, shard, got, order
        self.send, self.recv, self.local = send, recv, local

    @staticmethod
    def count(n_dp, n_fsdp):
        return n_fsdp // 2 - 1 + 1 + n_dp // 2 - 1 + 1

    def own(self):
        p = self.p
        return pltpu.make_async_copy(self.shard, self.got.at[p.dh, p.dl, p.fh, p.fl], self.local)

    def stage(self, k):
        p, g = self.p, self.got
        if k == 0:
            out = []
            for o in range(1, p.m):
                to = p.dev(fh=lax.rem(p.fh + o, p.m))
                dst = g.at[p.dh, p.dl, p.fh, p.fl]
                out.append(copy_to(self.shard, dst, self.send.at[o - 1], self.recv.at[o - 1], to))
            return out
        i = p.m - 1
        if k == 3:
            ref = g.at[:, p.dl]
            return [copy_to(ref, ref, self.send.at[i], self.recv.at[i], p.dev(dl=1 - p.dl))]
        if (k == 1) == (self.order == "x"):
            ref = g.at[p.dh, p.dl, :, p.fl] if k == 1 else g.at[:, p.dl, :, p.fl]
            return [copy_to(ref, ref, self.send.at[i + 1], self.recv.at[i + 1], p.dev(fl=1 - p.fl))]
        ref = g.at[p.dh, p.dl, :, p.fl] if k == 1 else g.at[p.dh, p.dl]
        out = []
        for o in range(1, p.nh):
            to = p.dev(dh=lax.rem(p.dh + o, p.nh))
            out.append(copy_to(ref, ref, self.send.at[i + 1 + o], self.recv.at[i + 1 + o], to))
        return out

    def start(self, k):
        for c in self.stage(k):
            c.start()

    def wait(self, k):
        if k == 0:
            self.own().wait()
        for c in self.stage(k):
            c.wait()

    def turn(self, k):
        self.wait(k)
        self.start(k + 1)


def front_kernel(
    ways,
    plan,
    len_ref,
    tok_ref,
    wqkv,
    win,
    wback,
    wout,
    vec_in,
    bias_in,
    band_ref,
    hm_ref,
    qkv_ref,
    near_ref,
    fa_ref,
    fb_ref,
    rn_ref,
    p_ref,
    m1_ref,
    m2_ref,
    c_ref,
    w_ref,
    vec_ref,
    bin_ref,
    g_in,
    g_back,
    g_out,
    all_s,
    st_ref,
    t_ref,
    ga,
    gb,
    small,
    g_small,
    send,
    recv,
    local,
):
    step = pl.program_id(0)
    steps = pl.num_programs(0) // 2
    rows, width = tok_ref.shape
    groups = width // GW
    head = width // HEADS
    scale = head ** (-0.5)
    length = len_ref[0, 0]
    n_dp, n_fsdp = ways
    cols = vec_in.shape[1]
    place = Place(n_dp, n_fsdp)
    part = ga.shape[-1]
    half_in = win.shape[1] // 2
    half_back = wback.shape[0] // 2

    def piece(j, shard, got, order):
        return Gather(place, shard, got, send.at[j], recv.at[j], local.at[j], order)

    first = [
        piece(0, small, g_small, "x"),
        piece(1, wqkv.at[:, pl.ds(0, part)], ga, "x"),
        piece(2, wqkv.at[:, pl.ds(part, wqkv.shape[1] - part)], gb, "y"),
    ]
    rest = []
    for i in range(2):
        cut = pl.ds(i * half_in, half_in)
        rest.append(piece(3 + i, win.at[:, cut], g_in.at[:, :, :, :, :, cut], "x"))
    for i in range(2):
        cut = pl.ds(i * half_back, half_back)
        rest.append(piece(5 + i, wback.at[cut], g_back.at[:, :, :, :, cut], "y"))
    rest.append(piece(7, wout, g_out, "y"))
    sets = [[rest[0], rest[2]], [rest[1], rest[3], rest[4]]]

    @pl.when(step == 0)
    def _():
        small[...] = jnp.zeros_like(small)
        small[:2, :cols] = vec_in[...]
        small[2:3, :cols] = bias_in[...]
        for x in first + rest:
            x.own().start()
        greet(place)
        for x in first:
            x.start(0)
        for k in range(3):
            for x in first:
                x.turn(k)
            if k == 1:
                for x in sets[0] + sets[1]:
                    x.start(0)
        st_ref[...] = jnp.zeros_like(st_ref)
        t_ref[...] = jnp.zeros_like(t_ref)
        all_s[:HALO] = jnp.zeros((HALO, 3 * width), bf16)
        all_s[HALO + steps * rows :] = jnp.zeros((HALO, 3 * width), bf16)
        for x in first:
            x.wait(3)
        join_pairs(w_ref, ga, 0, wqkv.shape[1])
        join_pairs(w_ref, gb, part, wqkv.shape[1])
        lane = lax.broadcasted_iota(jnp.int32, (128, width), 0)
        col = lax.broadcasted_iota(jnp.int32, (128, width), 1)

        def place_small(f, total):
            spot = ((lane + f * cols == col) & (lane < cols)).astype(bf16)
            block = jnp.concatenate(
                [g_small[d // 2, d % 2, f // 2, lax.rem(f, 2)] for d in range(n_dp)], axis=0
            )
            return total + nn(block, spot)

        total = lax.fori_loop(0, n_fsdp, place_small, jnp.zeros((16 * n_dp, width), f32))
        for d in range(n_dp):
            vec_ref[2 * d : 2 * d + 2] = total[16 * d : 16 * d + 2]
            bin_ref[0:1, d * width : (d + 1) * width] = total[16 * d + 2 : 16 * d + 3]

    for at, moves in plan.items():

        @pl.when(step == at)
        def _(moves=moves):
            for which, k in moves:
                for x in sets[which]:
                    if k < 3:
                        x.turn(k)
                    else:
                        x.wait(k)

    @pl.when(step < steps)
    def _():
        z, _ = moments(tok_ref[...].astype(f32))
        h = (z * vec_ref[0:1] + vec_ref[1:2]).astype(bf16)
        lo = pl.multiple_of(HALO + step * rows, HALO)
        q = nn(h, w_ref[:, :width]).astype(bf16)
        qkv_ref[:, :width] = q
        all_s[pl.ds(lo, rows), :width] = q
        valid = row_valid(step, rows, GW, length)
        for g in range(groups):
            kc = slice(width + g * GW, width + (g + 1) * GW)
            vc = slice(2 * width + g * GW, 2 * width + (g + 1) * GW)
            k = nn(h, w_ref[:, kc]).astype(bf16)
            v = nn(h, w_ref[:, vc]).astype(bf16)
            qkv_ref[:, kc] = k
            qkv_ref[:, vc] = v
            all_s[pl.ds(lo, rows), kc] = k
            all_s[pl.ds(lo, rows), vc] = v
            kw = k.astype(f32)
            phi = jnp.where(valid, lift(kw), 0.0)
            bent = jnp.where(valid, jnp.tanh(kw), 0.0)
            both = jnp.concatenate([phi.astype(bf16), bent.astype(bf16)], axis=1)
            st_ref[g] += tn(v, both)
            t_ref[g] += fold8(phi)

    @pl.when(step == steps - 1)
    def _():
        mask = same_head(head).astype(f32)
        inv_len = 1.0 / length.astype(f32)
        ones = jnp.ones((8, GW), f32)
        for g in range(groups):
            tb = jnp.sum(t_ref[g], axis=0, keepdims=True) * mask
            s1 = st_ref[g][:, :GW] * mask
            s2 = st_ref[g][:, GW:] * mask
            c_col = jnp.sum(s1, axis=1, keepdims=True) / jnp.sum(tb, axis=1, keepdims=True)
            c_row = nt_exact(ones, s1) / nt_exact(ones, tb)
            m1_ref[g, :GW] = (s1 - c_col * tb).astype(bf16)
            m1_ref[g, GW:] = tb.astype(bf16)
            m2_ref[g] = (s2 * inv_len).astype(bf16)
            c_ref[g] = c_row

    @pl.when(step >= steps)
    def _():
        hm = hm_ref[...]
        at = (step - steps) * rows
        for b in range(rows // QB):
            base = at + b * QB - HALO
            key = base + lax.broadcasted_iota(jnp.int32, (KW, GW), 0)
            bias = jnp.where((key >= 0) & (key < length), band_ref[...], -1e30)
            here = pl.ds(pl.multiple_of(at + b * QB + HALO, HALO), QB)
            window = pl.ds(pl.multiple_of(at + b * QB, QB), KW)
            for g in range(groups):
                cut = slice(g * GW, (g + 1) * GW)
                kc = slice(width + g * GW, width + (g + 1) * GW)
                vc = slice(2 * width + g * GW, 2 * width + (g + 1) * GW)
                qs = spread_rows(all_s[here, cut] * scale, hm)
                s = nt(all_s[window, kc], qs) + bias
                e = jnp.exp(s - jnp.max(s, axis=0, keepdims=True))
                p = (e * (1.0 / jnp.sum(e, axis=0, keepdims=True))).astype(bf16)
                p_ref[b, :, cut] = p
                o = tn(p, all_s[window, vc])
                near_ref[b * QB : (b + 1) * QB, cut] = pick_heads(o, head).astype(bf16)
        for g in range(groups):
            cut = slice(g * GW, (g + 1) * GW)
            q = all_s[pl.ds(pl.multiple_of(at + HALO, HALO), rows), cut].astype(f32)
            both = nt(lift(q).astype(bf16), m1_ref[g])
            rn = 1.0 / both[:, GW:]
            rn_ref[:, cut] = rn.astype(bf16)
            fa_ref[:, cut] = (both[:, :GW] * rn).astype(bf16)
            fb_ref[:, cut] = nt(jnp.tanh(q).astype(bf16), m2_ref[g]).astype(bf16)


def join_pairs(ref, got, lo, step):
    nh, _, m, _, r, c = got.shape
    for d in range(2 * nh):
        for f in range(2 * m):
            ref[f * r : (f + 1) * r, d * step + lo : d * step + lo + c] = got[d // 2, d % 2, f // 2, f % 2]


def front_pass(ways, length, tokens, w_qkv, w_in, w_back, w_out, vec, bias, tile, plan):
    rows, width = tokens.shape
    groups = width // GW
    n_dp, n_fsdp = ways
    nh, m = n_dp // 2, n_fsdp // 2
    steps = rows // tile
    head = width // HEADS
    part = first_part(w_qkv.shape[1])
    const = lambda *shape: pl.BlockSpec(shape, lambda i: (0,) * len(shape))
    early = lambda i: (jnp.minimum(i, steps - 1), 0)
    late = pl.BlockSpec((tile, width), lambda i: (jnp.maximum(i - steps, 0), 0))
    hbm = pl.BlockSpec(memory_space=pl.ANY)
    sds = jax.ShapeDtypeStruct
    got = lambda r, c: (nh, 2, m, 2, r, c)
    hidden = w_in.shape[1] * n_dp
    pieces = 8
    per = Gather.count(n_dp, n_fsdp)
    return pl.pallas_call(
        functools.partial(front_kernel, ways, plan),
        grid=(2 * steps,),
        in_specs=[
            pl.BlockSpec(memory_space=pltpu.SMEM),
            pl.BlockSpec((tile, width), early),
            hbm,
            hbm,
            hbm,
            hbm,
            const(*vec.shape),
            const(*bias.shape),
            const(KW, GW),
            const(GW, GW),
        ],
        out_specs=[
            pl.BlockSpec((tile, 3 * width), early),
            late,
            late,
            late,
            late,
            pl.BlockSpec((tile // QB, KW, width), lambda i: (jnp.maximum(i - steps, 0), 0, 0)),
            const(groups, 2 * GW, GW),
            const(groups, GW, GW),
            const(groups, 8, GW),
            const(width, 3 * width),
            const(8, width),
            const(1, hidden),
            hbm,
            hbm,
            hbm,
        ],
        out_shape=[sds((rows, 3 * width), bf16)]
        + [sds((rows, width), bf16)] * 4
        + [
            sds((rows // QB, KW, width), bf16),
            sds((groups, 2 * GW, GW), bf16),
            sds((groups, GW, GW), bf16),
            sds((groups, 8, GW), f32),
            sds((width, 3 * width), bf16),
            sds((8, width), f32),
            sds((1, hidden), f32),
            sds(got(*w_in.shape), bf16),
            sds(got(*w_back.shape), bf16),
            sds(got(*w_out.shape), bf16),
        ],
        scratch_shapes=[
            pltpu.VMEM((rows + 2 * HALO, 3 * width), bf16),
            pltpu.VMEM((groups, GW, 2 * GW), f32),
            pltpu.VMEM((groups, 8, GW), f32),
            pltpu.VMEM(got(w_qkv.shape[0], part), bf16),
            pltpu.VMEM(got(w_qkv.shape[0], w_qkv.shape[1] - part), bf16),
            pltpu.VMEM((16, 128), bf16),
            pltpu.VMEM(got(16, 128), bf16),
            pltpu.SemaphoreType.DMA((pieces, per)),
            pltpu.SemaphoreType.DMA((pieces, per)),
            pltpu.SemaphoreType.DMA((pieces,)),
        ],
        compiler_params=pltpu.CompilerParams(
            collective_id=0, has_side_effects=True, vmem_limit_bytes=VMEM_LIMIT
        ),
        cost_estimate=pl.CostEstimate(
            flops=2 * rows * width * 8 * width, bytes_accessed=rows * width * 24, transcendentals=0
        ),
        name="front_pass",
    )(
        length,
        tokens,
        w_qkv,
        w_in,
        w_back,
        w_out,
        vec,
        bias,
        jnp.asarray(band_table(head)),
        jnp.asarray(head_table(head), bf16),
    )


def ffn_kernel(
    chunk,
    len_ref,
    tok_ref,
    cot_ref,
    near_ref,
    fa_ref,
    fb_ref,
    rn_ref,
    q_ref,
    c_ref,
    vec_ref,
    bin_ref,
    gw_out,
    gw_in,
    gw_back,
    out_ref,
    datt_ref,
    dmix_ref,
    dn_ref,
    gin_ref,
    gback_ref,
    gout_ref,
    gvec_ref,
    gbias_ref,
    m3_ref,
    m4_ref,
    dt_ref,
    a_in,
    a_back,
    a_out,
    a_st,
    a_bent,
    wout_ref,
    win_ref,
    wback_ref,
):
    step = pl.program_id(0)
    rows, width = tok_ref.shape
    hidden = win_ref.shape[1]
    groups = width // GW
    head = width // HEADS
    length = len_ref[0, 0]

    @pl.when(step == 0)
    def _():
        join_blocks(wout_ref, gw_out)
        join_blocks(win_ref, gw_in)
        join_blocks(wback_ref, gw_back)
        a_in[...] = jnp.zeros_like(a_in)
        a_back[...] = jnp.zeros_like(a_back)
        a_out[...] = jnp.zeros_like(a_out)
        a_st[...] = jnp.zeros_like(a_st)
        a_bent[...] = jnp.zeros_like(a_bent)
        gvec_ref[...] = jnp.zeros_like(gvec_ref)
        gbias_ref[...] = jnp.zeros_like(gbias_ref)

    c_row = jnp.concatenate([c_ref[g, 0:1] for g in range(groups)], axis=1)
    near = near_ref[...].astype(f32)
    fac = fa_ref[...].astype(f32)
    far_b = fb_ref[...].astype(f32)
    mixed = (
        vec_ref[5:6] * near + vec_ref[6:7] * (fac + c_row) + vec_ref[7:8] * far_b
    ).astype(bf16)
    resid = tok_ref[...].astype(f32) + nn(mixed, wout_ref[...])
    z2, r2 = moments(resid)
    h2 = (z2 * vec_ref[2:3] + vec_ref[3:4]).astype(bf16)
    valid = row_valid(step, rows, width, length)
    seed = jnp.where(valid, cot_ref[...].astype(f32), 0.0)
    d_ffn = seed.astype(bf16)
    s0 = math.sqrt(2.0 / math.pi)
    s1 = s0 * 0.044715
    ffn = jnp.zeros((rows, width), f32)
    dh2 = jnp.zeros((rows, width), f32)
    for lo in range(0, hidden, chunk):
        cols = slice(lo, lo + chunk)
        x = nn(h2, win_ref[:, cols]) + bin_ref[0:1, cols]
        x2 = x * x
        t = jnp.tanh(x * (s0 + s1 * x2))
        half = 0.5 + 0.5 * t
        act = x * half
        slope = half + (act - act * half) * (2 * s0 + 6 * s1 * x2)
        act = act.astype(bf16)
        ffn += nn(act, wback_ref[cols, :])
        a_back[:, cols] += tn(d_ffn, act)
        d_pre = slope * nt(d_ffn, wback_ref[cols, :])
        gbias_ref[:, cols] += fold8(d_pre)
        d_pre = d_pre.astype(bf16)
        a_in[:, cols] += tn(h2, d_pre)
        dh2 += nt(d_pre, win_ref[:, cols])
    out_ref[...] = jnp.where(valid, resid + ffn + vec_ref[4:5], 0.0).astype(bf16)
    gvec_ref[2] += fold8(dh2 * z2)
    gvec_ref[3] += fold8(dh2)
    gvec_ref[4] += fold8(seed)
    dz = dh2 * vec_ref[2:3]
    d_resid = seed + r2 * (
        dz
        - jnp.mean(dz, axis=-1, keepdims=True)
        - z2 * jnp.mean(dz * z2, axis=-1, keepdims=True)
    )
    d_attn = d_resid.astype(bf16)
    datt_ref[...] = d_attn
    a_out[...] += tn(mixed, d_attn)
    d_mix = nt(d_attn, wout_ref[...])
    dmix_ref[...] = d_mix.astype(bf16)
    gvec_ref[5] += fold8(d_mix * near)
    gvec_ref[6] += fold8(d_mix * fac)
    gvec_ref[7] += fold8(d_mix * far_b)
    gvec_ref[0] += fold8(d_mix)
    d_num = (vec_ref[6:7] * d_mix * rn_ref[...].astype(f32)).astype(bf16)
    dn_ref[...] = d_num
    d_den = (d_num.astype(f32) * fac).astype(bf16)
    d_far = (vec_ref[7:8] * d_mix).astype(bf16)
    for g in range(groups):
        cols = slice(g * GW, (g + 1) * GW)
        q = q_ref[:, cols].astype(f32)
        a_st[g] += tn(lift(q).astype(bf16), jnp.concatenate([d_num[:, cols], d_den[:, cols]], axis=1))
        a_bent[g] += tn(jnp.tanh(q).astype(bf16), d_far[:, cols])

    @pl.when(step == pl.num_programs(0) - 1)
    def _():
        mask = same_head(head).astype(f32)
        inv_len = 1.0 / length.astype(f32)
        ones = jnp.ones((8, GW), f32)
        for g in range(groups):
            m3_ref[g] = (a_st[g][:, :GW] * mask).astype(bf16)
            m4_ref[g] = (a_bent[g] * mask * inv_len).astype(bf16)
            dt_ref[g] = -nt_exact(ones, a_st[g][:, GW:] * mask)
        cut_blocks(gin_ref, a_in)
        cut_blocks(gback_ref, a_back, swap=True)
        cut_blocks(gout_ref, a_out)
        gvec_ref[6] += gvec_ref[0] * c_row


def third_pass(ways, length, tokens, cot, near, fa, fb, rn, qkv, c, vecs, b_in, w_out, w_in, w_back, tile, chunk):
    rows, width = tokens.shape
    hidden = w_in.shape[0] * w_in.shape[3]
    groups = width // GW
    n_dp, n_fsdp = ways
    const = lambda *shape: pl.BlockSpec(shape, lambda i: (0,) * len(shape))
    block = pl.BlockSpec((tile, width), lambda i: (i, 0))
    sds = jax.ShapeDtypeStruct
    return pl.pallas_call(
        functools.partial(ffn_kernel, chunk),
        grid=(rows // tile,),
        in_specs=[pl.BlockSpec(memory_space=pltpu.SMEM)]
        + [block] * 7
        + [
            const(groups, 8, GW),
            const(8, width),
            const(1, hidden),
            const(*w_out.shape),
            const(*w_in.shape),
            const(*w_back.shape),
        ],
        out_specs=[block] * 4
        + [
            const(n_dp, n_fsdp, width // n_fsdp, hidden // n_dp),
            const(n_dp, n_fsdp, width // n_dp, hidden // n_fsdp),
            const(n_dp, n_fsdp, width // n_fsdp, width // n_dp),
            const(8, 8, width),
            const(8, hidden),
            const(groups, GW, GW),
            const(groups, GW, GW),
            const(groups, 8, GW),
        ],
        out_shape=[sds((rows, width), bf16)] * 4
        + [
            sds((n_dp, n_fsdp, width // n_fsdp, hidden // n_dp), bf16),
            sds((n_dp, n_fsdp, width // n_dp, hidden // n_fsdp), bf16),
            sds((n_dp, n_fsdp, width // n_fsdp, width // n_dp), bf16),
            sds((8, 8, width), f32),
            sds((8, hidden), f32),
            sds((groups, GW, GW), bf16),
            sds((groups, GW, GW), bf16),
            sds((groups, 8, GW), f32),
        ],
        scratch_shapes=[
            pltpu.VMEM((width, hidden), f32),
            pltpu.VMEM((width, hidden), f32),
            pltpu.VMEM((width, width), f32),
            pltpu.VMEM((groups, GW, 2 * GW), f32),
            pltpu.VMEM((groups, GW, GW), f32),
            pltpu.VMEM((width, width), bf16),
            pltpu.VMEM((width, hidden), bf16),
            pltpu.VMEM((hidden, width), bf16),
        ],
        compiler_params=pltpu.CompilerParams(vmem_limit_bytes=VMEM_LIMIT),
        cost_estimate=pl.CostEstimate(
            flops=2 * rows * width * (6 * hidden + 4 * width),
            bytes_accessed=rows * width * 22,
            transcendentals=0,
        ),
        name="third_pass",
    )(length, tokens, cot, near, fa, fb, rn, qkv, c, vecs, b_in, w_out, w_in, w_back)


class Scatter:
    def __init__(self, place, src, out, bufs, send, recv, local, order):
        self.p, self.src, self.out, self.order = place, src, out, order
        self.acc, self.r0, self.r1, self.r2, self.r3 = bufs
        self.send, self.recv, self.local = send, recv, local

    @staticmethod
    def count(n_dp, n_fsdp):
        return 1 + 1 + (n_dp // 2 - 1) + (n_fsdp // 2 - 1)

    @staticmethod
    def scratch(n_dp, n_fsdp, r, c, order, dtype):
        nh, m = n_dp // 2, n_fsdp // 2
        if order == "x":
            one, two = (nh, m, r, c), (nh - 1, m, r, c)
        else:
            one, two = (nh - 1, m, 2, r, c), (m, r, c)
        shapes = [(nh, m, 2, r, c), (nh, m, 2, r, c), one, two, (m - 1, r, c)]
        return [pltpu.VMEM(s, dtype) for s in shapes]

    def own(self):
        return pltpu.make_async_copy(self.src.at[:, self.p.dl], self.acc, self.local)

    def stage(self, k):
        p = self.p
        if k == 0:
            ref = self.src.at[:, 1 - p.dl]
            return [copy_to(ref, self.r0, self.send.at[0], self.recv.at[0], p.dev(dl=1 - p.dl))]
        if k == 3:
            i = p.nh
            out = []
            for o in range(1, p.m):
                fh = lax.rem(p.fh + o, p.m)
                out.append(
                    copy_to(self.acc.at[p.dh, fh, p.fl], self.r3.at[o - 1], self.send.at[i + o], self.recv.at[i + o],
                            p.dev(fh=fh))
                )
            return out
        if (k == 1) == (self.order == "x"):
            ref = self.acc.at[:, :, 1 - p.fl] if k == 1 else self.acc.at[p.dh, :, 1 - p.fl]
            dst = self.r1 if k == 1 else self.r2
            return [copy_to(ref, dst, self.send.at[1], self.recv.at[1], p.dev(fl=1 - p.fl))]
        out = []
        for o in range(1, p.nh):
            dh = lax.rem(p.dh + o, p.nh)
            ref = self.acc.at[dh] if k == 1 else self.acc.at[dh, :, p.fl]
            dst = self.r1.at[o - 1] if k == 1 else self.r2.at[o - 1]
            out.append(copy_to(ref, dst, self.send.at[1 + o], self.recv.at[1 + o], p.dev(dh=dh)))
        return out

    def start(self, k):
        for c in self.stage(k):
            c.start()

    def turn(self, k):
        if k == 0:
            self.own().wait()
        for c in self.stage(k):
            c.wait()
        self.add(k)
        if k < 3:
            self.start(k + 1)

    def add(self, k):
        p, acc = self.p, self.acc
        nh, m = p.nh, p.m
        dt = acc.dtype

        def put(index, others):
            total = acc[index].astype(f32)
            for o in others:
                total = total + o.astype(f32)
            acc[index] = total.astype(dt)

        if k == 3:
            total = acc[p.dh, p.fh, p.fl].astype(f32)
            for o in range(1, m):
                total = total + self.r3[o - 1].astype(f32)
            self.out[...] = total
            return

        @pl.loop(0, m)
        def _(i):
            if k == 0:
                for a in range(nh):
                    for b in range(2):
                        put((a, i, b), [self.r0[a, i, b]])
            elif k == 1 and self.order == "x":
                for a in range(nh):
                    put((a, i, p.fl), [self.r1[a, i]])
            elif k == 1:
                for b in range(2):
                    put((p.dh, i, b), [self.r1[o - 1, i, b] for o in range(1, nh)])
            elif self.order == "x":
                put((p.dh, i, p.fl), [self.r2[o - 1, i] for o in range(1, nh)])
            else:
                put((p.dh, i, p.fl), [self.r2[i]])


def back_kernel(
    ways,
    plan,
    len_ref,
    q_ref,
    k_lo,
    k_ref,
    k_hi,
    v_lo,
    v_ref,
    v_hi,
    p_ref,
    dmix_ref,
    qkv_ref,
    tok_ref,
    datt_ref,
    dn_ref,
    fa_ref,
    dmp_ref,
    m1_ref,
    m2_ref,
    m3_ref,
    m4_ref,
    dt_ref,
    c_ref,
    vec_ref,
    w_ref,
    hm_ref,
    gv_ref,
    gbias_ref,
    s_in,
    s_back,
    s_out,
    dtok_ref,
    oqkv_ref,
    oin_ref,
    oback_ref,
    oout_ref,
    ovec_ref,
    obias_ref,
    kk,
    vv,
    dq_s,
    dk_s,
    dv_s,
    a_qkv,
    gvec_ref,
    ga_ref,
    gb_ref,
    gs_ref,
    rows_s,
    back_t,
    small_o,
    *rest,
):
    step = pl.program_id(0)
    steps = pl.num_programs(0) - 1
    rows, width = q_ref.shape
    groups = width // GW
    head = width // HEADS
    scale = head ** (-0.5)
    length = len_ref[0, 0]
    place = Place(*ways)
    n_dp, n_fsdp = ways
    cols = ovec_ref.shape[1]
    part = ga_ref.shape[-1]
    send, recv, local = rest[30:]

    def piece(j, src, out, order):
        return Scatter(place, src, out, rest[5 * j : 5 * j + 5], send.at[j], recv.at[j], local.at[j], order)

    ffn = [
        piece(0, s_in, oin_ref, "x"),
        piece(1, s_back, back_t, "y"),
        piece(2, s_out, oout_ref, "y"),
    ]
    last = [
        piece(3, ga_ref, oqkv_ref.at[:, pl.ds(0, part)], "x"),
        piece(4, gb_ref, oqkv_ref.at[:, pl.ds(part, oqkv_ref.shape[1] - part)], "y"),
        piece(5, gs_ref, small_o, "x"),
    ]

    @pl.when(step == 0)
    def _():
        dk_s[: 2 * HALO] = jnp.zeros((2 * HALO, width), f32)
        dv_s[: 2 * HALO] = jnp.zeros((2 * HALO, width), f32)
        a_qkv[...] = jnp.zeros_like(a_qkv)
        gvec_ref[...] = jnp.zeros_like(gvec_ref)
        for x in ffn:
            x.own().start()
        greet(place)
        for x in ffn:
            x.start(0)

    for at, moves in plan.items():

        @pl.when(step == at)
        def _(moves=moves):
            for k in moves:
                for x in ffn:
                    x.turn(k)

    @pl.when(step < steps)
    def _():
        kk[:HALO] = k_lo[...]
        kk[HALO : HALO + rows] = k_ref[...]
        kk[HALO + rows :] = k_hi[...]
        vv[:HALO] = v_lo[...]
        vv[HALO : HALO + rows] = v_ref[...]
        vv[HALO + rows :] = v_hi[...]
        hm = hm_ref[...]
        slot = lax.rem(step, 2)
        for g in range(groups):
            cut = slice(g * GW, (g + 1) * GW)
            for b in range(rows // QB):
                here = slice(b * QB, (b + 1) * QB)
                window = slice(b * QB, b * QB + KW)
                qs = spread_rows(q_ref[here, cut] * scale, hm)
                d_near = (vec_ref[5:6, cut] * dmix_ref[here, cut].astype(f32)).astype(bf16)
                ds = spread_rows(d_near, hm)
                p = p_ref[b, :, cut]
                pw = p.astype(f32)
                t = pw * nt(vv[window, cut], ds)
                d_s = (t - pw * jnp.sum(t, axis=0, keepdims=True)).astype(bf16)
                dk = nn(d_s, qs)
                dv = nn(p, ds)
                dq_s[slot, here, cut] = pick_heads(tn(d_s, kk[window, cut]), head) * scale
                lo = pl.ds(pl.multiple_of(lax.rem(step * rows + b * QB, 3 * rows), QB), QB)
                hi = pl.ds(pl.multiple_of(lax.rem(step * rows + (b + 1) * QB, 3 * rows), QB), QB)
                dk_s[lo, cut] += dk[:QB]
                dk_s[hi, cut] = dk[QB:]
                dv_s[lo, cut] += dv[:QB]
                dv_s[hi, cut] = dv[QB:]

    @pl.when(step > 0)
    def _():
        slot = lax.rem(step + 1, 2)
        z1, r1 = moments(tok_ref[...].astype(f32))
        h1 = (z1 * vec_ref[0:1] + vec_ref[1:2]).astype(bf16)
        valid = row_valid(step - 1, rows, GW, length)
        lo = pl.ds(pl.multiple_of(lax.rem((step - 1) * rows, 3 * rows) + HALO, HALO), rows - HALO)
        hi = pl.ds(pl.multiple_of(lax.rem(step * rows, 3 * rows), HALO), HALO)
        dqs, dks, dvs = [], [], []
        for g in range(groups):
            cut = slice(g * GW, (g + 1) * GW)
            q = qkv_ref[:, g * GW : (g + 1) * GW].astype(f32)
            k = qkv_ref[:, width + g * GW : width + (g + 1) * GW].astype(f32)
            v = qkv_ref[:, 2 * width + g * GW : 2 * width + (g + 1) * GW]
            d_num = dn_ref[:, cut]
            d_den = (d_num.astype(f32) * -fa_ref[:, cut].astype(f32)).astype(bf16)
            d_far = (vec_ref[7:8, cut] * dmp_ref[:, cut].astype(f32)).astype(bf16)
            bent_q = jnp.tanh(q)
            dq = (
                dq_s[slot, :, cut]
                + nn(jnp.concatenate([d_num, d_den], axis=1), m1_ref[g]) * jnp.minimum(lift(q), 1.0)
                + nn(d_far, m2_ref[g]) * (1.0 - bent_q * bent_q)
            )
            lift_k = lift(k)
            bent_k = jnp.tanh(k)
            v_cen = (v.astype(f32) - c_ref[g, 0:1]).astype(bf16)
            dk = (nt(v_cen, m3_ref[g]) + dt_ref[g, 0:1]) * jnp.minimum(lift_k, 1.0) + nt(
                v, m4_ref[g]
            ) * (1.0 - bent_k * bent_k)
            both = jnp.concatenate([lift_k.astype(bf16), bent_k.astype(bf16)], axis=1)
            dv = nn(both, jnp.concatenate([m3_ref[g], m4_ref[g]], axis=0))
            dqs.append(dq.astype(bf16))
            dks.append((jnp.concatenate([dk_s[lo, cut], dk_s[hi, cut]], axis=0) + jnp.where(valid, dk, 0.0)).astype(bf16))
            dvs.append((jnp.concatenate([dv_s[lo, cut], dv_s[hi, cut]], axis=0) + jnp.where(valid, dv, 0.0)).astype(bf16))
        d_qkv = jnp.concatenate(dqs + dks + dvs, axis=1)
        a_qkv[...] += tn(h1, d_qkv)
        dh1 = nt(d_qkv, w_ref[...])
        gvec_ref[0] += fold8(dh1 * z1)
        gvec_ref[1] += fold8(dh1)
        dz = dh1 * vec_ref[0:1]
        dtok_ref[...] = (
            datt_ref[...].astype(f32)
            + r1
            * (
                dz
                - jnp.mean(dz, axis=-1, keepdims=True)
                - z1 * jnp.mean(dz * z1, axis=-1, keepdims=True)
            )
        ).astype(bf16)

    @pl.when(step == steps)
    def _():
        oback_ref[...] = back_t[...].T
        step_cols = oqkv_ref.shape[1]
        cut_pairs(ga_ref, a_qkv, 0, step_cols)
        cut_pairs(gb_ref, a_qkv, part, step_cols)
        gs_ref[...] = jnp.zeros_like(gs_ref)
        rows_s[0:2] = jnp.sum(gvec_ref[...], axis=1)
        rows_s[2:8] = jnp.sum(gv_ref[2:8], axis=1)
        bias = jnp.sum(gbias_ref[...], axis=0, keepdims=True)
        for d in range(n_dp):
            pair = rows_s[2 * d : 2 * d + 2]
            for f in range(n_fsdp):
                spot = slice(f * cols, (f + 1) * cols)
                gs_ref[d // 2, d % 2, f // 2, f % 2, 0:2, :cols] = pair[:, spot]
                gs_ref[d // 2, d % 2, f // 2, f % 2, 2:3, :cols] = bias[:, d * width + f * cols : d * width + (f + 1) * cols]
        for x in last:
            x.own().start()
            x.start(0)
        for k in range(4):
            for x in last:
                x.turn(k)
        ovec_ref[...] = small_o[0:2, :cols]
        obias_ref[...] = small_o[2:3, :cols]


def cut_pairs(ref, acc, lo, step):
    nh, _, m, _, r, c = ref.shape
    for d in range(2 * nh):
        for f in range(2 * m):
            block = acc[f * r : (f + 1) * r, d * step + lo : d * step + lo + c]
            ref[d // 2, d % 2, f // 2, f % 2] = block.astype(ref.dtype)


def back_pass(
    ways, length, qkv, p, d_mix, tokens, d_attn, d_num, fa, m1, m2, m3, m4, dt, c, vecs, w_qkv, gv, gbias, s_in, s_back, s_out, tile, plan
):
    rows, width = tokens.shape
    groups = width // GW
    steps = rows // tile
    n_dp, n_fsdp = ways
    r, c_all = width // n_fsdp, 3 * width // n_dp
    part = first_part(c_all)
    nh, m = n_dp // 2, n_fsdp // 2
    hbm = pl.BlockSpec(memory_space=pl.ANY)
    back_shape = s_back.shape[-2:]
    outs = [
        (r, c_all),
        s_in.shape[-2:],
        back_shape[::-1],
        s_out.shape[-2:],
        (2, width // n_fsdp),
        (1, gbias.shape[1] // (n_dp * n_fsdp)),
    ]
    kinds = [
        (*s_in.shape[-2:], "x", bf16),
        (*back_shape, "y", bf16),
        (*s_out.shape[-2:], "y", bf16),
        (r, part, "x", bf16),
        (r, c_all - part, "y", bf16),
        (8, 128, "x", f32),
    ]
    bufs = [b for k in kinds for b in Scatter.scratch(n_dp, n_fsdp, *k)]
    per = Scatter.count(n_dp, n_fsdp)
    got = lambda *s: (nh, 2, m, 2, *s)
    const = lambda *shape: pl.BlockSpec(shape, lambda i: (0,) * len(shape))
    now = lambda i: jnp.minimum(i, steps - 1)
    old = lambda i: jnp.maximum(i - 1, 0)
    per = tile // HALO
    last = rows // HALO - 1

    def halo(col):
        return [
            pl.BlockSpec((HALO, width), lambda i: (jnp.maximum(now(i) * per - 1, 0), col)),
            pl.BlockSpec((tile, width), lambda i: (now(i), col)),
            pl.BlockSpec((HALO, width), lambda i: (jnp.minimum((now(i) + 1) * per, last), col)),
        ]

    block = pl.BlockSpec((tile, width), lambda i: (now(i), 0))
    late = pl.BlockSpec((tile, width), lambda i: (old(i), 0))
    head = width // HEADS
    sds = jax.ShapeDtypeStruct
    return pl.pallas_call(
        functools.partial(back_kernel, ways, plan),
        grid=(steps + 1,),
        in_specs=[
            pl.BlockSpec(memory_space=pltpu.SMEM),
            block,
            *halo(1),
            *halo(2),
            pl.BlockSpec((tile // QB, KW, width), lambda i: (now(i), 0, 0)),
            block,
            pl.BlockSpec((tile, 3 * width), lambda i: (old(i), 0)),
            late,
            late,
            late,
            late,
            late,
            const(groups, 2 * GW, GW),
            const(groups, GW, GW),
            const(groups, GW, GW),
            const(groups, GW, GW),
            const(groups, 8, GW),
            const(groups, 8, GW),
            const(8, width),
            const(width, 3 * width),
            const(GW, GW),
            const(*gv.shape),
            const(*gbias.shape),
            hbm,
            hbm,
            hbm,
        ],
        out_specs=[late] + [const(*s) for s in outs],
        out_shape=[sds((rows, width), bf16)] + [sds(s, f32) for s in outs],
        scratch_shapes=[
            pltpu.VMEM((tile + 2 * HALO, width), bf16),
            pltpu.VMEM((tile + 2 * HALO, width), bf16),
            pltpu.VMEM((2, tile, width), f32),
            pltpu.VMEM((3 * tile, width), f32),
            pltpu.VMEM((3 * tile, width), f32),
            pltpu.VMEM((width, 3 * width), f32),
            pltpu.VMEM((2, 8, width), f32),
            pltpu.VMEM(got(r, part), bf16),
            pltpu.VMEM(got(r, c_all - part), bf16),
            pltpu.VMEM(got(8, 128), f32),
            pltpu.VMEM((8, width), f32),
            pltpu.VMEM(back_shape, f32),
            pltpu.VMEM((8, 128), f32),
            *bufs,
            pltpu.SemaphoreType.DMA((6, per)),
            pltpu.SemaphoreType.DMA((6, per)),
            pltpu.SemaphoreType.DMA((6,)),
        ],
        compiler_params=pltpu.CompilerParams(
            collective_id=1, has_side_effects=True, vmem_limit_bytes=VMEM_LIMIT
        ),
        cost_estimate=pl.CostEstimate(
            flops=2 * rows * width * 14 * width, bytes_accessed=rows * width * 24, transcendentals=0
        ),
        name="back_pass",
    )(
        length,
        qkv,
        qkv,
        qkv,
        qkv,
        qkv,
        qkv,
        qkv,
        p,
        d_mix,
        qkv,
        tokens,
        d_attn,
        d_num,
        fa,
        d_mix,
        m1,
        m2,
        m3,
        m4,
        dt,
        c,
        vecs,
        w_qkv,
        jnp.asarray(head_table(head), bf16),
        gv,
        gbias,
        s_in,
        s_back,
        s_out,
    )


TILE = 512
CHUNK = 512
FRONT_PLAN = {2: [(0, 0)], 4: [(0, 1), (1, 0)], 6: [(0, 2)], 7: [(1, 1)], 10: [(0, 3), (1, 2)], 13: [(1, 3)]}
BACK_PLAN = {2: [0], 4: [1], 5: [2], 7: [3]}


def shards(
    tokens, cotangent, w_qkv, w_out, w_in, w_back, vec_params, b_in, item_lengths, bucket_counts, *, ways
):
    n_dp, n_fsdp = ways
    (
        qkv,
        near,
        fa,
        fb,
        rn,
        p,
        m1,
        m2,
        c,
        qkv_w,
        vecs,
        in_bias,
        g_in,
        g_back,
        g_out,
    ) = front_pass(
        ways, item_lengths, tokens, w_qkv, w_in, w_back, w_out, vec_params, b_in[None], TILE, FRONT_PLAN
    )

    def blocks(g):
        return g.reshape(n_dp, n_fsdp, *g.shape[-2:])

    def pairs(g):
        return g.reshape(n_dp // 2, 2, n_fsdp // 2, 2, *g.shape[-2:])

    (out, d_attn, d_mix, d_num, s_in, s_back, s_out, g_vec, g_bias, m3, m4, dt) = third_pass(
        ways,
        item_lengths,
        tokens,
        cotangent,
        near,
        fa,
        fb,
        rn,
        qkv,
        c,
        vecs,
        in_bias,
        blocks(g_out),
        blocks(g_in),
        blocks(g_back),
        TILE,
        CHUNK,
    )
    d_tok, r_qkv, r_in, r_back, r_out, r_vec, r_bias = back_pass(
        ways,
        item_lengths,
        qkv,
        p,
        d_mix,
        tokens,
        d_attn,
        d_num,
        fa,
        m1,
        m2,
        m3,
        m4,
        dt,
        c,
        vecs,
        qkv_w,
        g_vec,
        g_bias,
        pairs(s_in),
        pairs(s_back),
        pairs(s_out),
        TILE,
        BACK_PLAN,
    )
    return (out, d_tok, r_qkv, r_out, r_in, r_back, r_vec, r_bias[0])


def solution(mesh):
    in_specs = (
        P(("dp", "fsdp"), None),
        P(("dp", "fsdp"), None),
        P("fsdp", "dp"),
        P("fsdp", "dp"),
        P("fsdp", "dp"),
        P("fsdp", "dp"),
        P("dp", "fsdp"),
        P(("dp", "fsdp")),
        P(("dp", "fsdp"), None),
        P(("dp", "fsdp"), None),
    )
    out_specs = (
        P(("dp", "fsdp"), None),
        P(("dp", "fsdp"), None),
        P("fsdp", "dp"),
        P("fsdp", "dp"),
        P("fsdp", "dp"),
        P("fsdp", "dp"),
        P("dp", "fsdp"),
        P(("dp", "fsdp")),
    )
    ways = (mesh.shape["dp"], mesh.shape["fsdp"])
    body = functools.partial(shards, ways=ways)
    return jax.shard_map(body, mesh=mesh, in_specs=in_specs, out_specs=out_specs, check_vma=False)
```

time: 800 us -> 274 us (0.34)
  waiting for transfers between devices: 340 us -> 0 us
  blocking collectives: 221 us -> 0 us
  Pallas kernels: 199 us -> 265 us
  between operations: 17 us -> 0.71 us
    reduce_scatter x6 -> x0, waiting for transfers between devices: 292 us -> none  [the longest x1 66.1 us: spread(): lax.psum_scatter(section_one[2], 'fsdp', scatter_dimension=0, tiled=True)]
    all_gather x8 -> x0, blocking collectives: 172 us -> none  [the longest x1 35.2 us: collect(): lax.all_gather(w_qkv, 'fsdp', axis=0, tiled=True)]
    pallas_call x3 -> x2, Pallas kernels: 104 us -> 169 us  [the longest x1 95 us: back_pass(): pl.pallas_call(functools.partial(back_kernel, ways, plan), grid=(steps +...]
    unnamed x3 -> x0, blocking collectives: 49.2 us -> none
    unnamed x15 -> x0, waiting for transfers between devices: 48.4 us -> none
  transfers between devices with their start and end apart: 12 -> 0, of which waited for: 7 -> 0; matrix products, arithmetic and copies ran while one was open for 3% -> 0% of each run, Pallas kernels for 13% -> 0%
where the time goes in v3:
time: 274 us
  Pallas kernels  265 us (97%)
  local copies, waits for them, and re-layouts  8.22 us (3%)
    pallas_call x1, Pallas kernels, third_pass(): pl.pallas_call(functools.partial(ffn_kernel, chunk), grid=(rows // tile,)...  95.3 us
    pallas_call x1, Pallas kernels, back_pass(): pl.pallas_call(functools.partial(back_kernel, ways, plan), grid=(steps +...  95 us
    pallas_call x1, Pallas kernels, front_pass(): pl.pallas_call(functools.partial(front_kernel, ways, plan), grid=(2 * ste...  74.5 us
    unnamed x19, local copies, waits for them, and re-layouts  8.22 us

profile of v3, /device:TPU:0, one launch (start us, length us, event | category | flops | bytes accessed | tf_op | source)
XLA Modules:
  0.0 273.7 jit_solution(9372831653947691487)
XLA Ops:
  0.6 74.5 %front_pass.1 = (bf16[4096,1536]{1,0:T(8,128)(2,1)}, bf16[4096,512]{1,0:T(8,128)(2,1)}, bf16[4096,512]{1,0:T(8,128)(2,1)}, bf16[4096,512]{1,0:T(8,128)(2,1)}, bf...) custom-call(s32[1,4]{1,0:T(1,128)} %len_ref.5, ...), custom_call_target="tpu_custom_call" | custom-call | flops 17179869184 | bytes 50331648 | tf_op jit(solution)/shard_map/front_pass/pallas_call | solution.py:425
  75.1 95.3 %third_pass.1 = (bf16[4096,512]{1,0:T(8,128)(2,1)}, bf16[4096,512]{1,0:T(8,128)(2,1)}, bf16[4096,512]{1,0:T(8,128)(2,1)}, bf16[4096,512]{1,0:T(8,128)(2,1)}, bf1...) custom-call(s32[1,4]{1,0:T(1,128)} %len_ref.5, ...), custom_call_target="tpu_custom_call" | custom-call | flops 60129542144 | bytes 46137344 | tf_op jit(solution)/shard_map/third_pass/pallas_call | solution.py:646
  170.4 95.0 %back_pass.1 = (bf16[4096,512]{1,0:T(8,128)(2,1)}, f32[64,384]{1,0:T(8,128)}, f32[64,512]{1,0:T(8,128)}, f32[256,128]{1,0:T(8,128)}, f32[64,128]{1,0:T(8,128)}, /*index=5*/f32[2,64]{1,0:T(2,128)}, f32[1,64]{1,0:T(1,128)}) custom-call(s32[1,4]{1,0:T(1,128)} %len_ref.5, bf16[4096,1536]{1,0:T(8,128)(2,1)} %get-tuple-element.46.q_ref.k_lo.k_ref.k_hi.v_lo.v_ref.v_hi.qkv_ref, ...), custom_call_target="tpu_custom_call" | custom-call | flops 30064771072 | bytes 50331648 | tf_op jit(solution)/shard_map/back_pass/pallas_call | solution.py:1066
  265.4 0.0 copy-start.2
  265.4 0.0 copy-start.3
  265.4 0.0 copy-start.1
  265.4 0.0 copy-start
  265.4 0.0 copy-start.4
  265.4 0.0 copy-start.5
  265.4 4.6 %copy.27 = bf16[4096,512]{1,0:T(8,128)(2,1)} copy(bf16[4096,512]{1,0:T(8,128)(2,1)} %get-tuple-element.85) | data formatting | bytes 8388608
  270.0 0.0 copy-done.2
  270.0 0.6 copy.28
  270.6 0.0 copy-done.3
  270.6 0.6 copy.29
  271.3 0.0 copy-done.1
  271.3 0.7 copy.30
  271.9 0.0 copy-done
  271.9 0.7 copy.31
  272.6 0.0 copy-done.4
  272.6 0.6 copy.32
  273.1 0.0 copy-done.5
  273.1 0.5 copy.33
Async XLA Ops:
  265.4 4.6 %copy-start.2 = (f32[64,384]{1,0:T(8,128)S(1)}, f32[64,384]{1,0:T(8,128)}, u32[]{:S(2)}) copy-start(f32[64,384]{1,0:T(8,128)} %get-tuple-element.86) | copy-start | bytes 294916
  265.4 5.3 %copy-start.3 = (f32[64,128]{1,0:T(8,128)S(1)}, f32[64,128]{1,0:T(8,128)}, u32[]{:S(2)}) copy-start(f32[64,128]{1,0:T(8,128)} %get-tuple-element.87) | copy-start | bytes 98308
  265.4 5.9 %copy-start.1 = (f32[64,512]{1,0:T(8,128)S(1)}, f32[64,512]{1,0:T(8,128)}, u32[]{:S(2)}) copy-start(f32[64,512]{1,0:T(8,128)} %get-tuple-element.88) | copy-start | bytes 393220
  265.4 6.5 %copy-start = (f32[256,128]{1,0:T(8,128)S(1)}, f32[256,128]{1,0:T(8,128)}, u32[]{:S(2)}) copy-start(f32[256,128]{1,0:T(8,128)} %get-tuple-element.89) | copy-start | bytes 393220
  265.4 7.2 %copy-start.4 = (f32[2,64]{1,0:T(2,128)S(1)}, f32[2,64]{1,0:T(2,128)}, u32[]{:S(2)}) copy-start(f32[2,64]{1,0:T(2,128)} %get-tuple-element.90) | copy-start | bytes 1540
  265.4 7.7 %copy-start.5 = (f32[1,64]{1,0:T(1,128)S(1)}, f32[1,64]{1,0:T(1,128)}, u32[]{:S(2)}) copy-start(f32[1,64]{1,0:T(1,128)} %get-tuple-element.75) | copy-start | bytes 772

commit v4 on v3

--- a/solution.py
+++ b/solution.py
@@ -46,7 +46,7 @@
 
 
 def lift(t):
-    return jnp.where(t > 0, t + 1.0, jnp.exp(jnp.minimum(t, 0.0)))
+    return jnp.where(t > 0, t + 1, jnp.exp(jnp.minimum(t, 0)))
 
 
 def moments(x):
@@ -83,6 +83,10 @@
     return out
 
 
+def turned(hidden, n_fsdp):
+    return hidden // n_fsdp >= 128
+
+
 def join_blocks(ref, got, lo=0, step=None):
     n_dp, n_fsdp, r, c = got.shape
     step = c if step is None else step
@@ -91,16 +95,21 @@
             ref[f * r : (f + 1) * r, d * step + lo : d * step + lo + c] = got[d, f]
 
 
-def cut_blocks(ref, acc, lo=0, step=None, swap=False):
+def cut_blocks(ref, acc):
     n_dp, n_fsdp, r, c = ref.shape
-    step = c if step is None else step
     for d in range(n_dp):
         for f in range(n_fsdp):
-            if swap:
-                block = acc[d * r : (d + 1) * r, f * c : (f + 1) * c]
-            else:
-                block = acc[f * r : (f + 1) * r, d * step + lo : d * step + lo + c]
-            ref[d, f] = block.astype(ref.dtype)
+            ref[d, f] = acc[f * r : (f + 1) * r, d * c : (d + 1) * c].astype(ref.dtype)
+
+
+def cut_turned(ref, acc):
+    n_dp, n_fsdp, r, c = ref.shape
+    width, hidden = acc.shape
+    wide, deep = width // n_dp, hidden // n_fsdp
+    for d in range(n_dp):
+        for f in range(n_fsdp):
+            block = acc[d * wide : (d + 1) * wide, f * deep : (f + 1) * deep]
+            ref[d, f] = (block if turned(hidden, n_fsdp) else block.T).astype(ref.dtype)
 
 
 def band_table(head):
@@ -155,8 +164,8 @@
 
 
 class Gather:
-    def __init__(self, place, shard, got, send, recv, local, order):
-        self.p, self.shard, self.got, self.order = place, shard, got, order
+    def __init__(self, place, shard, got, send, recv, local, order, way=None):
+        self.p, self.shard, self.got, self.order, self.way = place, shard, got, order, way
         self.send, self.recv, self.local = send, recv, local
 
     @staticmethod
@@ -165,7 +174,11 @@
 
     def own(self):
         p = self.p
-        return pltpu.make_async_copy(self.shard, self.got.at[p.dh, p.dl, p.fh, p.fl], self.local)
+        src = self.shard if self.way is None else self.way
+        return pltpu.make_async_copy(src, self.got.at[p.dh, p.dl, p.fh, p.fl], self.local)
+
+    def fetch(self):
+        return pltpu.make_async_copy(self.shard, self.way, self.local)
 
     def stage(self, k):
         p, g = self.p, self.got
@@ -208,6 +221,7 @@
 def front_kernel(
     ways,
     plan,
+    qkv_steps,
     len_ref,
     tok_ref,
     wqkv,
@@ -224,6 +238,7 @@
     fb_ref,
     rn_ref,
     p_ref,
+    h1t_ref,
     m1_ref,
     m2_ref,
     c_ref,
@@ -240,12 +255,15 @@
     gb,
     small,
     g_small,
+    way_in,
+    way_back,
+    way_out,
     send,
     recv,
     local,
 ):
     step = pl.program_id(0)
-    steps = pl.num_programs(0) // 2
+    steps = qkv_steps
     rows, width = tok_ref.shape
     groups = width // GW
     head = width // HEADS
@@ -258,8 +276,8 @@
     half_in = win.shape[1] // 2
     half_back = wback.shape[0] // 2
 
-    def piece(j, shard, got, order):
-        return Gather(place, shard, got, send.at[j], recv.at[j], local.at[j], order)
+    def piece(j, shard, got, order, way=None):
+        return Gather(place, shard, got, send.at[j], recv.at[j], local.at[j], order, way)
 
     first = [
         piece(0, small, g_small, "x"),
@@ -269,11 +287,11 @@
     rest = []
     for i in range(2):
         cut = pl.ds(i * half_in, half_in)
-        rest.append(piece(3 + i, win.at[:, cut], g_in.at[:, :, :, :, :, cut], "x"))
+        rest.append(piece(3 + i, win.at[:, cut], g_in.at[:, :, :, :, :, cut], "x", way_in.at[:, cut]))
     for i in range(2):
         cut = pl.ds(i * half_back, half_back)
-        rest.append(piece(5 + i, wback.at[cut], g_back.at[:, :, :, :, cut], "y"))
-    rest.append(piece(7, wout, g_out, "y"))
+        rest.append(piece(5 + i, wback.at[cut], g_back.at[:, :, :, :, cut], "y", way_back.at[cut]))
+    rest.append(piece(7, wout, g_out, "y", way_out))
     sets = [[rest[0], rest[2]], [rest[1], rest[3], rest[4]]]
 
     @pl.when(step == 0)
@@ -281,14 +299,20 @@
         small[...] = jnp.zeros_like(small)
         small[:2, :cols] = vec_in[...]
         small[2:3, :cols] = bias_in[...]
-        for x in first + rest:
+        for x in first:
             x.own().start()
+        for x in rest:
+            x.fetch().start()
         greet(place)
         for x in first:
             x.start(0)
         for k in range(3):
             for x in first:
                 x.turn(k)
+            if k == 0:
+                for x in rest:
+                    x.fetch().wait()
+                    x.own().start()
             if k == 1:
                 for x in sets[0] + sets[1]:
                     x.start(0)
@@ -315,10 +339,9 @@
             vec_ref[2 * d : 2 * d + 2] = total[16 * d : 16 * d + 2]
             bin_ref[0:1, d * width : (d + 1) * width] = total[16 * d + 2 : 16 * d + 3]
 
-    for at, moves in plan.items():
-
+    def advance(at, moves):
         @pl.when(step == at)
-        def _(moves=moves):
+        def _():
             for which, k in moves:
                 for x in sets[which]:
                     if k < 3:
@@ -326,10 +349,15 @@
                     else:
                         x.wait(k)
 
+    for at, moves in plan.items():
+        if at < 2 * steps:
+            advance(at, moves)
+
     @pl.when(step < steps)
     def _():
         z, _ = moments(tok_ref[...].astype(f32))
         h = (z * vec_ref[0:1] + vec_ref[1:2]).astype(bf16)
+        h1t_ref[...] = h.T
         lo = pl.multiple_of(HALO + step * rows, HALO)
         q = nn(h, w_ref[:, :width]).astype(bf16)
         qkv_ref[:, :width] = q
@@ -344,12 +372,10 @@
             qkv_ref[:, vc] = v
             all_s[pl.ds(lo, rows), kc] = k
             all_s[pl.ds(lo, rows), vc] = v
-            kw = k.astype(f32)
-            phi = jnp.where(valid, lift(kw), 0.0)
-            bent = jnp.where(valid, jnp.tanh(kw), 0.0)
-            both = jnp.concatenate([phi.astype(bf16), bent.astype(bf16)], axis=1)
-            st_ref[g] += tn(v, both)
-            t_ref[g] += fold8(phi)
+            phi = jnp.where(valid, lift(k), 0)
+            bent = jnp.where(valid, jnp.tanh(k), 0)
+            st_ref[g] += tn(v, jnp.concatenate([phi, bent], axis=1))
+            t_ref[g] += fold8(phi.astype(f32))
 
     @pl.when(step == steps - 1)
     def _():
@@ -360,8 +386,8 @@
             tb = jnp.sum(t_ref[g], axis=0, keepdims=True) * mask
             s1 = st_ref[g][:, :GW] * mask
             s2 = st_ref[g][:, GW:] * mask
-            c_col = jnp.sum(s1, axis=1, keepdims=True) / jnp.sum(tb, axis=1, keepdims=True)
-            c_row = nt_exact(ones, s1) / nt_exact(ones, tb)
+            c_row = (nt_exact(ones, s1) / nt_exact(ones, tb)).astype(bf16).astype(f32)
+            c_col = jnp.broadcast_to(c_row[0:1], (GW, GW)).T
             m1_ref[g, :GW] = (s1 - c_col * tb).astype(bf16)
             m1_ref[g, GW:] = tb.astype(bf16)
             m2_ref[g] = (s2 * inv_len).astype(bf16)
@@ -390,12 +416,14 @@
                 near_ref[b * QB : (b + 1) * QB, cut] = pick_heads(o, head).astype(bf16)
         for g in range(groups):
             cut = slice(g * GW, (g + 1) * GW)
-            q = all_s[pl.ds(pl.multiple_of(at + HALO, HALO), rows), cut].astype(f32)
-            both = nt(lift(q).astype(bf16), m1_ref[g])
+            q = all_s[pl.ds(pl.multiple_of(at + HALO, HALO), rows), cut]
+            both = nt(lift(q), m1_ref[g])
             rn = 1.0 / both[:, GW:]
             rn_ref[:, cut] = rn.astype(bf16)
             fa_ref[:, cut] = (both[:, :GW] * rn).astype(bf16)
-            fb_ref[:, cut] = nt(jnp.tanh(q).astype(bf16), m2_ref[g]).astype(bf16)
+            fb_ref[:, cut] = nt(jnp.tanh(q), m2_ref[g]).astype(bf16)
+
+    advance(2 * steps - 1, plan[2 * steps])
 
 
 def join_pairs(ref, got, lo, step):
@@ -423,7 +451,7 @@
     pieces = 8
     per = Gather.count(n_dp, n_fsdp)
     return pl.pallas_call(
-        functools.partial(front_kernel, ways, plan),
+        functools.partial(front_kernel, ways, plan, steps),
         grid=(2 * steps,),
         in_specs=[
             pl.BlockSpec(memory_space=pltpu.SMEM),
@@ -444,6 +472,7 @@
             late,
             late,
             pl.BlockSpec((tile // QB, KW, width), lambda i: (jnp.maximum(i - steps, 0), 0, 0)),
+            pl.BlockSpec((width, tile), lambda i: (0, jnp.minimum(i, steps - 1))),
             const(groups, 2 * GW, GW),
             const(groups, GW, GW),
             const(groups, 8, GW),
@@ -458,6 +487,7 @@
         + [sds((rows, width), bf16)] * 4
         + [
             sds((rows // QB, KW, width), bf16),
+            sds((width, rows), bf16),
             sds((groups, 2 * GW, GW), bf16),
             sds((groups, GW, GW), bf16),
             sds((groups, 8, GW), f32),
@@ -476,6 +506,9 @@
             pltpu.VMEM(got(w_qkv.shape[0], w_qkv.shape[1] - part), bf16),
             pltpu.VMEM((16, 128), bf16),
             pltpu.VMEM(got(16, 128), bf16),
+            pltpu.VMEM(w_in.shape, bf16),
+            pltpu.VMEM(w_back.shape, bf16),
+            pltpu.VMEM(w_out.shape, bf16),
             pltpu.SemaphoreType.DMA((pieces, per)),
             pltpu.SemaphoreType.DMA((pieces, per)),
             pltpu.SemaphoreType.DMA((pieces,)),
@@ -616,9 +649,9 @@
     d_far = (vec_ref[7:8] * d_mix).astype(bf16)
     for g in range(groups):
         cols = slice(g * GW, (g + 1) * GW)
-        q = q_ref[:, cols].astype(f32)
-        a_st[g] += tn(lift(q).astype(bf16), jnp.concatenate([d_num[:, cols], d_den[:, cols]], axis=1))
-        a_bent[g] += tn(jnp.tanh(q).astype(bf16), d_far[:, cols])
+        q = q_ref[:, cols]
+        a_st[g] += tn(lift(q), jnp.concatenate([d_num[:, cols], d_den[:, cols]], axis=1))
+        a_bent[g] += tn(jnp.tanh(q), d_far[:, cols])
 
     @pl.when(step == pl.num_programs(0) - 1)
     def _():
@@ -630,7 +663,7 @@
             m4_ref[g] = (a_bent[g] * mask * inv_len).astype(bf16)
             dt_ref[g] = -nt_exact(ones, a_st[g][:, GW:] * mask)
         cut_blocks(gin_ref, a_in)
-        cut_blocks(gback_ref, a_back, swap=True)
+        cut_turned(gback_ref, a_back)
         cut_blocks(gout_ref, a_out)
         gvec_ref[6] += gvec_ref[0] * c_row
 
@@ -640,6 +673,8 @@
     hidden = w_in.shape[0] * w_in.shape[3]
     groups = width // GW
     n_dp, n_fsdp = ways
+    back = (width // n_dp, hidden // n_fsdp)
+    back = back if turned(hidden, n_fsdp) else back[::-1]
     const = lambda *shape: pl.BlockSpec(shape, lambda i: (0,) * len(shape))
     block = pl.BlockSpec((tile, width), lambda i: (i, 0))
     sds = jax.ShapeDtypeStruct
@@ -659,7 +694,7 @@
         out_specs=[block] * 4
         + [
             const(n_dp, n_fsdp, width // n_fsdp, hidden // n_dp),
-            const(n_dp, n_fsdp, width // n_dp, hidden // n_fsdp),
+            const(n_dp, n_fsdp, *back),
             const(n_dp, n_fsdp, width // n_fsdp, width // n_dp),
             const(8, 8, width),
             const(8, hidden),
@@ -670,7 +705,7 @@
         out_shape=[sds((rows, width), bf16)] * 4
         + [
             sds((n_dp, n_fsdp, width // n_fsdp, hidden // n_dp), bf16),
-            sds((n_dp, n_fsdp, width // n_dp, hidden // n_fsdp), bf16),
+            sds((n_dp, n_fsdp, *back), bf16),
             sds((n_dp, n_fsdp, width // n_fsdp, width // n_dp), bf16),
             sds((8, 8, width), f32),
             sds((8, hidden), f32),
@@ -800,6 +835,7 @@
 def back_kernel(
     ways,
     plan,
+    late_plan,
     len_ref,
     q_ref,
     k_lo,
@@ -810,12 +846,11 @@
     v_hi,
     p_ref,
     dmix_ref,
-    qkv_ref,
+    dn_ref,
+    fa_ref,
     tok_ref,
     datt_ref,
-    dn_ref,
-    fa_ref,
-    dmp_ref,
+    h1t_ref,
     m1_ref,
     m2_ref,
     m3_ref,
@@ -839,137 +874,195 @@
     obias_ref,
     kk,
     vv,
-    dq_s,
-    dk_s,
-    dv_s,
-    a_qkv,
-    gvec_ref,
+    far_s,
+    dp_s,
+    ds_s,
+    all_d,
+    carry,
+    gvec_s,
     ga_ref,
     gb_ref,
     gs_ref,
     rows_s,
     back_t,
     small_o,
+    late_src,
+    late_got,
     *rest,
 ):
     step = pl.program_id(0)
-    steps = pl.num_programs(0) - 1
     rows, width = q_ref.shape
+    total = h1t_ref.shape[1]
+    steps = total // rows
     groups = width // GW
     head = width // HEADS
     scale = head ** (-0.5)
     length = len_ref[0, 0]
-    place = Place(*ways)
     n_dp, n_fsdp = ways
+    place = Place(n_dp, n_fsdp)
     cols = ovec_ref.shape[1]
+    c_all = oqkv_ref.shape[1]
     part = ga_ref.shape[-1]
-    send, recv, local = rest[30:]
+    send, recv, local, late_send, late_recv = rest[30:]
+    final = steps + 1 + place.nh
+    last_rows = tok_ref.shape[0]
 
     def piece(j, src, out, order):
         return Scatter(place, src, out, rest[5 * j : 5 * j + 5], send.at[j], recv.at[j], local.at[j], order)
 
-    ffn = [
+    early = [
         piece(0, s_in, oin_ref, "x"),
         piece(1, s_back, back_t, "y"),
         piece(2, s_out, oout_ref, "y"),
+        piece(5, gs_ref, small_o, "x"),
     ]
     last = [
         piece(3, ga_ref, oqkv_ref.at[:, pl.ds(0, part)], "x"),
-        piece(4, gb_ref, oqkv_ref.at[:, pl.ds(part, oqkv_ref.shape[1] - part)], "y"),
-        piece(5, gs_ref, small_o, "x"),
+        piece(4, gb_ref, oqkv_ref.at[:, pl.ds(part, c_all - part)], "y"),
     ]
 
     @pl.when(step == 0)
     def _():
-        dk_s[: 2 * HALO] = jnp.zeros((2 * HALO, width), f32)
-        dv_s[: 2 * HALO] = jnp.zeros((2 * HALO, width), f32)
-        a_qkv[...] = jnp.zeros_like(a_qkv)
-        gvec_ref[...] = jnp.zeros_like(gvec_ref)
-        for x in ffn:
+        for x in early[:3]:
             x.own().start()
-        greet(place)
-        for x in ffn:
+        greet_all(place)
+        for x in early[:3]:
             x.start(0)
+        carry[...] = jnp.zeros_like(carry)
+        gvec_s[...] = jnp.zeros_like(gvec_s)
+        gs_ref[...] = jnp.zeros_like(gs_ref)
+        late_src[...] = jnp.zeros_like(late_src)
+        rows_s[0:2] = jnp.zeros((2, width), f32)
+        rows_s[2:8] = jnp.sum(gv_ref[2:8], axis=1)
+        bias = jnp.sum(gbias_ref[...], axis=0, keepdims=True)
+        for d in range(n_dp):
+            pair = rows_s[2 * d : 2 * d + 2]
+            for f in range(n_fsdp):
+                spot = slice(f * cols, (f + 1) * cols)
+                at = d * width + f * cols
+                gs_ref[d // 2, d % 2, f // 2, f % 2, 0:2, :cols] = pair[:, spot]
+                gs_ref[d // 2, d % 2, f // 2, f % 2, 2:3, :cols] = bias[:, at : at + cols]
+        early[3].own().start()
+        early[3].start(0)
 
     for at, moves in plan.items():
 
         @pl.when(step == at)
         def _(moves=moves):
             for k in moves:
-                for x in ffn:
+                for x in early:
                     x.turn(k)
+
+    def far_keys(at, slot, live):
+        valid = row_valid(at, rows, GW, length) & live
+        here = pl.ds(pl.multiple_of(at * rows + HALO, HALO), rows)
+        for g in range(groups):
+            cut = slice(g * GW, (g + 1) * GW)
+            kc = slice(width + g * GW, width + (g + 1) * GW)
+            vc = slice(2 * width + g * GW, 2 * width + (g + 1) * GW)
+            k = kk[slot, HALO : HALO + rows, cut]
+            v = vv[slot, HALO : HALO + rows, cut]
+            lift_k = lift(k)
+            bent_k = jnp.tanh(k)
+            bent = bent_k.astype(f32)
+            v_cen = v - c_ref[g, 0:1].astype(bf16)
+            dk = (nt(v_cen, m3_ref[g]) + dt_ref[g, 0:1]) * jnp.minimum(lift_k, 1.0).astype(f32)
+            dk += nt(v, m4_ref[g]) * (1.0 - bent * bent)
+            both = jnp.concatenate([lift_k, bent_k], axis=1)
+            dv = nn(both, jnp.concatenate([m3_ref[g], m4_ref[g]], axis=0))
+            all_d[here, kc] = (all_d[here, kc].astype(f32) + jnp.where(valid, dk, 0.0)).astype(bf16)
+            all_d[here, vc] = (all_d[here, vc].astype(f32) + jnp.where(valid, dv, 0.0)).astype(bf16)
 
     @pl.when(step < steps)
     def _():
-        kk[:HALO] = k_lo[...]
-        kk[HALO : HALO + rows] = k_ref[...]
-        kk[HALO + rows :] = k_hi[...]
-        vv[:HALO] = v_lo[...]
-        vv[HALO : HALO + rows] = v_ref[...]
-        vv[HALO + rows :] = v_hi[...]
+        slot = lax.rem(step, 2)
+        kk[slot, :HALO] = k_lo[...]
+        kk[slot, HALO : HALO + rows] = k_ref[...]
+        kk[slot, HALO + rows :] = k_hi[...]
+        vv[slot, :HALO] = v_lo[...]
+        vv[slot, HALO : HALO + rows] = v_ref[...]
+        vv[slot, HALO + rows :] = v_hi[...]
         hm = hm_ref[...]
-        slot = lax.rem(step, 2)
+        blend = vec_ref[...].astype(bf16)
+        base = step * rows
         for g in range(groups):
             cut = slice(g * GW, (g + 1) * GW)
+            kc = slice(width + g * GW, width + (g + 1) * GW)
+            vc = slice(2 * width + g * GW, 2 * width + (g + 1) * GW)
+            q = q_ref[:, cut]
+            d_num = dn_ref[:, cut]
+            d_den = -d_num * fa_ref[:, cut]
+            d_mix = dmix_ref[:, cut]
+            bent = jnp.tanh(q).astype(f32)
+            far = nn(jnp.concatenate([d_num, d_den], axis=1), m1_ref[g]) * jnp.minimum(lift(q), 1.0).astype(f32)
+            far_s[:, cut] = far + nn(blend[7:8, cut] * d_mix, m2_ref[g]) * (1.0 - bent * bent)
             for b in range(rows // QB):
                 here = slice(b * QB, (b + 1) * QB)
                 window = slice(b * QB, b * QB + KW)
-                qs = spread_rows(q_ref[here, cut] * scale, hm)
-                d_near = (vec_ref[5:6, cut] * dmix_ref[here, cut].astype(f32)).astype(bf16)
-                ds = spread_rows(d_near, hm)
-                p = p_ref[b, :, cut]
-                pw = p.astype(f32)
-                t = pw * nt(vv[window, cut], ds)
-                d_s = (t - pw * jnp.sum(t, axis=0, keepdims=True)).astype(bf16)
-                dk = nn(d_s, qs)
-                dv = nn(p, ds)
-                dq_s[slot, here, cut] = pick_heads(tn(d_s, kk[window, cut]), head) * scale
-                lo = pl.ds(pl.multiple_of(lax.rem(step * rows + b * QB, 3 * rows), QB), QB)
-                hi = pl.ds(pl.multiple_of(lax.rem(step * rows + (b + 1) * QB, 3 * rows), QB), QB)
-                dk_s[lo, cut] += dk[:QB]
-                dk_s[hi, cut] = dk[QB:]
-                dv_s[lo, cut] += dv[:QB]
-                dv_s[hi, cut] = dv[QB:]
-
-    @pl.when(step > 0)
+                ds = spread_rows(blend[5:6, cut] * dmix_ref[here, cut], hm)
+                dp_s[g, b] = nt(vv[slot, window, cut], ds)
+            for b in range(rows // QB):
+                pw = p_ref[b, :, cut].astype(f32)
+                t = pw * dp_s[g, b]
+                ds_s[g, b] = (t - pw * jnp.sum(t, axis=0, keepdims=True)).astype(bf16)
+            old_k = carry[0, :, cut]
+            old_v = carry[1, :, cut]
+            for b in range(rows // QB):
+                here = slice(b * QB, (b + 1) * QB)
+                window = slice(b * QB, b * QB + KW)
+                d_s = ds_s[g, b]
+                dk = nn(d_s, spread_rows(q_ref[here, cut] * scale, hm))
+                dv = nn(p_ref[b, :, cut], spread_rows(blend[5:6, cut] * dmix_ref[here, cut], hm))
+                dq = pick_heads(tn(d_s, kk[slot, window, cut]), head) * scale + far_s[here, cut]
+                lo = pl.ds(pl.multiple_of(base + b * QB, QB), QB)
+                all_d[pl.ds(pl.multiple_of(base + b * QB + HALO, HALO), QB), cut] = dq.astype(bf16)
+                all_d[lo, kc] = (old_k + dk[:QB]).astype(bf16)
+                all_d[lo, vc] = (old_v + dv[:QB]).astype(bf16)
+                old_k = dk[QB:]
+                old_v = dv[QB:]
+            carry[0, :, cut] = old_k
+            carry[1, :, cut] = old_v
+        far_keys(jnp.maximum(step - 1, 0), 1 - slot, step > 0)
+
+    @pl.when(step == steps)
     def _():
-        slot = lax.rem(step + 1, 2)
+        all_d[total:, width : 2 * width] = carry[0].astype(bf16)
+        all_d[total:, 2 * width :] = carry[1].astype(bf16)
+        far_keys(steps - 1, (steps - 1) % 2, True)
+
+    for dh in range(n_dp // 2):
+
+        @pl.when(step == steps + 1 + dh)
+        def _(dh=dh):
+            grad = nn(h1t_ref[...], all_d[HALO : HALO + total, dh * 2 * c_all : (dh + 1) * 2 * c_all])
+            r = ga_ref.shape[-2]
+            for dl in range(2):
+                for f in range(n_fsdp):
+                    block = grad[f * r : (f + 1) * r, dl * c_all : (dl + 1) * c_all].astype(bf16)
+                    ga_ref[dh, dl, f // 2, f % 2] = block[:, :part]
+                    gb_ref[dh, dl, f // 2, f % 2] = block[:, part:]
+
+    @pl.when(step == final)
+    def _():
+        for x in last:
+            x.own().start()
+            x.start(0)
+
+    for at, moves in late_plan.items():
+
+        @pl.when(step == final + at)
+        def _(moves=moves):
+            for k in moves:
+                for x in last:
+                    x.turn(k)
+
+    @pl.when(step >= final)
+    def _():
+        here = pl.ds(pl.multiple_of((step - final) * last_rows + HALO, HALO), last_rows)
         z1, r1 = moments(tok_ref[...].astype(f32))
-        h1 = (z1 * vec_ref[0:1] + vec_ref[1:2]).astype(bf16)
-        valid = row_valid(step - 1, rows, GW, length)
-        lo = pl.ds(pl.multiple_of(lax.rem((step - 1) * rows, 3 * rows) + HALO, HALO), rows - HALO)
-        hi = pl.ds(pl.multiple_of(lax.rem(step * rows, 3 * rows), HALO), HALO)
-        dqs, dks, dvs = [], [], []
-        for g in range(groups):
-            cut = slice(g * GW, (g + 1) * GW)
-            q = qkv_ref[:, g * GW : (g + 1) * GW].astype(f32)
-            k = qkv_ref[:, width + g * GW : width + (g + 1) * GW].astype(f32)
-            v = qkv_ref[:, 2 * width + g * GW : 2 * width + (g + 1) * GW]
-            d_num = dn_ref[:, cut]
-            d_den = (d_num.astype(f32) * -fa_ref[:, cut].astype(f32)).astype(bf16)
-            d_far = (vec_ref[7:8, cut] * dmp_ref[:, cut].astype(f32)).astype(bf16)
-            bent_q = jnp.tanh(q)
-            dq = (
-                dq_s[slot, :, cut]
-                + nn(jnp.concatenate([d_num, d_den], axis=1), m1_ref[g]) * jnp.minimum(lift(q), 1.0)
-                + nn(d_far, m2_ref[g]) * (1.0 - bent_q * bent_q)
-            )
-            lift_k = lift(k)
-            bent_k = jnp.tanh(k)
-            v_cen = (v.astype(f32) - c_ref[g, 0:1]).astype(bf16)
-            dk = (nt(v_cen, m3_ref[g]) + dt_ref[g, 0:1]) * jnp.minimum(lift_k, 1.0) + nt(
-                v, m4_ref[g]
-            ) * (1.0 - bent_k * bent_k)
-            both = jnp.concatenate([lift_k.astype(bf16), bent_k.astype(bf16)], axis=1)
-            dv = nn(both, jnp.concatenate([m3_ref[g], m4_ref[g]], axis=0))
-            dqs.append(dq.astype(bf16))
-            dks.append((jnp.concatenate([dk_s[lo, cut], dk_s[hi, cut]], axis=0) + jnp.where(valid, dk, 0.0)).astype(bf16))
-            dvs.append((jnp.concatenate([dv_s[lo, cut], dv_s[hi, cut]], axis=0) + jnp.where(valid, dv, 0.0)).astype(bf16))
-        d_qkv = jnp.concatenate(dqs + dks + dvs, axis=1)
-        a_qkv[...] += tn(h1, d_qkv)
-        dh1 = nt(d_qkv, w_ref[...])
-        gvec_ref[0] += fold8(dh1 * z1)
-        gvec_ref[1] += fold8(dh1)
+        dh1 = nt(all_d[here], w_ref[...])
+        gvec_s[0] += fold8(dh1 * z1)
+        gvec_s[1] += fold8(dh1)
         dz = dh1 * vec_ref[0:1]
         dtok_ref[...] = (
             datt_ref[...].astype(f32)
@@ -981,56 +1074,120 @@
             )
         ).astype(bf16)
 
-    @pl.when(step == steps)
+    @pl.when(step == final + total // last_rows - 1)
     def _():
-        oback_ref[...] = back_t[...].T
-        step_cols = oqkv_ref.shape[1]
-        cut_pairs(ga_ref, a_qkv, 0, step_cols)
-        cut_pairs(gb_ref, a_qkv, part, step_cols)
-        gs_ref[...] = jnp.zeros_like(gs_ref)
-        rows_s[0:2] = jnp.sum(gvec_ref[...], axis=1)
-        rows_s[2:8] = jnp.sum(gv_ref[2:8], axis=1)
-        bias = jnp.sum(gbias_ref[...], axis=0, keepdims=True)
-        for d in range(n_dp):
-            pair = rows_s[2 * d : 2 * d + 2]
-            for f in range(n_fsdp):
-                spot = slice(f * cols, (f + 1) * cols)
-                gs_ref[d // 2, d % 2, f // 2, f % 2, 0:2, :cols] = pair[:, spot]
-                gs_ref[d // 2, d % 2, f // 2, f % 2, 2:3, :cols] = bias[:, d * width + f * cols : d * width + (f + 1) * cols]
+        rows_s[0:2] = jnp.sum(gvec_s[...], axis=1)
+        for f in range(n_fsdp):
+            late_src[f, 0:2, :cols] = rows_s[0:2, f * cols : (f + 1) * cols]
+        d, f = lax.axis_index("dp"), lax.axis_index("fsdp")
+        me = d * n_fsdp + f
+
+        def late(o):
+            to = lax.rem(f + o, n_fsdp)
+            return copy_to(
+                late_src.at[to], late_got.at[me], late_send.at[o], late_recv.at[me], {"dp": 0, "fsdp": to}
+            )
+
+        @pl.when(d > 0)
+        def _():
+            late(0).start()
+
+        for o in range(1, n_fsdp):
+            late(o).start()
+        oback_ref[...] = back_t[...].T if turned(gbias_ref.shape[1], n_fsdp) else back_t[...]
         for x in last:
-            x.own().start()
-            x.start(0)
-        for k in range(4):
-            for x in last:
-                x.turn(k)
-        ovec_ref[...] = small_o[0:2, :cols]
+            x.turn(3)
+
+        @pl.when(d > 0)
+        def _():
+            late(0).wait_send()
+            ovec_ref[...] = small_o[0:2, :cols]
+
+        for o in range(1, n_fsdp):
+            late(o).wait_send()
+
+        @pl.when(d == 0)
+        def _():
+            late_got[me] = late_src[f]
+
+            @pl.loop(0, n_dp * n_fsdp)
+            def _(s):
+                @pl.when(s != me)
+                def _():
+                    copy_to(
+                        late_src.at[0], late_got.at[s], late_send.at[0], late_recv.at[s], {"dp": 0, "fsdp": 0}
+                    ).wait_recv()
+
+            ovec_ref[...] = jnp.sum(late_got[...], axis=0)[0:2, :cols]
+
         obias_ref[...] = small_o[2:3, :cols]
 
 
-def cut_pairs(ref, acc, lo, step):
-    nh, _, m, _, r, c = ref.shape
-    for d in range(2 * nh):
-        for f in range(2 * m):
-            block = acc[f * r : (f + 1) * r, d * step + lo : d * step + lo + c]
-            ref[d // 2, d % 2, f // 2, f % 2] = block.astype(ref.dtype)
+def greet_all(place):
+    d, f = lax.axis_index("dp"), lax.axis_index("fsdp")
+    n_dp, n_fsdp = 2 * place.nh, 2 * place.m
+    barrier = pltpu.get_barrier_semaphore()
+    who = place.partners()
+    for dev in who:
+        pl.semaphore_signal(barrier, inc=1, device_id=dev, device_id_type=MESH)
+
+    @pl.when(d == 0)
+    def _():
+        @pl.loop(0, n_dp)
+        def _(i):
+            @pl.loop(0, n_fsdp)
+            def _(j):
+                @pl.when((i != 0) | (j != f))
+                def _():
+                    pl.semaphore_signal(barrier, inc=1, device_id={"dp": i, "fsdp": j}, device_id_type=MESH)
+
+    pl.semaphore_wait(barrier, len(who) + n_fsdp - (d == 0).astype(jnp.int32))
 
 
 def back_pass(
-    ways, length, qkv, p, d_mix, tokens, d_attn, d_num, fa, m1, m2, m3, m4, dt, c, vecs, w_qkv, gv, gbias, s_in, s_back, s_out, tile, plan
+    ways,
+    length,
+    qkv,
+    p,
+    d_mix,
+    tokens,
+    d_attn,
+    d_num,
+    fa,
+    h1t,
+    m1,
+    m2,
+    m3,
+    m4,
+    dt,
+    c,
+    vecs,
+    w_qkv,
+    gv,
+    gbias,
+    s_in,
+    s_back,
+    s_out,
+    tile,
+    last_tile,
+    plan,
+    late_plan,
 ):
     rows, width = tokens.shape
     groups = width // GW
     steps = rows // tile
     n_dp, n_fsdp = ways
+    nh, m = n_dp // 2, n_fsdp // 2
     r, c_all = width // n_fsdp, 3 * width // n_dp
     part = first_part(c_all)
-    nh, m = n_dp // 2, n_fsdp // 2
+    per = Scatter.count(n_dp, n_fsdp)
+    final = steps + 1 + nh
     hbm = pl.BlockSpec(memory_space=pl.ANY)
     back_shape = s_back.shape[-2:]
     outs = [
         (r, c_all),
         s_in.shape[-2:],
-        back_shape[::-1],
+        back_shape[::-1] if turned(gbias.shape[1], n_fsdp) else back_shape,
         s_out.shape[-2:],
         (2, width // n_fsdp),
         (1, gbias.shape[1] // (n_dp * n_fsdp)),
@@ -1044,49 +1201,53 @@
         (8, 128, "x", f32),
     ]
     bufs = [b for k in kinds for b in Scatter.scratch(n_dp, n_fsdp, *k)]
-    per = Scatter.count(n_dp, n_fsdp)
     got = lambda *s: (nh, 2, m, 2, *s)
-    const = lambda *shape: pl.BlockSpec(shape, lambda i: (0,) * len(shape))
-    now = lambda i: jnp.minimum(i, steps - 1)
-    old = lambda i: jnp.maximum(i - 1, 0)
-    per = tile // HALO
-    last = rows // HALO - 1
+
+    def const(*shape):
+        return pl.BlockSpec(shape, lambda i: (0,) * len(shape))
+
+    def kept(*shape):
+        return pl.BlockSpec(shape, lambda i: (0,) * len(shape), pipeline_mode=pl.Buffered(1))
+
+    one = lambda i: jnp.minimum(i, steps - 1)
+    end = lambda i: jnp.maximum(i - final, 0)
+    per_tile = tile // HALO
+    top = rows // HALO - 1
 
     def halo(col):
         return [
-            pl.BlockSpec((HALO, width), lambda i: (jnp.maximum(now(i) * per - 1, 0), col)),
-            pl.BlockSpec((tile, width), lambda i: (now(i), col)),
-            pl.BlockSpec((HALO, width), lambda i: (jnp.minimum((now(i) + 1) * per, last), col)),
+            pl.BlockSpec((HALO, width), lambda i: (jnp.maximum(one(i) * per_tile - 1, 0), col)),
+            pl.BlockSpec((tile, width), lambda i: (one(i), col)),
+            pl.BlockSpec((HALO, width), lambda i: (jnp.minimum((one(i) + 1) * per_tile, top), col)),
         ]
 
-    block = pl.BlockSpec((tile, width), lambda i: (now(i), 0))
-    late = pl.BlockSpec((tile, width), lambda i: (old(i), 0))
+    block = pl.BlockSpec((tile, width), lambda i: (one(i), 0))
+    late = pl.BlockSpec((last_tile, width), lambda i: (end(i), 0))
     head = width // HEADS
     sds = jax.ShapeDtypeStruct
     return pl.pallas_call(
-        functools.partial(back_kernel, ways, plan),
-        grid=(steps + 1,),
+        functools.partial(back_kernel, ways, plan, late_plan),
+        grid=(final + rows // last_tile,),
         in_specs=[
             pl.BlockSpec(memory_space=pltpu.SMEM),
             block,
             *halo(1),
             *halo(2),
-            pl.BlockSpec((tile // QB, KW, width), lambda i: (now(i), 0, 0)),
+            pl.BlockSpec((tile // QB, KW, width), lambda i: (one(i), 0, 0)),
             block,
-            pl.BlockSpec((tile, 3 * width), lambda i: (old(i), 0)),
+            block,
+            block,
             late,
             late,
-            late,
-            late,
-            late,
-            const(groups, 2 * GW, GW),
-            const(groups, GW, GW),
-            const(groups, GW, GW),
-            const(groups, GW, GW),
+            kept(width, rows),
+            kept(groups, 2 * GW, GW),
+            kept(groups, GW, GW),
+            kept(groups, GW, GW),
+            kept(groups, GW, GW),
             const(groups, 8, GW),
             const(groups, 8, GW),
             const(8, width),
-            const(width, 3 * width),
+            kept(width, 3 * width),
             const(GW, GW),
             const(*gv.shape),
             const(*gbias.shape),
@@ -1097,12 +1258,13 @@
         out_specs=[late] + [const(*s) for s in outs],
         out_shape=[sds((rows, width), bf16)] + [sds(s, f32) for s in outs],
         scratch_shapes=[
-            pltpu.VMEM((tile + 2 * HALO, width), bf16),
-            pltpu.VMEM((tile + 2 * HALO, width), bf16),
-            pltpu.VMEM((2, tile, width), f32),
-            pltpu.VMEM((3 * tile, width), f32),
-            pltpu.VMEM((3 * tile, width), f32),
-            pltpu.VMEM((width, 3 * width), f32),
+            pltpu.VMEM((2, tile + 2 * HALO, width), bf16),
+            pltpu.VMEM((2, tile + 2 * HALO, width), bf16),
+            pltpu.VMEM((tile, width), f32),
+            pltpu.VMEM((groups, tile // QB, KW, GW), f32),
+            pltpu.VMEM((groups, tile // QB, KW, GW), bf16),
+            pltpu.VMEM((rows + 2 * HALO, 3 * width), bf16),
+            pltpu.VMEM((2, QB, width), f32),
             pltpu.VMEM((2, 8, width), f32),
             pltpu.VMEM(got(r, part), bf16),
             pltpu.VMEM(got(r, c_all - part), bf16),
@@ -1110,10 +1272,14 @@
             pltpu.VMEM((8, width), f32),
             pltpu.VMEM(back_shape, f32),
             pltpu.VMEM((8, 128), f32),
+            pltpu.VMEM((n_fsdp, 8, 128), f32),
+            pltpu.VMEM((n_dp * n_fsdp, 8, 128), f32),
             *bufs,
             pltpu.SemaphoreType.DMA((6, per)),
             pltpu.SemaphoreType.DMA((6, per)),
             pltpu.SemaphoreType.DMA((6,)),
+            pltpu.SemaphoreType.DMA((n_fsdp,)),
+            pltpu.SemaphoreType.DMA((n_dp * n_fsdp,)),
         ],
         compiler_params=pltpu.CompilerParams(
             collective_id=1, has_side_effects=True, vmem_limit_bytes=VMEM_LIMIT
@@ -1133,12 +1299,11 @@
         qkv,
         p,
         d_mix,
-        qkv,
+        d_num,
+        fa,
         tokens,
         d_attn,
-        d_num,
-        fa,
-        d_mix,
+        h1t,
         m1,
         m2,
         m3,
@@ -1156,10 +1321,32 @@
     )
 
 
+def hand_kernel(n, *refs):
+    for j in range(n):
+        refs[n + j][...] = refs[j][...]
+
+
+def hand_over(arrays, parts):
+    first = arrays[0]
+    block = pl.BlockSpec((first.shape[0] // parts, first.shape[1]), lambda i: (i, 0))
+    specs = [block] + [pl.BlockSpec(a.shape, lambda i: (0, 0)) for a in arrays[1:]]
+    return pl.pallas_call(
+        functools.partial(hand_kernel, len(arrays)),
+        grid=(parts,),
+        in_specs=specs,
+        out_specs=specs,
+        out_shape=[jax.ShapeDtypeStruct(a.shape, a.dtype) for a in arrays],
+        name="hand_over",
+    )(*arrays)
+
+
+FRONT_TILE = 1024
 TILE = 512
+LAST_TILE = 1024
 CHUNK = 512
-FRONT_PLAN = {2: [(0, 0)], 4: [(0, 1), (1, 0)], 6: [(0, 2)], 7: [(1, 1)], 10: [(0, 3), (1, 2)], 13: [(1, 3)]}
-BACK_PLAN = {2: [0], 4: [1], 5: [2], 7: [3]}
+FRONT_PLAN = {2: [(0, 0), (1, 0)], 3: [(0, 1), (1, 1)], 6: [(0, 2), (1, 2)], 8: [(0, 3), (1, 3)]}
+BACK_PLAN = {4: [0], 7: [1], 9: [2], 10: [3]}
+LATE_PLAN = {1: [0], 2: [1], 3: [2]}
 
 
 def shards(
@@ -1173,6 +1360,7 @@
         fb,
         rn,
         p,
+        h1t,
         m1,
         m2,
         c,
@@ -1183,7 +1371,7 @@
         g_back,
         g_out,
     ) = front_pass(
-        ways, item_lengths, tokens, w_qkv, w_in, w_back, w_out, vec_params, b_in[None], TILE, FRONT_PLAN
+        ways, item_lengths, tokens, w_qkv, w_in, w_back, w_out, vec_params, b_in[None], FRONT_TILE, FRONT_PLAN
     )
 
     def blocks(g):
@@ -1221,6 +1409,7 @@
         d_attn,
         d_num,
         fa,
+        h1t,
         m1,
         m2,
         m3,
@@ -1235,7 +1424,12 @@
         pairs(s_back),
         pairs(s_out),
         TILE,
+        LAST_TILE,
         BACK_PLAN,
+        LATE_PLAN,
+    )
+    d_tok, r_qkv, r_out, r_in, r_back, r_vec, r_bias = hand_over(
+        [d_tok, r_qkv, r_out, r_in, r_back, r_vec, r_bias], 4
     )
     return (out, d_tok, r_qkv, r_out, r_in, r_back, r_vec, r_bias[0])
 

time: 274 us -> 258 us (0.942)
  Pallas kernels: 265 us -> 256 us
  local copies, waits for them, and re-layouts: 8.22 us -> 0 us
    unnamed x19 -> x0, local copies, waits for them, and re-layouts: 8.22 us -> none
    pallas_call x2 -> x3, Pallas kernels: 169 us -> 162 us  [the longest x1 89.4 us: back_pass(): pl.pallas_call(functools.partial(back_kernel, ways, plan, late_plan), gri...]
where the time goes in v4:
time: 258 us; the launch traced here: 257 us
  Pallas kernels  256 us (99%)
    pallas_call x1, Pallas kernels, third_pass(): pl.pallas_call(functools.partial(ffn_kernel, chunk), grid=(rows // tile,)...  94.5 us
    pallas_call x1, Pallas kernels, back_pass(): pl.pallas_call(functools.partial(back_kernel, ways, plan, late_plan), gri...  89.4 us
    pallas_call x1, Pallas kernels, front_pass(): pl.pallas_call(functools.partial(front_kernel, ways, plan, steps), grid=(...  67.6 us

profile of v4, /device:TPU:0, one launch (start us, length us, event | category | flops | bytes accessed | tf_op | source)
XLA Modules:
  0.0 257.3 jit_solution(107368447782961751)
XLA Ops:
  0.6 67.6 %front_pass.1 = (bf16[4096,1536]{1,0:T(8,128)(2,1)}, bf16[4096,512]{1,0:T(8,128)(2,1)}, bf16[4096,512]{1,0:T(8,128)(2,1)}, bf16[4096,512]{1,0:T(8,128)(2,1)}, bf...) custom-call(s32[1,4]{1,0:T(1,128)} %len_ref.5, ...), custom_call_target="tpu_custom_call" | custom-call | flops 17179869184 | bytes 50331648 | tf_op jit(solution)/shard_map/front_pass/pallas_call | solution.py:453
  68.2 94.5 %third_pass.1 = (bf16[4096,512]{1,0:T(8,128)(2,1)}, bf16[4096,512]{1,0:T(8,128)(2,1)}, bf16[4096,512]{1,0:T(8,128)(2,1)}, bf16[4096,512]{1,0:T(8,128)(2,1)}, bf1...) custom-call(s32[1,4]{1,0:T(1,128)} %len_ref.5, ...), custom_call_target="tpu_custom_call" | custom-call | flops 60129542144 | bytes 46137344 | tf_op jit(solution)/shard_map/third_pass/pallas_call | solution.py:681
  162.8 89.4 %back_pass.1 = (bf16[4096,512]{1,0:T(8,128)(2,1)}, f32[64,384]{1,0:T(8,128)}, f32[64,512]{1,0:T(8,128)}, f32[256,128]{1,0:T(8,128)}, f32[64,128]{1,0:T(8,128)}, /*index=5*/f32[2,64]{1,0:T(2,128)}, f32[1,64]{1,0:T(1,128)}) custom-call(s32[1,4]{1,0:T(1,128)} %len_ref.5, bf16[4096,1536]{1,0:T(8,128)(2,1)} %get-tuple-element.54.q_ref.k_lo.k_ref.k_hi.v_lo.v_ref.v_hi, ...), custom_call_target="tpu_custom_call" | custom-call | flops 30064771072 | bytes 50331648 | tf_op jit(solution)/shard_map/back_pass/pallas_call | solution.py:1228
  252.1 5.0 %hand_over.1 = (bf16[4096,512]{1,0:T(8,128)(2,1)}, f32[64,384]{1,0:T(8,128)}, f32[64,128]{1,0:T(8,128)}, f32[64,512]{1,0:T(8,128)}, f32[256,128]{1,0:T(8,128)}, /*index=5*/f32[2,64]{1,0:T(2,128)}, f32[1,64]{1,0:T(1,128)}) custom-call(bf16[4096,512]{1,0:T(8,128)(2,1)} %get-tuple-element.78.refs_0_, f32[64,384]{1,0:T(8,128)} %get-tuple-element.79.refs_1_, ...), custom_call_target="tpu_custom_call" | custom-call | tf_op jit(solution)/shard_map/hand_over/pallas_call | solution.py:1333

commit v5 on v4

--- a/solution.py
+++ b/solution.py
@@ -41,10 +41,6 @@
     )
 
 
-def first_part(cols):
-    return 128 * ((cols // 128 + 1) // 2) if cols >= 256 else cols // 2
-
-
 def lift(t):
     return jnp.where(t > 0, t + 1, jnp.exp(jnp.minimum(t, 0)))
 
@@ -58,6 +54,11 @@
 
 def fold8(x):
     return jnp.sum(x.reshape(x.shape[0] // 8, 8, x.shape[1]), axis=0)
+
+
+def fold4(x):
+    n = x.shape[0] // 4
+    return (x[:n] + x[n : 2 * n]) + (x[2 * n : 3 * n] + x[3 * n :])
 
 
 def row_valid(step, rows, width, length):
@@ -251,8 +252,7 @@
     all_s,
     st_ref,
     t_ref,
-    ga,
-    gb,
+    g_qkv,
     small,
     g_small,
     way_in,
@@ -272,26 +272,23 @@
     n_dp, n_fsdp = ways
     cols = vec_in.shape[1]
     place = Place(n_dp, n_fsdp)
-    part = ga.shape[-1]
     half_in = win.shape[1] // 2
     half_back = wback.shape[0] // 2
 
     def piece(j, shard, got, order, way=None):
         return Gather(place, shard, got, send.at[j], recv.at[j], local.at[j], order, way)
 
-    first = [
-        piece(0, small, g_small, "x"),
-        piece(1, wqkv.at[:, pl.ds(0, part)], ga, "x"),
-        piece(2, wqkv.at[:, pl.ds(part, wqkv.shape[1] - part)], gb, "y"),
-    ]
+    first = [[piece(7, small, g_small, "x")], []]
+    for i, (which, cut, order) in enumerate(qkv_parts(*wqkv.shape)):
+        first[which].append(piece(8 + i, wqkv.at[cut], g_qkv.at[(slice(None),) * 4 + cut], order))
     rest = []
     for i in range(2):
         cut = pl.ds(i * half_in, half_in)
-        rest.append(piece(3 + i, win.at[:, cut], g_in.at[:, :, :, :, :, cut], "x", way_in.at[:, cut]))
+        rest.append(piece(i, win.at[:, cut], g_in.at[:, :, :, :, :, cut], "x", way_in.at[:, cut]))
     for i in range(2):
         cut = pl.ds(i * half_back, half_back)
-        rest.append(piece(5 + i, wback.at[cut], g_back.at[:, :, :, :, cut], "y", way_back.at[cut]))
-    rest.append(piece(7, wout, g_out, "y", way_out))
+        rest.append(piece(2 + i, wback.at[cut], g_back.at[:, :, :, :, cut], "y", way_back.at[cut]))
+    rest.append(piece(4, wout, g_out, "y", way_out))
     sets = [[rest[0], rest[2]], [rest[1], rest[3], rest[4]]]
 
     @pl.when(step == 0)
@@ -299,31 +296,30 @@
         small[...] = jnp.zeros_like(small)
         small[:2, :cols] = vec_in[...]
         small[2:3, :cols] = bias_in[...]
-        for x in first:
+        for x in first[0] + first[1]:
             x.own().start()
         for x in rest:
             x.fetch().start()
         greet(place)
-        for x in first:
+        for x in first[0] + first[1]:
             x.start(0)
+        for x in rest:
+            x.fetch().wait()
+            x.own().start()
         for k in range(3):
-            for x in first:
-                x.turn(k)
+            for group in first:
+                for x in group:
+                    x.turn(k)
             if k == 0:
-                for x in rest:
-                    x.fetch().wait()
-                    x.own().start()
-            if k == 1:
                 for x in sets[0] + sets[1]:
                     x.start(0)
         st_ref[...] = jnp.zeros_like(st_ref)
         t_ref[...] = jnp.zeros_like(t_ref)
         all_s[:HALO] = jnp.zeros((HALO, 3 * width), bf16)
         all_s[HALO + steps * rows :] = jnp.zeros((HALO, 3 * width), bf16)
-        for x in first:
+        for x in first[0] + first[1]:
             x.wait(3)
-        join_pairs(w_ref, ga, 0, wqkv.shape[1])
-        join_pairs(w_ref, gb, part, wqkv.shape[1])
+        join_pairs(w_ref, g_qkv)
         lane = lax.broadcasted_iota(jnp.int32, (128, width), 0)
         col = lax.broadcasted_iota(jnp.int32, (128, width), 1)
 
@@ -426,11 +422,24 @@
     advance(2 * steps - 1, plan[2 * steps])
 
 
-def join_pairs(ref, got, lo, step):
+def join_pairs(ref, got):
     nh, _, m, _, r, c = got.shape
     for d in range(2 * nh):
         for f in range(2 * m):
-            ref[f * r : (f + 1) * r, d * step + lo : d * step + lo + c] = got[d // 2, d % 2, f // 2, f % 2]
+            ref[f * r : (f + 1) * r, d * c : (d + 1) * c] = got[d // 2, d % 2, f // 2, f % 2]
+
+
+def qkv_parts(r, c):
+    if c % 384:
+        return [(0, (pl.ds(0, r), pl.ds(0, c)), "x")]
+    third = c // 3
+    whole = pl.ds(0, r)
+    parts = [(0, (whole, pl.ds(0, third)), "x"), (0, (whole, pl.ds(third, third)), "y")]
+    rest = pl.ds(2 * third, third)
+    if r % 32:
+        return parts + [(1, (whole, rest), "x")]
+    half = r // 2
+    return parts + [(1, (pl.ds(0, half), rest), "x"), (1, (pl.ds(half, half), rest), "y")]
 
 
 def front_pass(ways, length, tokens, w_qkv, w_in, w_back, w_out, vec, bias, tile, plan):
@@ -440,7 +449,6 @@
     nh, m = n_dp // 2, n_fsdp // 2
     steps = rows // tile
     head = width // HEADS
-    part = first_part(w_qkv.shape[1])
     const = lambda *shape: pl.BlockSpec(shape, lambda i: (0,) * len(shape))
     early = lambda i: (jnp.minimum(i, steps - 1), 0)
     late = pl.BlockSpec((tile, width), lambda i: (jnp.maximum(i - steps, 0), 0))
@@ -448,7 +456,7 @@
     sds = jax.ShapeDtypeStruct
     got = lambda r, c: (nh, 2, m, 2, r, c)
     hidden = w_in.shape[1] * n_dp
-    pieces = 8
+    pieces = 8 + len(qkv_parts(*w_qkv.shape))
     per = Gather.count(n_dp, n_fsdp)
     return pl.pallas_call(
         functools.partial(front_kernel, ways, plan, steps),
@@ -502,8 +510,7 @@
             pltpu.VMEM((rows + 2 * HALO, 3 * width), bf16),
             pltpu.VMEM((groups, GW, 2 * GW), f32),
             pltpu.VMEM((groups, 8, GW), f32),
-            pltpu.VMEM(got(w_qkv.shape[0], part), bf16),
-            pltpu.VMEM(got(w_qkv.shape[0], w_qkv.shape[1] - part), bf16),
+            pltpu.VMEM(got(*w_qkv.shape), bf16),
             pltpu.VMEM((16, 128), bf16),
             pltpu.VMEM(got(16, 128), bf16),
             pltpu.VMEM(w_in.shape, bf16),
@@ -570,92 +577,90 @@
     wout_ref,
     win_ref,
     wback_ref,
+    act_s,
+    pre_s,
 ):
     step = pl.program_id(0)
     rows, width = tok_ref.shape
     hidden = win_ref.shape[1]
     groups = width // GW
-    head = width // HEADS
+    head_size = width // HEADS
+    steps = pl.num_programs(0)
     length = len_ref[0, 0]
+    c_row = jnp.concatenate([c_ref[g, 0:1] for g in range(groups)], axis=1)
+    blend = vec_ref[...].astype(bf16)
+    s0 = math.sqrt(2.0 / math.pi)
+    s1 = s0 * 0.044715
 
     @pl.when(step == 0)
     def _():
         join_blocks(wout_ref, gw_out)
         join_blocks(win_ref, gw_in)
         join_blocks(wback_ref, gw_back)
-        a_in[...] = jnp.zeros_like(a_in)
-        a_back[...] = jnp.zeros_like(a_back)
-        a_out[...] = jnp.zeros_like(a_out)
-        a_st[...] = jnp.zeros_like(a_st)
-        a_bent[...] = jnp.zeros_like(a_bent)
-        gvec_ref[...] = jnp.zeros_like(gvec_ref)
-        gbias_ref[...] = jnp.zeros_like(gbias_ref)
-
-    c_row = jnp.concatenate([c_ref[g, 0:1] for g in range(groups)], axis=1)
-    near = near_ref[...].astype(f32)
-    fac = fa_ref[...].astype(f32)
-    far_b = fb_ref[...].astype(f32)
+        for ref in (a_in, a_back, a_out, a_st, a_bent, gvec_ref, gbias_ref):
+            ref[...] = jnp.zeros_like(ref)
+
+    near = near_ref[...]
+    fac = fa_ref[...]
+    far_b = fb_ref[...]
     mixed = (
-        vec_ref[5:6] * near + vec_ref[6:7] * (fac + c_row) + vec_ref[7:8] * far_b
+        vec_ref[5:6] * near.astype(f32)
+        + vec_ref[6:7] * (fac.astype(f32) + c_row)
+        + vec_ref[7:8] * far_b.astype(f32)
     ).astype(bf16)
     resid = tok_ref[...].astype(f32) + nn(mixed, wout_ref[...])
     z2, r2 = moments(resid)
     h2 = (z2 * vec_ref[2:3] + vec_ref[3:4]).astype(bf16)
     valid = row_valid(step, rows, width, length)
-    seed = jnp.where(valid, cot_ref[...].astype(f32), 0.0)
-    d_ffn = seed.astype(bf16)
-    s0 = math.sqrt(2.0 / math.pi)
-    s1 = s0 * 0.044715
-    ffn = jnp.zeros((rows, width), f32)
-    dh2 = jnp.zeros((rows, width), f32)
+    d_ffn = jnp.where(valid, cot_ref[...], 0)
+    seed = d_ffn.astype(f32)
     for lo in range(0, hidden, chunk):
         cols = slice(lo, lo + chunk)
         x = nn(h2, win_ref[:, cols]) + bin_ref[0:1, cols]
         x2 = x * x
-        t = jnp.tanh(x * (s0 + s1 * x2))
-        half = 0.5 + 0.5 * t
+        half = 0.5 + 0.5 * jnp.tanh(x * (s0 + s1 * x2))
         act = x * half
         slope = half + (act - act * half) * (2 * s0 + 6 * s1 * x2)
         act = act.astype(bf16)
-        ffn += nn(act, wback_ref[cols, :])
+        act_s[:, cols] = act
         a_back[:, cols] += tn(d_ffn, act)
         d_pre = slope * nt(d_ffn, wback_ref[cols, :])
         gbias_ref[:, cols] += fold8(d_pre)
         d_pre = d_pre.astype(bf16)
+        pre_s[:, cols] = d_pre
         a_in[:, cols] += tn(h2, d_pre)
-        dh2 += nt(d_pre, win_ref[:, cols])
-    out_ref[...] = jnp.where(valid, resid + ffn + vec_ref[4:5], 0.0).astype(bf16)
-    gvec_ref[2] += fold8(dh2 * z2)
+    dh2 = nt(pre_s[...], win_ref[...])
+    both = dh2 * z2
+    gvec_ref[2] += fold8(both)
     gvec_ref[3] += fold8(dh2)
     gvec_ref[4] += fold8(seed)
     dz = dh2 * vec_ref[2:3]
-    d_resid = seed + r2 * (
-        dz
-        - jnp.mean(dz, axis=-1, keepdims=True)
-        - z2 * jnp.mean(dz * z2, axis=-1, keepdims=True)
-    )
+    mean_z = jnp.mean(both * vec_ref[2:3], axis=-1, keepdims=True)
+    d_resid = seed + r2 * (dz - jnp.mean(dz, axis=-1, keepdims=True) - z2 * mean_z)
     d_attn = d_resid.astype(bf16)
     datt_ref[...] = d_attn
+    ffn = nn(act_s[...], wback_ref[...])
+    out_ref[...] = jnp.where(valid, resid + ffn + vec_ref[4:5], 0.0).astype(bf16)
     a_out[...] += tn(mixed, d_attn)
-    d_mix = nt(d_attn, wout_ref[...])
-    dmix_ref[...] = d_mix.astype(bf16)
-    gvec_ref[5] += fold8(d_mix * near)
-    gvec_ref[6] += fold8(d_mix * fac)
-    gvec_ref[7] += fold8(d_mix * far_b)
-    gvec_ref[0] += fold8(d_mix)
-    d_num = (vec_ref[6:7] * d_mix * rn_ref[...].astype(f32)).astype(bf16)
+    d_mix = nt(d_attn, wout_ref[...]).astype(bf16)
+    dmix_ref[...] = d_mix
+    gvec_ref[5] += fold8(fold4(d_mix * near).astype(f32))
+    gvec_ref[6] += fold8(fold4(d_mix * fac).astype(f32))
+    gvec_ref[7] += fold8(fold4(d_mix * far_b).astype(f32))
+    gvec_ref[0] += fold8(fold4(d_mix).astype(f32))
+    d_num = blend[6:7] * d_mix * rn_ref[...]
     dn_ref[...] = d_num
-    d_den = (d_num.astype(f32) * fac).astype(bf16)
-    d_far = (vec_ref[7:8] * d_mix).astype(bf16)
+    d_den = d_num * fac
+    d_far = blend[7:8] * d_mix
     for g in range(groups):
         cols = slice(g * GW, (g + 1) * GW)
         q = q_ref[:, cols]
         a_st[g] += tn(lift(q), jnp.concatenate([d_num[:, cols], d_den[:, cols]], axis=1))
         a_bent[g] += tn(jnp.tanh(q), d_far[:, cols])
 
-    @pl.when(step == pl.num_programs(0) - 1)
+    @pl.when(step == steps - 1)
     def _():
-        mask = same_head(head).astype(f32)
+        mask = same_head(head_size).astype(f32)
         inv_len = 1.0 / length.astype(f32)
         ones = jnp.ones((8, GW), f32)
         for g in range(groups):
@@ -668,28 +673,38 @@
         gvec_ref[6] += gvec_ref[0] * c_row
 
 
-def third_pass(ways, length, tokens, cot, near, fa, fb, rn, qkv, c, vecs, b_in, w_out, w_in, w_back, tile, chunk):
+def third_pass(
+    ways, length, tokens, cot, near, fa, fb, rn, qkv, c, vecs, b_in, w_out, w_in, w_back, tile, chunk
+):
     rows, width = tokens.shape
     hidden = w_in.shape[0] * w_in.shape[3]
     groups = width // GW
+    steps = rows // tile
     n_dp, n_fsdp = ways
     back = (width // n_dp, hidden // n_fsdp)
     back = back if turned(hidden, n_fsdp) else back[::-1]
-    const = lambda *shape: pl.BlockSpec(shape, lambda i: (0,) * len(shape))
+
+    def const(*shape):
+        return pl.BlockSpec(shape, lambda i: (0,) * len(shape))
+
+    def kept(*shape):
+        return pl.BlockSpec(shape, lambda i: (0,) * len(shape), pipeline_mode=pl.Buffered(1))
+
+    sds = jax.ShapeDtypeStruct
     block = pl.BlockSpec((tile, width), lambda i: (i, 0))
-    sds = jax.ShapeDtypeStruct
+    deep = pltpu.VMEM((tile, hidden), bf16)
     return pl.pallas_call(
         functools.partial(ffn_kernel, chunk),
-        grid=(rows // tile,),
+        grid=(steps,),
         in_specs=[pl.BlockSpec(memory_space=pltpu.SMEM)]
         + [block] * 7
         + [
             const(groups, 8, GW),
             const(8, width),
             const(1, hidden),
-            const(*w_out.shape),
-            const(*w_in.shape),
-            const(*w_back.shape),
+            kept(*w_out.shape),
+            kept(*w_in.shape),
+            kept(*w_back.shape),
         ],
         out_specs=[block] * 4
         + [
@@ -722,6 +737,8 @@
             pltpu.VMEM((width, width), bf16),
             pltpu.VMEM((width, hidden), bf16),
             pltpu.VMEM((hidden, width), bf16),
+            deep,
+            deep,
         ],
         compiler_params=pltpu.CompilerParams(vmem_limit_bytes=VMEM_LIMIT),
         cost_estimate=pl.CostEstimate(
@@ -880,8 +897,7 @@
     all_d,
     carry,
     gvec_s,
-    ga_ref,
-    gb_ref,
+    gq_ref,
     gs_ref,
     rows_s,
     back_t,
@@ -902,31 +918,33 @@
     place = Place(n_dp, n_fsdp)
     cols = ovec_ref.shape[1]
     c_all = oqkv_ref.shape[1]
-    part = ga_ref.shape[-1]
-    send, recv, local, late_send, late_recv = rest[30:]
+    send, recv, local, late_send, late_recv = rest[-5:]
     final = steps + 1 + place.nh
     last_rows = tok_ref.shape[0]
 
-    def piece(j, src, out, order):
+    used = [0]
+
+    def piece(src, out, order):
+        j = used[0]
+        used[0] += 1
         return Scatter(place, src, out, rest[5 * j : 5 * j + 5], send.at[j], recv.at[j], local.at[j], order)
 
-    early = [
-        piece(0, s_in, oin_ref, "x"),
-        piece(1, s_back, back_t, "y"),
-        piece(2, s_out, oout_ref, "y"),
-        piece(5, gs_ref, small_o, "x"),
-    ]
-    last = [
-        piece(3, ga_ref, oqkv_ref.at[:, pl.ds(0, part)], "x"),
-        piece(4, gb_ref, oqkv_ref.at[:, pl.ds(part, c_all - part)], "y"),
-    ]
+    sets = [[], [], [], []]
+    every = (slice(None),) * 4
+    for i, (cut_in, cut_back) in enumerate(ffn_parts(s_in.shape[-2:], s_back.shape[-2:])):
+        sets[i].append(piece(s_in.at[every + cut_in], oin_ref.at[cut_in], "x"))
+        sets[i].append(piece(s_back.at[every + cut_back], back_t.at[cut_back], "y"))
+    sets[1].append(piece(s_out, oout_ref, "y"))
+    sets[1].append(piece(gs_ref, small_o, "x"))
+    for which, cut, order in qkv_parts(*oqkv_ref.shape):
+        sets[2 + which].append(piece(gq_ref.at[every + cut], oqkv_ref.at[cut], order))
 
     @pl.when(step == 0)
     def _():
-        for x in early[:3]:
+        for x in sets[0] + sets[1][:-1]:
             x.own().start()
         greet_all(place)
-        for x in early[:3]:
+        for x in sets[0] + sets[1][:-1]:
             x.start(0)
         carry[...] = jnp.zeros_like(carry)
         gvec_s[...] = jnp.zeros_like(gvec_s)
@@ -942,15 +960,15 @@
                 at = d * width + f * cols
                 gs_ref[d // 2, d % 2, f // 2, f % 2, 0:2, :cols] = pair[:, spot]
                 gs_ref[d // 2, d % 2, f // 2, f % 2, 2:3, :cols] = bias[:, at : at + cols]
-        early[3].own().start()
-        early[3].start(0)
+        sets[1][-1].own().start()
+        sets[1][-1].start(0)
 
     for at, moves in plan.items():
 
         @pl.when(step == at)
         def _(moves=moves):
-            for k in moves:
-                for x in early:
+            for which, k in moves:
+                for x in sets[which]:
                     x.turn(k)
 
     def far_keys(at, slot, live):
@@ -1035,25 +1053,26 @@
         @pl.when(step == steps + 1 + dh)
         def _(dh=dh):
             grad = nn(h1t_ref[...], all_d[HALO : HALO + total, dh * 2 * c_all : (dh + 1) * 2 * c_all])
-            r = ga_ref.shape[-2]
+            r = gq_ref.shape[-2]
             for dl in range(2):
                 for f in range(n_fsdp):
-                    block = grad[f * r : (f + 1) * r, dl * c_all : (dl + 1) * c_all].astype(bf16)
-                    ga_ref[dh, dl, f // 2, f % 2] = block[:, :part]
-                    gb_ref[dh, dl, f // 2, f % 2] = block[:, part:]
+                    block = grad[f * r : (f + 1) * r, dl * c_all : (dl + 1) * c_all]
+                    gq_ref[dh, dl, f // 2, f % 2] = block.astype(bf16)
 
     @pl.when(step == final)
     def _():
-        for x in last:
+        for x in sets[2] + sets[3]:
             x.own().start()
             x.start(0)
 
     for at, moves in late_plan.items():
+        if at == "end":
+            continue
 
         @pl.when(step == final + at)
         def _(moves=moves):
-            for k in moves:
-                for x in last:
+            for which, k in moves:
+                for x in sets[which]:
                     x.turn(k)
 
     @pl.when(step >= final)
@@ -1095,8 +1114,9 @@
         for o in range(1, n_fsdp):
             late(o).start()
         oback_ref[...] = back_t[...].T if turned(gbias_ref.shape[1], n_fsdp) else back_t[...]
-        for x in last:
-            x.turn(3)
+        for which, k in late_plan["end"]:
+            for x in sets[which]:
+                x.turn(k)
 
         @pl.when(d > 0)
         def _():
@@ -1121,6 +1141,19 @@
             ovec_ref[...] = jnp.sum(late_got[...], axis=0)[0:2, :cols]
 
         obias_ref[...] = small_o[2:3, :cols]
+
+
+def ffn_parts(shape_in, shape_back):
+    (r, c), (rb, cb) = shape_in, shape_back
+    out = []
+    for i in range(2):
+        cut_in = (pl.ds(0, r), pl.ds(i * c // 2, c // 2))
+        if cb % 256:
+            cut_back = (pl.ds(i * rb // 2, rb // 2), pl.ds(0, cb))
+        else:
+            cut_back = (pl.ds(0, rb), pl.ds(i * cb // 2, cb // 2))
+        out.append((cut_in, cut_back))
+    return out
 
 
 def greet_all(place):
@@ -1179,7 +1212,6 @@
     n_dp, n_fsdp = ways
     nh, m = n_dp // 2, n_fsdp // 2
     r, c_all = width // n_fsdp, 3 * width // n_dp
-    part = first_part(c_all)
     per = Scatter.count(n_dp, n_fsdp)
     final = steps + 1 + nh
     hbm = pl.BlockSpec(memory_space=pl.ANY)
@@ -1192,14 +1224,14 @@
         (2, width // n_fsdp),
         (1, gbias.shape[1] // (n_dp * n_fsdp)),
     ]
-    kinds = [
-        (*s_in.shape[-2:], "x", bf16),
-        (*back_shape, "y", bf16),
-        (*s_out.shape[-2:], "y", bf16),
-        (r, part, "x", bf16),
-        (r, c_all - part, "y", bf16),
-        (8, 128, "x", f32),
-    ]
+    kinds = []
+    for cut_in, cut_back in ffn_parts(s_in.shape[-2:], back_shape):
+        kinds.append((*(x.size for x in cut_in), "x", bf16))
+        kinds.append((*(x.size for x in cut_back), "y", bf16))
+    kinds.append((*s_out.shape[-2:], "y", bf16))
+    kinds.append((8, 128, "x", f32))
+    for _, cut, order in qkv_parts(r, c_all):
+        kinds.append((*(x.size for x in cut), order, bf16))
     bufs = [b for k in kinds for b in Scatter.scratch(n_dp, n_fsdp, *k)]
     got = lambda *s: (nh, 2, m, 2, *s)
 
@@ -1266,8 +1298,7 @@
             pltpu.VMEM((rows + 2 * HALO, 3 * width), bf16),
             pltpu.VMEM((2, QB, width), f32),
             pltpu.VMEM((2, 8, width), f32),
-            pltpu.VMEM(got(r, part), bf16),
-            pltpu.VMEM(got(r, c_all - part), bf16),
+            pltpu.VMEM(got(r, c_all), bf16),
             pltpu.VMEM(got(8, 128), f32),
             pltpu.VMEM((8, width), f32),
             pltpu.VMEM(back_shape, f32),
@@ -1275,9 +1306,9 @@
             pltpu.VMEM((n_fsdp, 8, 128), f32),
             pltpu.VMEM((n_dp * n_fsdp, 8, 128), f32),
             *bufs,
-            pltpu.SemaphoreType.DMA((6, per)),
-            pltpu.SemaphoreType.DMA((6, per)),
-            pltpu.SemaphoreType.DMA((6,)),
+            pltpu.SemaphoreType.DMA((len(kinds), per)),
+            pltpu.SemaphoreType.DMA((len(kinds), per)),
+            pltpu.SemaphoreType.DMA((len(kinds),)),
             pltpu.SemaphoreType.DMA((n_fsdp,)),
             pltpu.SemaphoreType.DMA((n_dp * n_fsdp,)),
         ],
@@ -1343,10 +1374,10 @@
 FRONT_TILE = 1024
 TILE = 512
 LAST_TILE = 1024
-CHUNK = 512
-FRONT_PLAN = {2: [(0, 0), (1, 0)], 3: [(0, 1), (1, 1)], 6: [(0, 2), (1, 2)], 8: [(0, 3), (1, 3)]}
-BACK_PLAN = {4: [0], 7: [1], 9: [2], 10: [3]}
-LATE_PLAN = {1: [0], 2: [1], 3: [2]}
+CHUNK = 256
+FRONT_PLAN = {1: [(0, 0), (1, 0)], 3: [(0, 1)], 4: [(1, 1)], 5: [(0, 2)], 6: [(1, 2)], 8: [(0, 3), (1, 3)]}
+BACK_PLAN = {2: [(0, 0)], 3: [(1, 0)], 4: [(0, 1)], 6: [(1, 1), (0, 2)], 8: [(1, 2), (0, 3)], 10: [(1, 3)]}
+LATE_PLAN = {1: [(2, 0), (3, 0)], 3: [(2, 1), (3, 1)], "end": [(2, 2), (3, 2), (2, 3), (3, 3)]}
 
 
 def shards(
@@ -1429,7 +1460,7 @@
         LATE_PLAN,
     )
     d_tok, r_qkv, r_out, r_in, r_back, r_vec, r_bias = hand_over(
-        [d_tok, r_qkv, r_out, r_in, r_back, r_vec, r_bias], 4
+        [d_tok, r_qkv, r_out, r_in, r_back, r_vec, r_bias], 8
     )
     return (out, d_tok, r_qkv, r_out, r_in, r_back, r_vec, r_bias[0])
 

time: 258 us -> 235 us (0.911)
  Pallas kernels: 256 us -> 233 us
    pallas_call x1, Pallas kernels: 89.4 us -> 77.9 us  [back_pass(): pl.pallas_call(functools.partial(back_kernel, ways, plan, late_plan), gri...]
    pallas_call x1, Pallas kernels: 94.5 us -> 84.3 us  [third_pass(): pl.pallas_call(functools.partial(ffn_kernel, chunk), grid=(steps,), in_sp...]
    pallas_call x1, Pallas kernels: 67.6 us -> 64.3 us  [front_pass(): pl.pallas_call(functools.partial(front_kernel, ways, plan, steps), grid=(...]
where the time goes in v5:
time: 235 us; the launch traced here: 234 us
  Pallas kernels  233 us (99%)
    pallas_call x1, Pallas kernels, third_pass(): pl.pallas_call(functools.partial(ffn_kernel, chunk), grid=(steps,), in_sp...  84.3 us
    pallas_call x1, Pallas kernels, back_pass(): pl.pallas_call(functools.partial(back_kernel, ways, plan, late_plan), gri...  77.9 us
    pallas_call x1, Pallas kernels, front_pass(): pl.pallas_call(functools.partial(front_kernel, ways, plan, steps), grid=(...  64.3 us
    pallas_call x1, Pallas kernels, hand_over(): pl.pallas_call(functools.partial(hand_kernel, len(arrays)), grid=(parts,)...  6.9 us

profile of v5, /device:TPU:0, one launch (start us, length us, event | category | flops | bytes accessed | tf_op | source)
XLA Modules:
  0.0 234.3 jit_solution(17095478558589669612)
XLA Ops:
  0.6 64.3 %front_pass.1 = (bf16[4096,1536]{1,0:T(8,128)(2,1)}, bf16[4096,512]{1,0:T(8,128)(2,1)}, bf16[4096,512]{1,0:T(8,128)(2,1)}, bf16[4096,512]{1,0:T(8,128)(2,1)}, bf...) custom-call(s32[1,4]{1,0:T(1,128)} %len_ref.5, ...), custom_call_target="tpu_custom_call" | custom-call | flops 17179869184 | bytes 50331648 | tf_op jit(solution)/shard_map/front_pass/pallas_call | solution.py:461
  64.9 84.3 %third_pass.1 = (bf16[4096,512]{1,0:T(8,128)(2,1)}, bf16[4096,512]{1,0:T(8,128)(2,1)}, bf16[4096,512]{1,0:T(8,128)(2,1)}, bf16[4096,512]{1,0:T(8,128)(2,1)}, bf1...) custom-call(s32[1,4]{1,0:T(1,128)} %len_ref.5, ...), custom_call_target="tpu_custom_call" | custom-call | flops 60129542144 | bytes 46137344 | tf_op jit(solution)/shard_map/third_pass/pallas_call | solution.py:696
  149.2 77.9 %back_pass.1 = (bf16[4096,512]{1,0:T(8,128)(2,1)}, f32[64,384]{1,0:T(8,128)}, f32[64,512]{1,0:T(8,128)}, f32[256,128]{1,0:T(8,128)}, f32[64,128]{1,0:T(8,128)}, /*index=5*/f32[2,64]{1,0:T(2,128)}, f32[1,64]{1,0:T(1,128)}) custom-call(s32[1,4]{1,0:T(1,128)} %len_ref.5, bf16[4096,1536]{1,0:T(8,128)(2,1)} %get-tuple-element.54.q_ref.k_lo.k_ref.k_hi.v_lo.v_ref.v_hi, ...), custom_call_target="tpu_custom_call" | custom-call | flops 30064771072 | bytes 50331648 | tf_op jit(solution)/shard_map/back_pass/pallas_call | solution.py:1260
  227.2 6.9 %hand_over.1 = (bf16[4096,512]{1,0:T(8,128)(2,1)}, f32[64,384]{1,0:T(8,128)}, f32[64,128]{1,0:T(8,128)}, f32[64,512]{1,0:T(8,128)}, f32[256,128]{1,0:T(8,128)}, /*index=5*/f32[2,64]{1,0:T(2,128)}, f32[1,64]{1,0:T(1,128)}) custom-call(bf16[4096,512]{1,0:T(8,128)(2,1)} %get-tuple-element.78.refs_0_, f32[64,384]{1,0:T(8,128)} %get-tuple-element.79.refs_1_, ...), custom_call_target="tpu_custom_call" | custom-call | tf_op jit(solution)/shard_map/hand_over/pallas_call | solution.py:1364

commit v6 on v5

--- a/solution.py
+++ b/solution.py
@@ -232,7 +232,6 @@
     vec_in,
     bias_in,
     band_ref,
-    hm_ref,
     qkv_ref,
     near_ref,
     fa_ref,
@@ -258,6 +257,8 @@
     way_in,
     way_back,
     way_out,
+    key_s,
+    qq_s,
     send,
     recv,
     local,
@@ -306,6 +307,13 @@
         for x in rest:
             x.fetch().wait()
             x.own().start()
+        st_ref[...] = jnp.zeros_like(st_ref)
+        t_ref[...] = jnp.zeros_like(t_ref)
+        all_s[:HALO] = jnp.zeros((HALO, 3 * width), bf16)
+        all_s[HALO + steps * rows :] = jnp.zeros((HALO, 3 * width), bf16)
+        qq_s[...] = jnp.zeros_like(qq_s)
+        key = lax.broadcasted_iota(jnp.int32, key_s.shape, 0) - HALO
+        key_s[...] = jnp.where((key >= 0) & (key < length), 0.0, -1e30)
         for k in range(3):
             for group in first:
                 for x in group:
@@ -313,10 +321,6 @@
             if k == 0:
                 for x in sets[0] + sets[1]:
                     x.start(0)
-        st_ref[...] = jnp.zeros_like(st_ref)
-        t_ref[...] = jnp.zeros_like(t_ref)
-        all_s[:HALO] = jnp.zeros((HALO, 3 * width), bf16)
-        all_s[HALO + steps * rows :] = jnp.zeros((HALO, 3 * width), bf16)
         for x in first[0] + first[1]:
             x.wait(3)
         join_pairs(w_ref, g_qkv)
@@ -391,20 +395,18 @@
 
     @pl.when(step >= steps)
     def _():
-        hm = hm_ref[...]
         at = (step - steps) * rows
         for b in range(rows // QB):
-            base = at + b * QB - HALO
-            key = base + lax.broadcasted_iota(jnp.int32, (KW, GW), 0)
-            bias = jnp.where((key >= 0) & (key < length), band_ref[...], -1e30)
             here = pl.ds(pl.multiple_of(at + b * QB + HALO, HALO), QB)
             window = pl.ds(pl.multiple_of(at + b * QB, QB), KW)
+            out_of_item = key_s[window]
+            bias = band_ref[...] + jnp.concatenate([out_of_item] * (GW // 128), axis=1)
             for g in range(groups):
                 cut = slice(g * GW, (g + 1) * GW)
                 kc = slice(width + g * GW, width + (g + 1) * GW)
                 vc = slice(2 * width + g * GW, 2 * width + (g + 1) * GW)
-                qs = spread_rows(all_s[here, cut] * scale, hm)
-                s = nt(all_s[window, kc], qs) + bias
+                put_heads(qq_s.at[g, b], all_s[here, cut] * scale, head)
+                s = nt(all_s[window, kc], qq_s[g, b]) + bias
                 e = jnp.exp(s - jnp.max(s, axis=0, keepdims=True))
                 p = (e * (1.0 / jnp.sum(e, axis=0, keepdims=True))).astype(bf16)
                 p_ref[b, :, cut] = p
@@ -471,7 +473,6 @@
             const(*vec.shape),
             const(*bias.shape),
             const(KW, GW),
-            const(GW, GW),
         ],
         out_specs=[
             pl.BlockSpec((tile, 3 * width), early),
@@ -516,6 +517,8 @@
             pltpu.VMEM(w_in.shape, bf16),
             pltpu.VMEM(w_back.shape, bf16),
             pltpu.VMEM(w_out.shape, bf16),
+            pltpu.VMEM((rows + 2 * HALO, 128), f32),
+            pltpu.VMEM((groups, tile // QB, GW, GW), bf16),
             pltpu.SemaphoreType.DMA((pieces, per)),
             pltpu.SemaphoreType.DMA((pieces, per)),
             pltpu.SemaphoreType.DMA((pieces,)),
@@ -537,7 +540,6 @@
         vec,
         bias,
         jnp.asarray(band_table(head)),
-        jnp.asarray(head_table(head), bf16),
     )
 
 
@@ -758,7 +760,7 @@
 
     @staticmethod
     def count(n_dp, n_fsdp):
-        return 1 + 1 + (n_dp // 2 - 1) + (n_fsdp // 2 - 1)
+        return n_dp // 2 + 1 + (n_dp // 2 - 1) + (n_fsdp // 2 - 1)
 
     @staticmethod
     def scratch(n_dp, n_fsdp, r, c, order, dtype):
@@ -773,13 +775,17 @@
     def own(self):
         return pltpu.make_async_copy(self.src.at[:, self.p.dl], self.acc, self.local)
 
-    def stage(self, k):
+    def stage(self, k, only=None):
         p = self.p
         if k == 0:
-            ref = self.src.at[:, 1 - p.dl]
-            return [copy_to(ref, self.r0, self.send.at[0], self.recv.at[0], p.dev(dl=1 - p.dl))]
+            to = p.dev(dl=1 - p.dl)
+            return [
+                copy_to(self.src.at[dh, 1 - p.dl], self.r0.at[dh], self.send.at[dh], self.recv.at[dh], to)
+                for dh in (range(p.nh) if only is None else [only])
+            ]
+        first = p.nh - 1
         if k == 3:
-            i = p.nh
+            i = first + p.nh
             out = []
             for o in range(1, p.m):
                 fh = lax.rem(p.fh + o, p.m)
@@ -791,13 +797,15 @@
         if (k == 1) == (self.order == "x"):
             ref = self.acc.at[:, :, 1 - p.fl] if k == 1 else self.acc.at[p.dh, :, 1 - p.fl]
             dst = self.r1 if k == 1 else self.r2
-            return [copy_to(ref, dst, self.send.at[1], self.recv.at[1], p.dev(fl=1 - p.fl))]
+            i = first + 1
+            return [copy_to(ref, dst, self.send.at[i], self.recv.at[i], p.dev(fl=1 - p.fl))]
         out = []
         for o in range(1, p.nh):
             dh = lax.rem(p.dh + o, p.nh)
             ref = self.acc.at[dh] if k == 1 else self.acc.at[dh, :, p.fl]
             dst = self.r1.at[o - 1] if k == 1 else self.r2.at[o - 1]
-            out.append(copy_to(ref, dst, self.send.at[1 + o], self.recv.at[1 + o], p.dev(dh=dh)))
+            i = first + 1 + o
+            out.append(copy_to(ref, dst, self.send.at[i], self.recv.at[i], p.dev(dh=dh)))
         return out
 
     def start(self, k):
@@ -819,6 +827,9 @@
         dt = acc.dtype
 
         def put(index, others):
+            if len(others) == 1:
+                acc[index] += others[0]
+                return
             total = acc[index].astype(f32)
             for o in others:
                 total = total + o.astype(f32)
@@ -867,7 +878,7 @@
     fa_ref,
     tok_ref,
     datt_ref,
-    h1t_ref,
+    h1t_hbm,
     m1_ref,
     m2_ref,
     m3_ref,
@@ -875,8 +886,7 @@
     dt_ref,
     c_ref,
     vec_ref,
-    w_ref,
-    hm_ref,
+    w_hbm,
     gv_ref,
     gbias_ref,
     s_in,
@@ -889,11 +899,15 @@
     oout_ref,
     ovec_ref,
     obias_ref,
+    h1t_ref,
+    w_ref,
     kk,
     vv,
     far_s,
     dp_s,
     ds_s,
+    dd_s,
+    qq_s,
     all_d,
     carry,
     gvec_s,
@@ -918,7 +932,11 @@
     place = Place(n_dp, n_fsdp)
     cols = ovec_ref.shape[1]
     c_all = oqkv_ref.shape[1]
-    send, recv, local, late_send, late_recv = rest[-5:]
+    send, recv, local, late_send, late_recv, fetch = rest[-6:]
+    fetches = [
+        pltpu.make_async_copy(h1t_hbm, h1t_ref, fetch.at[0]),
+        pltpu.make_async_copy(w_hbm, w_ref, fetch.at[1]),
+    ]
     final = steps + 1 + place.nh
     last_rows = tok_ref.shape[0]
 
@@ -946,7 +964,11 @@
         greet_all(place)
         for x in sets[0] + sets[1][:-1]:
             x.start(0)
+        for x in fetches:
+            x.start()
         carry[...] = jnp.zeros_like(carry)
+        dd_s[...] = jnp.zeros_like(dd_s)
+        qq_s[...] = jnp.zeros_like(qq_s)
         gvec_s[...] = jnp.zeros_like(gvec_s)
         gs_ref[...] = jnp.zeros_like(gs_ref)
         late_src[...] = jnp.zeros_like(late_src)
@@ -982,14 +1004,13 @@
             v = vv[slot, HALO : HALO + rows, cut]
             lift_k = lift(k)
             bent_k = jnp.tanh(k)
-            bent = bent_k.astype(f32)
             v_cen = v - c_ref[g, 0:1].astype(bf16)
-            dk = (nt(v_cen, m3_ref[g]) + dt_ref[g, 0:1]) * jnp.minimum(lift_k, 1.0).astype(f32)
-            dk += nt(v, m4_ref[g]) * (1.0 - bent * bent)
+            dk = (nt(v_cen, m3_ref[g]) + dt_ref[g, 0:1]) * jnp.minimum(lift_k, 1).astype(f32)
+            dk += nt(v, m4_ref[g]) * (1 - bent_k * bent_k).astype(f32)
             both = jnp.concatenate([lift_k, bent_k], axis=1)
             dv = nn(both, jnp.concatenate([m3_ref[g], m4_ref[g]], axis=0))
-            all_d[here, kc] = (all_d[here, kc].astype(f32) + jnp.where(valid, dk, 0.0)).astype(bf16)
-            all_d[here, vc] = (all_d[here, vc].astype(f32) + jnp.where(valid, dv, 0.0)).astype(bf16)
+            all_d[here, kc] += jnp.where(valid, dk.astype(bf16), 0)
+            all_d[here, vc] += jnp.where(valid, dv.astype(bf16), 0)
 
     @pl.when(step < steps)
     def _():
@@ -1000,7 +1021,6 @@
         vv[slot, :HALO] = v_lo[...]
         vv[slot, HALO : HALO + rows] = v_ref[...]
         vv[slot, HALO + rows :] = v_hi[...]
-        hm = hm_ref[...]
         blend = vec_ref[...].astype(bf16)
         base = step * rows
         for g in range(groups):
@@ -1011,26 +1031,28 @@
             d_num = dn_ref[:, cut]
             d_den = -d_num * fa_ref[:, cut]
             d_mix = dmix_ref[:, cut]
-            bent = jnp.tanh(q).astype(f32)
-            far = nn(jnp.concatenate([d_num, d_den], axis=1), m1_ref[g]) * jnp.minimum(lift(q), 1.0).astype(f32)
-            far_s[:, cut] = far + nn(blend[7:8, cut] * d_mix, m2_ref[g]) * (1.0 - bent * bent)
+            bent = jnp.tanh(q)
+            far = nn(jnp.concatenate([d_num, d_den], axis=1), m1_ref[g]) * jnp.minimum(lift(q), 1).astype(f32)
+            far_s[:, cut] = far + nn(blend[7:8, cut] * d_mix, m2_ref[g]) * (1 - bent * bent).astype(f32)
             for b in range(rows // QB):
                 here = slice(b * QB, (b + 1) * QB)
                 window = slice(b * QB, b * QB + KW)
-                ds = spread_rows(blend[5:6, cut] * dmix_ref[here, cut], hm)
-                dp_s[g, b] = nt(vv[slot, window, cut], ds)
+                put_heads(dd_s.at[g, b], blend[5:6, cut] * dmix_ref[here, cut], head)
+                dp_s[g, b] = nt(vv[slot, window, cut], dd_s[g, b]).astype(bf16)
             for b in range(rows // QB):
-                pw = p_ref[b, :, cut].astype(f32)
-                t = pw * dp_s[g, b]
-                ds_s[g, b] = (t - pw * jnp.sum(t, axis=0, keepdims=True)).astype(bf16)
+                p = p_ref[b, :, cut]
+                dp = dp_s[g, b]
+                dot = jnp.sum(fold4(p * dp).astype(f32), axis=0, keepdims=True)
+                ds_s[g, b] = p * (dp - dot.astype(bf16))
             old_k = carry[0, :, cut]
             old_v = carry[1, :, cut]
             for b in range(rows // QB):
                 here = slice(b * QB, (b + 1) * QB)
                 window = slice(b * QB, b * QB + KW)
                 d_s = ds_s[g, b]
-                dk = nn(d_s, spread_rows(q_ref[here, cut] * scale, hm))
-                dv = nn(p_ref[b, :, cut], spread_rows(blend[5:6, cut] * dmix_ref[here, cut], hm))
+                put_heads(qq_s.at[g, b], q_ref[here, cut] * scale, head)
+                dk = nn(d_s, qq_s[g, b])
+                dv = nn(p_ref[b, :, cut], dd_s[g, b])
                 dq = pick_heads(tn(d_s, kk[slot, window, cut]), head) * scale + far_s[here, cut]
                 lo = pl.ds(pl.multiple_of(base + b * QB, QB), QB)
                 all_d[pl.ds(pl.multiple_of(base + b * QB + HALO, HALO), QB), cut] = dq.astype(bf16)
@@ -1052,18 +1074,22 @@
 
         @pl.when(step == steps + 1 + dh)
         def _(dh=dh):
+            if dh == 0:
+                fetches[0].wait()
             grad = nn(h1t_ref[...], all_d[HALO : HALO + total, dh * 2 * c_all : (dh + 1) * 2 * c_all])
             r = gq_ref.shape[-2]
             for dl in range(2):
                 for f in range(n_fsdp):
                     block = grad[f * r : (f + 1) * r, dl * c_all : (dl + 1) * c_all]
                     gq_ref[dh, dl, f // 2, f % 2] = block.astype(bf16)
+            for x in sets[2] + sets[3]:
+                x.stage(0, dh)[0].start()
 
     @pl.when(step == final)
     def _():
+        fetches[1].wait()
         for x in sets[2] + sets[3]:
             x.own().start()
-            x.start(0)
 
     for at, moves in late_plan.items():
         if at == "end":
@@ -1141,6 +1167,12 @@
             ovec_ref[...] = jnp.sum(late_got[...], axis=0)[0:2, :cols]
 
         obias_ref[...] = small_o[2:3, :cols]
+
+
+def put_heads(ref, x, head):
+    for h in range(GW // head):
+        lanes = slice(h * head, (h + 1) * head)
+        ref[h * QB : (h + 1) * QB, lanes] = x[:, lanes]
 
 
 def ffn_parts(shape_in, shape_back):
@@ -1271,7 +1303,7 @@
             block,
             late,
             late,
-            kept(width, rows),
+            hbm,
             kept(groups, 2 * GW, GW),
             kept(groups, GW, GW),
             kept(groups, GW, GW),
@@ -1279,8 +1311,7 @@
             const(groups, 8, GW),
             const(groups, 8, GW),
             const(8, width),
-            kept(width, 3 * width),
-            const(GW, GW),
+            hbm,
             const(*gv.shape),
             const(*gbias.shape),
             hbm,
@@ -1290,11 +1321,15 @@
         out_specs=[late] + [const(*s) for s in outs],
         out_shape=[sds((rows, width), bf16)] + [sds(s, f32) for s in outs],
         scratch_shapes=[
+            pltpu.VMEM((width, rows), bf16),
+            pltpu.VMEM((width, 3 * width), bf16),
             pltpu.VMEM((2, tile + 2 * HALO, width), bf16),
             pltpu.VMEM((2, tile + 2 * HALO, width), bf16),
             pltpu.VMEM((tile, width), f32),
-            pltpu.VMEM((groups, tile // QB, KW, GW), f32),
             pltpu.VMEM((groups, tile // QB, KW, GW), bf16),
+            pltpu.VMEM((groups, tile // QB, KW, GW), bf16),
+            pltpu.VMEM((groups, tile // QB, GW, GW), bf16),
+            pltpu.VMEM((groups, tile // QB, GW, GW), bf16),
             pltpu.VMEM((rows + 2 * HALO, 3 * width), bf16),
             pltpu.VMEM((2, QB, width), f32),
             pltpu.VMEM((2, 8, width), f32),
@@ -1311,6 +1346,7 @@
             pltpu.SemaphoreType.DMA((len(kinds),)),
             pltpu.SemaphoreType.DMA((n_fsdp,)),
             pltpu.SemaphoreType.DMA((n_dp * n_fsdp,)),
+            pltpu.SemaphoreType.DMA((2,)),
         ],
         compiler_params=pltpu.CompilerParams(
             collective_id=1, has_side_effects=True, vmem_limit_bytes=VMEM_LIMIT
@@ -1343,7 +1379,6 @@
         c,
         vecs,
         w_qkv,
-        jnp.asarray(head_table(head), bf16),
         gv,
         gbias,
         s_in,
@@ -1375,9 +1410,9 @@
 TILE = 512
 LAST_TILE = 1024
 CHUNK = 256
-FRONT_PLAN = {1: [(0, 0), (1, 0)], 3: [(0, 1)], 4: [(1, 1)], 5: [(0, 2)], 6: [(1, 2)], 8: [(0, 3), (1, 3)]}
-BACK_PLAN = {2: [(0, 0)], 3: [(1, 0)], 4: [(0, 1)], 6: [(1, 1), (0, 2)], 8: [(1, 2), (0, 3)], 10: [(1, 3)]}
-LATE_PLAN = {1: [(2, 0), (3, 0)], 3: [(2, 1), (3, 1)], "end": [(2, 2), (3, 2), (2, 3), (3, 3)]}
+FRONT_PLAN = {1: [(0, 0)], 2: [(1, 0)], 3: [(0, 1)], 5: [(0, 2), (1, 1)], 7: [(1, 2)], 8: [(0, 3), (1, 3)]}
+BACK_PLAN = {2: [(0, 0)], 3: [(1, 0)], 4: [(0, 1)], 6: [(1, 1), (0, 2)], 7: [(1, 2)], 8: [(0, 3)], 12: [(1, 3)]}
+LATE_PLAN = {1: [(2, 0), (3, 0)], 2: [(2, 1)], 3: [(3, 1), (2, 2)], "end": [(3, 2), (2, 3), (3, 3)]}
 
 
 def shards(
@@ -1460,7 +1495,7 @@
         LATE_PLAN,
     )
     d_tok, r_qkv, r_out, r_in, r_back, r_vec, r_bias = hand_over(
-        [d_tok, r_qkv, r_out, r_in, r_back, r_vec, r_bias], 8
+        [d_tok, r_qkv, r_out, r_in, r_back, r_vec, r_bias], 2
     )
     return (out, d_tok, r_qkv, r_out, r_in, r_back, r_vec, r_bias[0])
 

time: 235 us -> 227 us (0.966)
  Pallas kernels: 233 us -> 226 us
    pallas_call x1, Pallas kernels: 77.9 us -> 74.5 us  [back_pass(): pl.pallas_call(functools.partial(back_kernel, ways, plan, late_plan), gri...]
    pallas_call x1, Pallas kernels: 6.9 us -> 3.96 us  [hand_over(): pl.pallas_call(functools.partial(hand_kernel, len(arrays)), grid=(parts,)...]
where the time goes in v6:
time: 227 us
  Pallas kernels  226 us (100%)
    pallas_call x1, Pallas kernels, third_pass(): pl.pallas_call(functools.partial(ffn_kernel, chunk), grid=(steps,), in_sp...  84.3 us
    pallas_call x1, Pallas kernels, back_pass(): pl.pallas_call(functools.partial(back_kernel, ways, plan, late_plan), gri...  74.5 us
    pallas_call x1, Pallas kernels, front_pass(): pl.pallas_call(functools.partial(front_kernel, ways, plan, steps), grid=(...  63.1 us

profile of v6, /device:TPU:0, one launch (start us, length us, event | category | flops | bytes accessed | tf_op | source)
XLA Modules:
  0.0 226.7 jit_solution(8696832307689282278)
XLA Ops:
  0.6 63.1 %front_pass.1 = (bf16[4096,1536]{1,0:T(8,128)(2,1)}, bf16[4096,512]{1,0:T(8,128)(2,1)}, bf16[4096,512]{1,0:T(8,128)(2,1)}, bf16[4096,512]{1,0:T(8,128)(2,1)}, bf...) custom-call(s32[1,4]{1,0:T(1,128)} %len_ref.5, ...), custom_call_target="tpu_custom_call" | custom-call | flops 17179869184 | bytes 50331648 | tf_op jit(solution)/shard_map/front_pass/pallas_call | solution.py:463
  63.7 84.3 %third_pass.1 = (bf16[4096,512]{1,0:T(8,128)(2,1)}, bf16[4096,512]{1,0:T(8,128)(2,1)}, bf16[4096,512]{1,0:T(8,128)(2,1)}, bf16[4096,512]{1,0:T(8,128)(2,1)}, bf1...) custom-call(s32[1,4]{1,0:T(1,128)} %len_ref.5, ...), custom_call_target="tpu_custom_call" | custom-call | flops 60129542144 | bytes 46137344 | tf_op jit(solution)/shard_map/third_pass/pallas_call | solution.py:698
  148.0 74.5 %back_pass.1 = (bf16[4096,512]{1,0:T(8,128)(2,1)}, f32[64,384]{1,0:T(8,128)}, f32[64,512]{1,0:T(8,128)}, f32[256,128]{1,0:T(8,128)}, f32[64,128]{1,0:T(8,128)}, /*index=5*/f32[2,64]{1,0:T(2,128)}, f32[1,64]{1,0:T(1,128)}) custom-call(s32[1,4]{1,0:T(1,128)} %len_ref.5, bf16[4096,1536]{1,0:T(8,128)(2,1)} %get-tuple-element.54.q_ref.k_lo.k_ref.k_hi.v_lo.v_ref.v_hi, ...), custom_call_target="tpu_custom_call" | custom-call | flops 30064771072 | bytes 50331648 | tf_op jit(solution)/shard_map/back_pass/pallas_call | solution.py:1292
  222.5 4.0 %hand_over.1 = (bf16[4096,512]{1,0:T(8,128)(2,1)}, f32[64,384]{1,0:T(8,128)}, f32[64,128]{1,0:T(8,128)}, f32[64,512]{1,0:T(8,128)}, f32[256,128]{1,0:T(8,128)}, /*index=5*/f32[2,64]{1,0:T(2,128)}, f32[1,64]{1,0:T(1,128)}) custom-call(bf16[4096,512]{1,0:T(8,128)(2,1)} %get-tuple-element.78.refs_0_, f32[64,384]{1,0:T(8,128)} %get-tuple-element.79.refs_1_, ...), custom_call_target="tpu_custom_call" | custom-call | tf_op jit(solution)/shard_map/hand_over/pallas_call | solution.py:1399

commit v7 on v6

--- a/solution.py
+++ b/solution.py
@@ -616,21 +616,26 @@
     valid = row_valid(step, rows, width, length)
     d_ffn = jnp.where(valid, cot_ref[...], 0)
     seed = d_ffn.astype(f32)
+    def add_grads(cols):
+        a_back[:, cols] += tn(d_ffn, act_s[:, cols])
+        a_in[:, cols] += tn(h2, pre_s[:, cols])
+
     for lo in range(0, hidden, chunk):
         cols = slice(lo, lo + chunk)
         x = nn(h2, win_ref[:, cols]) + bin_ref[0:1, cols]
+        if lo:
+            add_grads(slice(lo - chunk, lo))
         x2 = x * x
         half = 0.5 + 0.5 * jnp.tanh(x * (s0 + s1 * x2))
         act = x * half
         slope = half + (act - act * half) * (2 * s0 + 6 * s1 * x2)
         act = act.astype(bf16)
         act_s[:, cols] = act
-        a_back[:, cols] += tn(d_ffn, act)
         d_pre = slope * nt(d_ffn, wback_ref[cols, :])
         gbias_ref[:, cols] += fold8(d_pre)
         d_pre = d_pre.astype(bf16)
         pre_s[:, cols] = d_pre
-        a_in[:, cols] += tn(h2, d_pre)
+    add_grads(slice(hidden - chunk, hidden))
     dh2 = nt(pre_s[...], win_ref[...])
     both = dh2 * z2
     gvec_ref[2] += fold8(both)

time: 227 us -> 225 us (level)
  no operation moved by 1% of the time
where the time goes in v7:
time: 225 us
  Pallas kernels  224 us (100%)
    pallas_call x1, Pallas kernels, third_pass(): pl.pallas_call(functools.partial(ffn_kernel, chunk), grid=(steps,), in_sp...  82.5 us
    pallas_call x1, Pallas kernels, back_pass(): pl.pallas_call(functools.partial(back_kernel, ways, plan, late_plan), gri...  74.5 us
    pallas_call x1, Pallas kernels, front_pass(): pl.pallas_call(functools.partial(front_kernel, ways, plan, steps), grid=(...  63.1 us

profile of v7, /device:TPU:0, one launch (start us, length us, event | category | flops | bytes accessed | tf_op | source)
XLA Modules:
  0.0 224.9 jit_solution(8773623939764990789)
XLA Ops:
  0.6 63.1 %front_pass.1 = (bf16[4096,1536]{1,0:T(8,128)(2,1)}, bf16[4096,512]{1,0:T(8,128)(2,1)}, bf16[4096,512]{1,0:T(8,128)(2,1)}, bf16[4096,512]{1,0:T(8,128)(2,1)}, bf...) custom-call(s32[1,4]{1,0:T(1,128)} %len_ref.5, ...), custom_call_target="tpu_custom_call" | custom-call | flops 17179869184 | bytes 50331648 | tf_op jit(solution)/shard_map/front_pass/pallas_call | solution.py:463
  63.7 82.5 %third_pass.1 = (bf16[4096,512]{1,0:T(8,128)(2,1)}, bf16[4096,512]{1,0:T(8,128)(2,1)}, bf16[4096,512]{1,0:T(8,128)(2,1)}, bf16[4096,512]{1,0:T(8,128)(2,1)}, bf1...) custom-call(s32[1,4]{1,0:T(1,128)} %len_ref.5, ...), custom_call_target="tpu_custom_call" | custom-call | flops 60129542144 | bytes 46137344 | tf_op jit(solution)/shard_map/third_pass/pallas_call | solution.py:703
  146.2 74.5 %back_pass.1 = (bf16[4096,512]{1,0:T(8,128)(2,1)}, f32[64,384]{1,0:T(8,128)}, f32[64,512]{1,0:T(8,128)}, f32[256,128]{1,0:T(8,128)}, f32[64,128]{1,0:T(8,128)}, /*index=5*/f32[2,64]{1,0:T(2,128)}, f32[1,64]{1,0:T(1,128)}) custom-call(s32[1,4]{1,0:T(1,128)} %len_ref.5, bf16[4096,1536]{1,0:T(8,128)(2,1)} %get-tuple-element.54.q_ref.k_lo.k_ref.k_hi.v_lo.v_ref.v_hi, ...), custom_call_target="tpu_custom_call" | custom-call | flops 30064771072 | bytes 50331648 | tf_op jit(solution)/shard_map/back_pass/pallas_call | solution.py:1297
  220.7 4.0 %hand_over.1 = (bf16[4096,512]{1,0:T(8,128)(2,1)}, f32[64,384]{1,0:T(8,128)}, f32[64,128]{1,0:T(8,128)}, f32[64,512]{1,0:T(8,128)}, f32[256,128]{1,0:T(8,128)}, /*index=5*/f32[2,64]{1,0:T(2,128)}, f32[1,64]{1,0:T(1,128)}) custom-call(bf16[4096,512]{1,0:T(8,128)(2,1)} %get-tuple-element.78.refs_0_, f32[64,384]{1,0:T(8,128)} %get-tuple-element.79.refs_1_, ...), custom_call_target="tpu_custom_call" | custom-call | tf_op jit(solution)/shard_map/hand_over/pallas_call | solution.py:1404

commit v8 on v7

--- a/solution.py
+++ b/solution.py
@@ -1413,11 +1413,11 @@
 
 FRONT_TILE = 1024
 TILE = 512
-LAST_TILE = 1024
+LAST_TILE = 512
 CHUNK = 256
-FRONT_PLAN = {1: [(0, 0)], 2: [(1, 0)], 3: [(0, 1)], 5: [(0, 2), (1, 1)], 7: [(1, 2)], 8: [(0, 3), (1, 3)]}
-BACK_PLAN = {2: [(0, 0)], 3: [(1, 0)], 4: [(0, 1)], 6: [(1, 1), (0, 2)], 7: [(1, 2)], 8: [(0, 3)], 12: [(1, 3)]}
-LATE_PLAN = {1: [(2, 0), (3, 0)], 2: [(2, 1)], 3: [(3, 1), (2, 2)], "end": [(3, 2), (2, 3), (3, 3)]}
+FRONT_PLAN = {1: [(0, 0)], 2: [(1, 0)], 3: [(0, 1)], 4: [(1, 1)], 5: [(0, 2)], 7: [(1, 2)], 8: [(0, 3), (1, 3)]}
+BACK_PLAN = {2: [(0, 0)], 3: [(1, 0)], 4: [(0, 1)], 6: [(1, 1), (0, 2)], 7: [(1, 2)], 8: [(0, 3)], 14: [(1, 3)]}
+LATE_PLAN = {1: [(2, 0), (3, 0)], 3: [(2, 1)], 4: [(3, 1)], 5: [(2, 2)], 6: [(3, 2)], "end": [(2, 3), (3, 3)]}
 
 
 def shards(

time: 225 us -> 224 us (level)
  no operation moved by 1% of the time
where the time goes in v8:
time: 224 us
  Pallas kernels  223 us (100%)
    pallas_call x1, Pallas kernels, third_pass(): pl.pallas_call(functools.partial(ffn_kernel, chunk), grid=(steps,), in_sp...  82.5 us
    pallas_call x1, Pallas kernels, back_pass(): pl.pallas_call(functools.partial(back_kernel, ways, plan, late_plan), gri...  75.4 us
    pallas_call x1, Pallas kernels, front_pass(): pl.pallas_call(functools.partial(front_kernel, ways, plan, steps), grid=(...  61.3 us

profile of v8, /device:TPU:0, one launch (start us, length us, event | category | flops | bytes accessed | tf_op | source)
XLA Modules:
  0.0 224.0 jit_solution(5300099161469332757)
XLA Ops:
  0.6 61.3 %front_pass.1 = (bf16[4096,1536]{1,0:T(8,128)(2,1)}, bf16[4096,512]{1,0:T(8,128)(2,1)}, bf16[4096,512]{1,0:T(8,128)(2,1)}, bf16[4096,512]{1,0:T(8,128)(2,1)}, bf...) custom-call(s32[1,4]{1,0:T(1,128)} %len_ref.5, ...), custom_call_target="tpu_custom_call" | custom-call | flops 17179869184 | bytes 50331648 | tf_op jit(solution)/shard_map/front_pass/pallas_call | solution.py:463
  61.9 82.5 %third_pass.1 = (bf16[4096,512]{1,0:T(8,128)(2,1)}, bf16[4096,512]{1,0:T(8,128)(2,1)}, bf16[4096,512]{1,0:T(8,128)(2,1)}, bf16[4096,512]{1,0:T(8,128)(2,1)}, bf1...) custom-call(s32[1,4]{1,0:T(1,128)} %len_ref.5, ...), custom_call_target="tpu_custom_call" | custom-call | flops 60129542144 | bytes 46137344 | tf_op jit(solution)/shard_map/third_pass/pallas_call | solution.py:703
  144.4 75.4 %back_pass.1 = (bf16[4096,512]{1,0:T(8,128)(2,1)}, f32[64,384]{1,0:T(8,128)}, f32[64,512]{1,0:T(8,128)}, f32[256,128]{1,0:T(8,128)}, f32[64,128]{1,0:T(8,128)}, /*index=5*/f32[2,64]{1,0:T(2,128)}, f32[1,64]{1,0:T(1,128)}) custom-call(s32[1,4]{1,0:T(1,128)} %len_ref.5, bf16[4096,1536]{1,0:T(8,128)(2,1)} %get-tuple-element.54.q_ref.k_lo.k_ref.k_hi.v_lo.v_ref.v_hi, ...), custom_call_target="tpu_custom_call" | custom-call | flops 30064771072 | bytes 50331648 | tf_op jit(solution)/shard_map/back_pass/pallas_call | solution.py:1297
  219.8 4.0 %hand_over.1 = (bf16[4096,512]{1,0:T(8,128)(2,1)}, f32[64,384]{1,0:T(8,128)}, f32[64,128]{1,0:T(8,128)}, f32[64,512]{1,0:T(8,128)}, f32[256,128]{1,0:T(8,128)}, /*index=5*/f32[2,64]{1,0:T(2,128)}, f32[1,64]{1,0:T(1,128)}) custom-call(bf16[4096,512]{1,0:T(8,128)(2,1)} %get-tuple-element.78.refs_0_, f32[64,384]{1,0:T(8,128)} %get-tuple-element.79.refs_1_, ...), custom_call_target="tpu_custom_call" | custom-call | tf_op jit(solution)/shard_map/hand_over/pallas_call | solution.py:1404

commit v9 on v8

--- a/solution.py
+++ b/solution.py
@@ -616,9 +616,12 @@
     valid = row_valid(step, rows, width, length)
     d_ffn = jnp.where(valid, cot_ref[...], 0)
     seed = d_ffn.astype(f32)
+    h2_t = h2.T
+    seed_t = d_ffn.T
+
     def add_grads(cols):
-        a_back[:, cols] += tn(d_ffn, act_s[:, cols])
-        a_in[:, cols] += tn(h2, pre_s[:, cols])
+        a_back[:, cols] += nn(seed_t, act_s[:, cols])
+        a_in[:, cols] += nn(h2_t, pre_s[:, cols])
 
     for lo in range(0, hidden, chunk):
         cols = slice(lo, lo + chunk)

time: 224 us -> 224 us (level)
  no operation moved by 1% of the time
where the time goes in v9:
time: 224 us
  Pallas kernels  223 us (100%)
    pallas_call x1, Pallas kernels, third_pass(): pl.pallas_call(functools.partial(ffn_kernel, chunk), grid=(steps,), in_sp...  82.5 us
    pallas_call x1, Pallas kernels, back_pass(): pl.pallas_call(functools.partial(back_kernel, ways, plan, late_plan), gri...  75.4 us
    pallas_call x1, Pallas kernels, front_pass(): pl.pallas_call(functools.partial(front_kernel, ways, plan, steps), grid=(...  61.3 us

profile of v9, /device:TPU:0, one launch (start us, length us, event | category | flops | bytes accessed | tf_op | source)
XLA Modules:
  0.0 224.0 jit_solution(5300099161469332757)
XLA Ops:
  0.6 61.3 %front_pass.1 = (bf16[4096,1536]{1,0:T(8,128)(2,1)}, bf16[4096,512]{1,0:T(8,128)(2,1)}, bf16[4096,512]{1,0:T(8,128)(2,1)}, bf16[4096,512]{1,0:T(8,128)(2,1)}, bf...) custom-call(s32[1,4]{1,0:T(1,128)} %len_ref.5, ...), custom_call_target="tpu_custom_call" | custom-call | flops 17179869184 | bytes 50331648 | tf_op jit(solution)/shard_map/front_pass/pallas_call | solution.py:463
  61.9 82.5 %third_pass.1 = (bf16[4096,512]{1,0:T(8,128)(2,1)}, bf16[4096,512]{1,0:T(8,128)(2,1)}, bf16[4096,512]{1,0:T(8,128)(2,1)}, bf16[4096,512]{1,0:T(8,128)(2,1)}, bf1...) custom-call(s32[1,4]{1,0:T(1,128)} %len_ref.5, ...), custom_call_target="tpu_custom_call" | custom-call | flops 60129542144 | bytes 46137344 | tf_op jit(solution)/shard_map/third_pass/pallas_call | solution.py:706
  144.4 75.4 %back_pass.1 = (bf16[4096,512]{1,0:T(8,128)(2,1)}, f32[64,384]{1,0:T(8,128)}, f32[64,512]{1,0:T(8,128)}, f32[256,128]{1,0:T(8,128)}, f32[64,128]{1,0:T(8,128)}, /*index=5*/f32[2,64]{1,0:T(2,128)}, f32[1,64]{1,0:T(1,128)}) custom-call(s32[1,4]{1,0:T(1,128)} %len_ref.5, bf16[4096,1536]{1,0:T(8,128)(2,1)} %get-tuple-element.54.q_ref.k_lo.k_ref.k_hi.v_lo.v_ref.v_hi, ...), custom_call_target="tpu_custom_call" | custom-call | flops 30064771072 | bytes 50331648 | tf_op jit(solution)/shard_map/back_pass/pallas_call | solution.py:1300
  219.8 4.0 %hand_over.1 = (bf16[4096,512]{1,0:T(8,128)(2,1)}, f32[64,384]{1,0:T(8,128)}, f32[64,128]{1,0:T(8,128)}, f32[64,512]{1,0:T(8,128)}, f32[256,128]{1,0:T(8,128)}, /*index=5*/f32[2,64]{1,0:T(2,128)}, f32[1,64]{1,0:T(1,128)}) custom-call(bf16[4096,512]{1,0:T(8,128)(2,1)} %get-tuple-element.78.refs_0_, f32[64,384]{1,0:T(8,128)} %get-tuple-element.79.refs_1_, ...), custom_call_target="tpu_custom_call" | custom-call | tf_op jit(solution)/shard_map/hand_over/pallas_call | solution.py:1407
